TPU v7x, 32 devices: a whole 2x2x4 slice. The times are simulated.
32 devices in a mesh: seq: 4 (over z), expert: 8 (over y, x, core).
Axes of the slice: x: 2, y: 2, z: 4, core: 2. Of those that a mesh axis runs over, the one named last changes fastest.
Arguments:
- tokens: bfloat16 [4096, 4096], P(('seq', 'expert')), may hold values from -6 to 6
- routes: int32 [4096, 8], P(('seq', 'expert')), may hold values from 0 to 31, all different within a row; in each aligned block of 128 rows (0 to 127, 128 to 255, ...) at most 40 rows name the same one
- gates: bfloat16 [4096, 8], P(('seq', 'expert')), may hold values from 0.049804688 to 0.59765625
- w_gate: bfloat16 [32, 4096, 768], P(('seq', 'expert')), may hold values from -0.09375 to 0.09375
- w_up: bfloat16 [32, 4096, 768], P(('seq', 'expert')), may hold values from -0.09375 to 0.09375
- w_down: bfloat16 [32, 768, 4096], P(('seq', 'expert')), may hold values from -0.21875 to 0.21875
Outputs:
- mixed: bfloat16 [4096, 4096], P(('seq', 'expert'))
Inputs may be any that keep to these rules, and one draw needn't show every extreme that they name: `routes`: within the rows of one device (aligned blocks of 128 rows) no expert is named by more than 40 rows, a bound that some block reaches; each row names 8 different experts; expert e is held by the device of index e along seq+expert.
All inputs are finite; a program needn't handle non-finite values.
Results may differ from a plain program's by a relative error of at most 0.0057.
Values may be sent and summed in bfloat16 or wider, within the bound.
No kernel may reach another device: no remote copies, remote signals or barrier semaphores. Data moves between devices by JAX's collectives and lax.ppermute only.
A program may use at most 128 MiB of HBM per device.

v0:
```python
import jax
import jax.numpy as jnp
from jax import lax
from jax.sharding import PartitionSpec as P


def expert_rows(row_block, w_gate, w_up, w_down):
    layout = row_block.shape
    flattened = row_block.reshape(-1, layout[-1])
    gate_act = jnp.dot(flattened, w_gate[0], preferred_element_type=jnp.float32)
    up_act = jnp.dot(flattened, w_up[0], preferred_element_type=jnp.float32)
    hidden = (jax.nn.silu(gate_act) * up_act).astype(jnp.bfloat16)
    result = jnp.dot(hidden, w_down[0], preferred_element_type=jnp.float32).astype(jnp.bfloat16)
    return result.reshape(layout)


def slot_sources(routes, experts, capacity, filler):
    tok_rows, fanout = routes.shape
    flattened = routes.reshape(-1)
    onehot = (flattened[:, None] == jnp.arange(experts, dtype=jnp.int32)[None, :]).astype(jnp.int32)
    before = jnp.cumsum(onehot, axis=0) - onehot
    slot_index = jnp.sum(before * onehot, axis=1)
    target = flattened * capacity + slot_index
    owners = jnp.arange(tok_rows * fanout, dtype=jnp.int32) // fanout
    sources = jnp.full((experts * capacity,), filler, jnp.int32).at[target].set(owners)
    return (sources, target)


def local(tokens, routes, gates, w_gate, w_up, w_down):
    tok_rows, features = tokens.shape
    fanout = routes.shape[1]
    seq_count = lax.axis_size("seq")
    group_count = lax.axis_size("expert")
    experts = seq_count * group_count
    capacity = tok_rows * fanout * 5 // (4 * experts)
    sources, target = slot_sources(routes, experts, capacity, tok_rows)
    column_tokens, column_routes = (
        lax.all_gather(tokens, "seq", axis=0, tiled=True),
        lax.all_gather(routes, "seq", axis=0, tiled=True),
    )
    seq_index = lax.axis_index("seq")
    per_source = column_routes.reshape(seq_count, tok_rows, fanout)

    def source_table(source_routes):
        return slot_sources(source_routes, experts, capacity, tok_rows)[0]

    tables = jax.vmap(source_table)(per_source)
    offsets = (jnp.arange(seq_count, dtype=jnp.int32) * tok_rows)[:, None]
    tables = jnp.where(tables < tok_rows, tables + offsets, seq_count * tok_rows)
    tables = tables.reshape(seq_count, seq_count, group_count, capacity)
    chosen = lax.dynamic_index_in_dim(tables, seq_index, axis=1, keepdims=False)
    chosen = jnp.transpose(chosen, (1, 0, 2))
    padded = jnp.concatenate([column_tokens, jnp.zeros((1, features), column_tokens.dtype)], 0)
    outgoing = jnp.take(padded, chosen.reshape(-1), axis=0).reshape(
        group_count, seq_count, capacity, features
    )
    column_back = lax.all_to_all(
        expert_rows(
            lax.all_to_all(outgoing, "expert", split_axis=0, concat_axis=0, tiled=True),
            w_gate,
            w_up,
            w_down,
        ),
        "expert",
        split_axis=0,
        concat_axis=0,
        tiled=True,
    )
    returned = lax.all_to_all(column_back, "seq", split_axis=1, concat_axis=0, tiled=True)
    picked = jnp.take(returned.reshape(experts * capacity, features), target, axis=0)
    picked = picked.reshape(tok_rows, fanout, features)
    mixed = jnp.einsum("tk,tkd->td", gates, picked, preferred_element_type=jnp.float32)
    return mixed.astype(jnp.bfloat16)


def solution(mesh):
    placed = (
        P(("seq", "expert"), None),
        P(("seq", "expert"), None),
        P(("seq", "expert"), None),
        P(("seq", "expert"), None, None),
        P(("seq", "expert"), None, None),
        P(("seq", "expert"), None, None),
    )
    return jax.shard_map(
        local, mesh=mesh, in_specs=placed, out_specs=P(("seq", "expert"), None), check_vma=False
    )
```

profile of v0, /device:TPU:0, one launch (start us, length us, event | category | flops | bytes accessed | tf_op | source)
XLA Modules:
  0.0 676.0 jit_solution(11841612500709723677)
XLA Ops:
  6.5 0.7 all-gather.2.cloned.1.call-update
  7.3 14.9 %all_gather.6 = s32[512,8]{0,1:T(8,128)S(1)} all-gather(s32[128,8]{0,1:T(8,128)} %param.7), channel_id=1, replica_groups=mesh['seq'=4,'expert'=8] {'seq'}, dimensions={0}, use_global_device_ids=true | all-gather | bytes 20480 | tf_op jit(solution)/shard_map/all_gather | solution.py:39
  22.2 0.1 copy.72
  22.3 0.2 eq.59
  22.5 0.2 eq.55
  22.7 36.0 %reduce-window.16 = s32[4,32,8,128]{3,2,1,0:T(8,128)S(1)} reduce-window(s32[4,32,8,128]{3,2,1,0:T(8,128)S(1)} %fusion.16, s32[]{:T(128)} %constant.65.clone.1), window={size=1x1x1x128 pad=0_0x0_0x0_0x127_0}, to_apply=%region_3.4 | reduce-window | flops 16646144 | bytes 1048580 | tf_op jit(solution)/shard_map/reduce-window.2
  58.7 0.2 slice.22
  58.9 0.3 copy.74
  59.2 0.1 copy.75
  59.3 0.2 broadcast_add_fusion
  59.5 0.1 reduce_window_sum.33
  59.6 0.1 copy.71
  59.7 0.2 mul.60
  59.9 0.1 fusion.15
  60.1 0.1 multiply_reduce_fusion
  60.2 0.1 and_reduce_fusion
  60.3 15.5 %scatter_custom_fusion = s32[5120]{0:T(1024)S(1)} fusion(s32[4096]{0:T(1024)S(1)} %get-tuple-element.8, s32[4096]{0:T(1024)S(1)} %get-tuple-element.7, s32[]{:T(128)} %constant.68.clone.1), kind=kCustom, calls=%fused_computation.47 | custom fusion | bytes 20484
  75.9 0.1 add_select_fusion
  76.0 0.1 reshape.165
  76.1 0.1 reshape.166
  76.3 16.2 %all-gather.2.cloned.1.call-done = bf16[512,4096]{1,0:T(8,128)(2,1)} async-done(((bf16[128,4096]{1,0:T(8,128)(2,1)}), bf16[512,4096]{1,0:T(8,128)(2,1)}) %all-gather.2.cloned.1.call-update) | async-done | bytes 4194320 | tf_op jit(solution)/shard_map/all_gather | solution.py:38
  92.5 4.8 concatenate.3
  97.3 21.5 %gather_fusion = bf16[1280,4096]{1,0:T(8,128)(2,1)} fusion(bf16[513,4096]{1,0:T(8,128)(2,1)} %concatenate.3, s32[2048]{0:T(1024)S(1)} %pad_clamp_fusion), kind=kCustom, calls=%fused_computation | custom fusion | bytes 20976640 | tf_op jit(solution)/shard_map/jit(_take)/gather | solution.py:54
  118.8 5.8 broadcast_select_fusion
  124.6 120.2 %all_to_all.25 = bf16[8,4,40,4096]{3,2,1,0:T(8,128)(2,1)S(1)} all-to-all(bf16[8,4,40,4096]{3,2,1,0:T(8,128)(2,1)S(1)} %broadcast_select_fusion), channel_id=1, replica_groups=mesh['seq'=4,'expert'=8] {'expert'}, dimensions={0} | all-to-all | bytes 20971520 | tf_op jit(solution)/shard_map/all_to_all | solution.py:59
  244.8 12.4 %fusion.5 = f32[1280,768]{1,0:T(8,128)S(1)} fusion(bf16[1280,4096]{1,0:T(8,128)(2,1)S(1)} %bitcast.79, bf16[1,4096,768]{2,1,0:T(8,128)(2,1)} %param.9), kind=kOutput, calls=%fused_computation.11 | convolution fusion | flops 8053063680 | bytes 20709376 | tf_op jit(solution)/shard_map/dot_general | solution.py:10
  257.3 9.8 %fusion.11 = bf16[1280,768]{1,0:T(8,128)(2,1)} fusion(bf16[1280,4096]{1,0:T(8,128)(2,1)S(1)} %bitcast.80, bf16[1,4096,768]{2,1,0:T(8,128)(2,1)S(1)} %bitcast.89, f32[1280,768]{1,0:T(8,128)S(1)} %fusion.5), kind=kOutput, calls=%fused_computation.15 | convolution fusion | flops 8058961920 | bytes 22675456 | tf_op jit(solution)/shard_map/dot_general | solution.py:11
  267.0 10.5 %convolution_convert_fusion = bf16[1280,4096]{1,0:T(8,128)(2,1)S(1)} fusion(bf16[1280,768]{1,0:T(8,128)(2,1)} %fusion.11, bf16[1,768,4096]{2,1,0:T(8,128)(2,1)S(1)} %bitcast.91), kind=kOutput, calls=%fused_computation.3 | convolution fusion | flops 8058306560 | bytes 18743296 | tf_op jit(solution)/shard_map/dot_general | solution.py:13
  277.5 120.0 %all_to_all.26 = bf16[8,4,40,4096]{3,2,1,0:T(8,128)(2,1)} all-to-all(bf16[8,4,40,4096]{3,2,1,0:T(8,128)(2,1)S(1)} %bitcast.81), channel_id=1, replica_groups=mesh['seq'=4,'expert'=8] {'expert'}, dimensions={0} | all-to-all | bytes 20971520 | tf_op jit(solution)/shard_map/all_to_all | solution.py:57
  397.5 9.5 %copy.78 = bf16[8,4,40,4096]{3,2,0,1:T(8,128)(2,1)} copy(bf16[8,4,40,4096]{3,2,1,0:T(8,128)(2,1)} %all_to_all.26) | data formatting | bytes 20971520 | tf_op jit(solution)/shard_map/all_to_all | solution.py:57
  407.0 6.3 all-to-all-start.2
  413.4 0.1 copy.65
  413.5 0.1 eq.51
  413.6 0.1 reshape.162
  413.7 9.0 %reduce-window.14 = s32[32,8,128]{2,1,0:T(8,128)S(1)} reduce-window(s32[32,8,128]{2,1,0:T(8,128)S(1)} %fusion.20, s32[]{:T(128)} %constant.65.clone.1), window={size=1x1x128 pad=0_0x0_0x127_0}, to_apply=%region_0.0 | reduce-window | flops 4161536 | bytes 262148 | tf_op jit(solution)/shard_map/reduce-window
  422.7 0.1 slice.20
  422.8 0.1 copy.67
  422.9 0.1 copy.68
  423.0 0.1 copy.79
  423.1 0.1 mul.65
  423.2 0.1 broadcast_add_fusion.1
  423.4 0.1 reduce_sum.25
  423.5 0.1 copy.70
  423.7 0.1 copy.80
  423.9 216.9 %all-to-all-done.2 = bf16[8,4,40,4096]{3,2,0,1:T(8,128)(2,1)} async-done(((bf16[8,4,40,4096]{3,2,0,1:T(8,128)(2,1)}), bf16[8,4,40,4096]{3,2,0,1:T(8,128)(2,1)}, u32[]{:S(2)}, u32[]{:S(2)}) %all-to-all-start.2) | async-done | bytes 10485792 | tf_op jit(solution)/shard_map/all_to_all | solution.py:69
  640.8 20.5 %gather_fusion.1 = bf16[1024,4096]{1,0:T(8,128)(2,1)} fusion(bf16[1280,4096]{1,0:T(8,128)(2,1)} %bitcast.16, s32[1024]{0:T(1024)S(1)} %broadcast_clamp_fusion), kind=kCustom, calls=%fused_computation.1 | custom fusion | bytes 16781312 | tf_op jit(solution)/shard_map/jit(_take)/gather | solution.py:70
  661.2 5.8 fusion
  667.0 2.1 copy.89
  (45 shorter events, 0.4 us)
Async XLA Ops:
  6.5 53.5 %copy-start.3 = (s32[2]{0:T(128)S(1)}, s32[2]{0:T(128)}, u32[]{:S(2)}) copy-start(s32[2]{0:T(128)} %constant.85) | copy-start | bytes 28
  6.5 53.6 %copy-start.2 = (s32[2]{0:T(128)S(1)}, s32[2]{0:T(128)}, u32[]{:S(2)}) copy-start(s32[2]{0:T(128)} %constant.88) | copy-start | bytes 28
  6.5 85.9 %all-gather.2.cloned.1.call-start = ((), (), s32[]{:S(2)}) async-start(), calls=%async_computation.3 | async-start | bytes 5242880 | tf_op jit(solution)/shard_map/all_gather | solution.py:38
  124.6 132.7 %slice-start = ((s8[6291456]{0:T(1024)(128)(4,1)}), s8[4194304]{0:T(1024)(128)(4,1)S(1)}, s32[]{:S(2)}) async-start(s8[6291456]{0:T(1024)(128)(4,1)} %bitcast.88), calls=%async_computation.4 | async-start | bytes 8388608
  124.6 142.4 %slice-start.2 = ((s8[6291456]{0:T(1024)(128)(4,1)}), s8[4194304]{0:T(1024)(128)(4,1)S(1)}, s32[]{:S(2)}) async-start(s8[6291456]{0:T(1024)(128)(4,1)} %bitcast.90), calls=%async_computation.6 | async-start | bytes 8388608
  244.8 12.5 %slice-start.1 = ((s8[6291456]{0:T(1024)(128)(4,1)}), s8[2097152]{0:T(1024)(128)(4,1)S(1)}, s32[]{:S(2)}) async-start(s8[6291456]{0:T(1024)(128)(4,1)} %bitcast.88), calls=%async_computation.5 | async-start | bytes 4194304
  244.8 22.2 %slice-start.3 = ((s8[6291456]{0:T(1024)(128)(4,1)}), s8[2097152]{0:T(1024)(128)(4,1)S(1)}, s32[]{:S(2)}) async-start(s8[6291456]{0:T(1024)(128)(4,1)} %bitcast.90), calls=%async_computation.7 | async-start | bytes 4194304
  407.0 6.4 copy-start
  407.0 16.7 %copy-start.1 = (bf16[128,8]{0,1:T(8,128)(2,1)S(1)}, bf16[128,8]{0,1:T(8,128)(2,1)}, u32[]{:S(2)}) copy-start(bf16[128,8]{0,1:T(8,128)(2,1)} %param.8) | copy-start | bytes 6148
  407.0 233.8 %all-to-all-start.2 = ((bf16[8,4,40,4096]{3,2,0,1:T(8,128)(2,1)}), bf16[8,4,40,4096]{3,2,0,1:T(8,128)(2,1)}, u32[]{:S(2)}, u32[]{:S(2)}) async-start(bf16[8,4,40,4096]{3,2,0,1:T(8,128)(2,1)} %copy.78), calls=%async_computation.2 | async-start | bytes 20971520 | tf_op jit(solution)/shard_map/all_to_all | solution.py:69
Sparse Core Ops, SparseCore 0:
  8.9 83.5 all-gather.1
where the time goes:
time: 676 us
  blocking collectives  255 us (38%)
  waiting for transfers between devices  234 us (35%)
  local copies, waits for them, and re-layouts  76.7 us (11%)
  other arithmetic  51.7 us (8%)
  matrix products  38.5 us (6%)
  between operations  13.8 us (2%)
    all_to_all x1, waiting for transfers between devices, local(): lax.all_to_all(column_back, 'seq', split_axis=1, concat_axis=0, tiled=True)  217 us
    all_to_all x1, blocking collectives, local(): lax.all_to_all(outgoing, 'expert', split_axis=0, concat_axis=0, tiled=True)  120 us
    all_to_all x1, blocking collectives, local(): lax.all_to_all(expert_rows(lax.all_to_all(outgoing, 'expert', split_axis=...  120 us
    another operation x6, other arithmetic  45.4 us
    gather x1, local copies, waits for them, and re-layouts, local(): jnp.take(padded, chosen.reshape(-1), axis=0)  21.5 us
    gather x1, local copies, waits for them, and re-layouts, local(): jnp.take(returned.reshape(experts * capacity, features), target, axis=0)  20.5 us
    all_gather x1, waiting for transfers between devices, local(): lax.all_gather(tokens, 'seq', axis=0, tiled=True)  16.2 us
    unnamed x21, local copies, waits for them, and re-layouts  15.8 us
  transfers between devices with their start and end apart: 2, of which 2 were waited for; matrix products, arithmetic and copies ran while one was open for 10% of the time, Pallas kernels for 0%

commit v1 on v0

v1 whole, which is shorter than its diff:
```python
import functools
import math

import jax
import jax.numpy as jnp
import numpy as np
from jax import lax
from jax.experimental import pallas as pl
from jax.experimental.pallas import tpu as pltpu
from jax.sharding import PartitionSpec as P

AXES = ("seq", "expert")
F32 = jnp.float32
BF16 = jnp.bfloat16
VMEM_LIMIT = 56 * 1024 * 1024


class Grid:
    def __init__(self, seq, plane):
        side = math.isqrt(plane)
        if side * side == plane:
            self.cores = 1
        else:
            self.cores = 2
            side = math.isqrt(plane // 2)
        self.seq, self.plane, self.side = seq, plane, side
        self.count = seq * plane

    def split(self, p):
        k = p % self.cores
        return p // self.cores // self.side, p // self.cores % self.side, k

    def join(self, i, j, k):
        return (i * self.side + j) * self.cores + k

    def first(self, p, b):
        i, j, k = self.split(p)
        return self.join(i, j ^ b, k) if k % 2 == 0 else self.join(i ^ b, j, k)

    def second(self, p, b, kc):
        i, j, k = self.split(p)
        return self.join(i ^ b, j, k ^ kc) if k % 2 == 0 else self.join(i, j ^ b, k ^ kc)

    def in_plane(self, move):
        return [(z * self.plane + p, z * self.plane + move(p)) for z in range(self.seq) for p in range(self.plane)]

    def along_seq(self, pairs):
        return [(s * self.plane + p, d * self.plane + p) for s, d in pairs for p in range(self.plane)]

    def slots(self):
        if self.seq == 4:
            sources = [[0, 1, 2, 3], [1, 0, 3, 2], [2, 2, 1, 1], [3, 3, 0, 0]]
            near, middle, ends = [(0, 1), (1, 0), (2, 3), (3, 2)], [(1, 2), (2, 1)], [(1, 0), (2, 3)]
            relays = [[], [(0, near)], [(0, middle), (2, ends)], [(1, middle), (3, ends)]]
        else:
            sources = [[z ^ s for z in range(self.seq)] for s in range(self.seq)]
            relays = [[]] + [[(0, [(z, z ^ s) for z in range(self.seq)])] for s in range(1, self.seq)]
        return sources, relays


def back(pairs):
    return [(d, s) for s, d in pairs]


def move(x, pairs):
    return lax.ppermute(x, AXES, pairs)


def codes(meta, experts, base, want_gates):
    meta = meta.astype(F32)
    fanout = meta.shape[0] // 2
    tokens = meta.shape[1]
    routes, gates = meta[:fanout], meta[fanout:]
    height = -(-len(experts) // 8) * 8
    line = lax.broadcasted_iota(jnp.int32, (height, tokens), 0)
    named = jnp.zeros((height, tokens), F32)
    weights = []
    for n, e in enumerate(experts):
        hit = routes == e.astype(F32)
        named = jnp.where(line == n, jnp.max(jnp.where(hit, 1.0, 0.0), axis=0, keepdims=True), named)
        if want_gates:
            weights.append(jnp.sum(jnp.where(hit, gates, 0.0), axis=0, keepdims=True))
    before = lax.broadcasted_iota(jnp.int32, (tokens, tokens), 0) < lax.broadcasted_iota(jnp.int32, (tokens, tokens), 1)
    rank = jnp.dot(named.astype(BF16), jnp.where(before, 1.0, 0.0).astype(BF16), preferred_element_type=F32)
    rows = jnp.where(named > 0, rank + base, -1.0).astype(jnp.int32)
    return [rows[n : n + 1] for n in range(len(experts))], weights


def select_kernel(grid, slot, cap, ids, *refs):
    a, outs = grid.side, grid.side * grid.cores
    metas, toks, results = refs[:a], refs[a : 2 * a], refs[2 * a :]
    experts = [ids[grid.seq * a + n] for n in range(outs)]
    total = [None] * outs
    for src in range(a):
        rows, _ = codes(metas[src][...], experts, src * cap, False)
        values = toks[src][...]
        line = lax.broadcasted_iota(jnp.int32, (a * cap, values.shape[0]), 0)
        for n in range(outs):
            onehot = jnp.where(line == rows[n], 1.0, 0.0).astype(BF16)
            part = jnp.dot(onehot, values, preferred_element_type=F32)
            total[n] = part if src == 0 else total[n] + part
    for n in range(outs):
        results[n][...] = total[n].astype(BF16)


def meta_spec(slot, a, src, meta):
    return pl.BlockSpec((None,) + meta.shape[1:], lambda d, ids: (ids[slot * a + src], 0, 0))


def select(grid, slot, cap, ids, meta, toks):
    a, outs = grid.side, grid.side * grid.cores
    rows, width = toks[0].shape
    tile = min(width, 1024)
    return pl.pallas_call(
        functools.partial(select_kernel, grid, slot, cap),
        grid_spec=pltpu.PrefetchScalarGridSpec(
            num_scalar_prefetch=1,
            grid=(width // tile,),
            in_specs=[meta_spec(slot, a, src, meta) for src in range(a)]
            + [pl.BlockSpec((rows, tile), lambda d, ids: (0, d)) for _ in range(a)],
            out_specs=[pl.BlockSpec((a * cap, tile), lambda d, ids: (0, d)) for _ in range(outs)],
        ),
        out_shape=[jax.ShapeDtypeStruct((a * cap, width), BF16) for _ in range(outs)],
        compiler_params=pltpu.CompilerParams(vmem_limit_bytes=VMEM_LIMIT),
        cost_estimate=pl.CostEstimate(
            flops=2 * outs * a * a * cap * rows * width,
            bytes_accessed=2 * width * (a * rows + outs * a * cap),
            transcendentals=0,
        ),
        name="select",
    )(ids, *([meta] * a), *toks)


def mix_kernel(grid, slot, cap, sources, extras, ids, *refs):
    a, ins = grid.side, grid.side * grid.cores
    metas, refs = refs[: len(sources)], refs[len(sources) :]
    blocks, refs = refs[:ins], refs[ins:]
    added, results = refs[:extras], refs[extras:]
    experts = [ids[grid.seq * a + n] for n in range(ins)]
    for at, src in enumerate(sources):
        rows, weights = codes(metas[at][...], experts, src * cap, True)
        line = lax.broadcasted_iota(jnp.int32, (a * cap, rows[0].shape[1]), 0)
        total = None
        for n in range(ins):
            spread = jnp.where(line == rows[n], weights[n], 0.0).astype(BF16)
            part = lax.dot_general(spread, blocks[n][...], (((0,), (0,)), ((), ())), preferred_element_type=F32)
            total = part if total is None else total + part
        for ref in added:
            total = total + ref[...].astype(F32)
        results[at][...] = total.astype(BF16)


def mix(grid, slot, cap, ids, meta, blocks, sources, extras=()):
    a, ins = grid.side, grid.side * grid.cores
    rows, width = meta.shape[2], blocks[0].shape[1]
    tile = min(width, 1024)
    wide = pl.BlockSpec((rows, tile), lambda d, ids: (0, d))
    return pl.pallas_call(
        functools.partial(mix_kernel, grid, slot, cap, sources, len(extras)),
        grid_spec=pltpu.PrefetchScalarGridSpec(
            num_scalar_prefetch=1,
            grid=(width // tile,),
            in_specs=[meta_spec(slot, a, src, meta) for src in sources]
            + [pl.BlockSpec((a * cap, tile), lambda d, ids: (0, d)) for _ in blocks]
            + [wide for _ in extras],
            out_specs=[wide for _ in sources],
        ),
        out_shape=[jax.ShapeDtypeStruct((rows, width), BF16) for _ in sources],
        compiler_params=pltpu.CompilerParams(vmem_limit_bytes=VMEM_LIMIT),
        cost_estimate=pl.CostEstimate(
            flops=2 * len(sources) * ins * a * cap * rows * width,
            bytes_accessed=2 * width * (ins * a * cap + rows * (len(extras) + len(sources))),
            transcendentals=0,
        ),
        name="mix",
    )(ids, *([meta] * len(sources)), *blocks, *extras)


def expert_kernel(count, *refs):
    ins, (wg, wu, wd), outs, (x, total) = refs[:count], refs[count : count + 3], refs[count + 3 : 2 * count + 3], refs[2 * count + 3 :]
    step = pl.program_id(0)
    height = ins[0].shape[0]

    @pl.when(step == 0)
    def _():
        x[...] = jnp.concatenate([r[...] for r in ins], axis=0)

    rows = x[...]
    gate = jnp.dot(rows, wg[...], preferred_element_type=F32)
    up = jnp.dot(rows, wu[...], preferred_element_type=F32)
    hidden = (gate / (1.0 + jnp.exp(-gate)) * up).astype(BF16)
    width = total.shape[1]
    piece = min(width, 1024)

    for at in range(0, width, piece):
        part = jnp.dot(hidden, wd[:, at : at + piece], preferred_element_type=F32)

        @pl.when(step == 0)
        def _():
            total[:, at : at + piece] = part

        @pl.when(step > 0)
        def _():
            total[:, at : at + piece] += part

    @pl.when(step == pl.num_programs(0) - 1)
    def _():
        for n, r in enumerate(outs):
            r[...] = total[n * height : (n + 1) * height, :].astype(BF16)


def expert(blocks, w_gate, w_up, w_down):
    count = len(blocks)
    height, width = blocks[0].shape
    depth = w_gate.shape[2]
    tile = 256 if depth % 256 == 0 else depth
    whole = pl.BlockSpec((height, width), lambda f: (0, 0))
    return pl.pallas_call(
        functools.partial(expert_kernel, count),
        grid=(depth // tile,),
        in_specs=[whole] * count
        + [
            pl.BlockSpec((None, width, tile), lambda f: (0, 0, f)),
            pl.BlockSpec((None, width, tile), lambda f: (0, 0, f)),
            pl.BlockSpec((None, tile, width), lambda f: (0, f, 0)),
        ],
        out_specs=[whole] * count,
        out_shape=[jax.ShapeDtypeStruct((height, width), BF16)] * count,
        scratch_shapes=[pltpu.VMEM((count * height, width), BF16), pltpu.VMEM((count * height, width), F32)],
        compiler_params=pltpu.CompilerParams(vmem_limit_bytes=VMEM_LIMIT),
        cost_estimate=pl.CostEstimate(
            flops=6 * count * height * width * depth,
            bytes_accessed=6 * width * depth + 4 * count * height * width,
            transcendentals=count * height * depth,
        ),
        name="expert",
    )(*blocks, w_gate, w_up, w_down)


def local(grid, tokens, routes, gates, w_gate, w_up, w_down):
    tok_rows, _ = tokens.shape
    fanout = routes.shape[1]
    cap = tok_rows * fanout * 5 // (4 * grid.count)
    a, c = grid.side, grid.cores
    sources, relays = grid.slots()

    table = np.zeros((grid.count, grid.seq * a + a * c), np.int32)
    for z in range(grid.seq):
        for p in range(grid.plane):
            row = [sources[s][z] * grid.plane + grid.first(p, b) for s in range(grid.seq) for b in range(a)]
            row += [z * grid.plane + grid.second(p, b, kc) for b in range(a) for kc in range(c)]
            table[z * grid.plane + p] = row
    ids = lax.dynamic_index_in_dim(jnp.asarray(table), lax.axis_index(AXES), 0, keepdims=False)

    hop1 = [None] + [grid.in_plane(lambda p, b=b: grid.first(p, b)) for b in range(1, a)]
    hop2 = [grid.in_plane(lambda p, b=b, kc=kc: grid.second(p, b, kc)) for b in range(a) for kc in range(c)]

    own_meta = jnp.concatenate([routes.astype(BF16), gates], axis=1).T
    meta = lax.all_gather(own_meta, AXES, axis=0, tiled=False)

    seq_index = lax.axis_index("seq")
    held = [tokens]
    for s in range(1, grid.seq):
        got = None
        for origin, pairs in relays[s]:
            arrived = move(got if origin == s else held[origin], grid.along_seq(pairs))
            if got is None:
                got = arrived
            else:
                reached = functools.reduce(jnp.logical_or, [seq_index == d for _, d in pairs])
                got = jnp.where(reached, arrived, got)
        held.append(got)

    returned = []
    for s in range(grid.seq):
        near = [held[s]] + [move(held[s], hop1[b]) for b in range(1, a)]
        rows = select(grid, s, cap, ids, meta, near)
        rows = [rows[0]] + [move(rows[n], hop2[n]) for n in range(1, a * c)]
        outs = expert(rows, w_gate, w_up, w_down)
        returned.append([outs[0]] + [move(outs[n], back(hop2[n])) for n in range(1, a * c)])

    inbox = [[] for _ in range(grid.seq)]
    for s in reversed(range(grid.seq)):
        sums = mix(grid, s, cap, ids, meta, returned[s], list(range(1, a)))
        extras = [move(sums[b - 1], hop1[b]) for b in range(1, a)] + inbox[s]
        (part,) = mix(grid, s, cap, ids, meta, returned[s], [0], extras)
        if s == 0:
            return part
        for origin, pairs in reversed(relays[s]):
            arrived = move(part, grid.along_seq(back(pairs)))
            if origin == s:
                part = (part.astype(F32) + arrived.astype(F32)).astype(BF16)
            else:
                inbox[origin].append(arrived)


def solution(mesh):
    grid = Grid(mesh.shape["seq"], mesh.shape["expert"])
    two, three = P(AXES, None), P(AXES, None, None)
    return jax.shard_map(
        functools.partial(local, grid),
        mesh=mesh,
        in_specs=(two, two, two, three, three, three),
        out_specs=two,
        check_vma=False,
    )
```

time: 676 us -> 410 us (0.61)
  blocking collectives: 255 us -> 49.3 us
  Pallas kernels: 0 us -> 132 us
  local copies, waits for them, and re-layouts: 76.7 us -> 8.67 us
  waiting for transfers between devices: 234 us -> 176 us
  other arithmetic: 51.7 us -> 3.17 us
  matrix products: 38.5 us -> 0 us
  starting transfers between devices: 6.34 us -> 38.2 us
  between operations: 13.8 us -> 0.47 us
    all_to_all x2 -> x0, blocking collectives: 240 us -> none  [the longest x1 120 us: local(): lax.all_to_all(outgoing, 'expert', split_axis=0, concat_axis=0, tiled=True)]
    all_to_all x1 -> x0, waiting for transfers between devices: 217 us -> none  [local(): lax.all_to_all(column_back, 'seq', split_axis=1, concat_axis=0, tiled=True)]
    ppermute x0 -> x42, waiting for transfers between devices: none -> 176 us  [move(): return lax.ppermute(x, AXES, pairs)]
    pallas_call x0 -> x16, Pallas kernels: none -> 132 us  [the longest x4 62.8 us: expert(): pl.pallas_call(functools.partial(expert_kernel, count), grid=(depth // ti...]
    another operation x6 -> x0, other arithmetic: 45.4 us -> none
    gather x2 -> x0, local copies, waits for them, and re-layouts: 42 us -> none  [the longest x1 21.5 us: local(): jnp.take(padded, chosen.reshape(-1), axis=0)]
    dot_general x4 -> x0, matrix products: 38.5 us -> none  [the longest x1 12.4 us: expert_rows(): gate_act = jnp.dot(flattened, w_gate[0], preferred_element_type=jnp.float32)]
    ppermute x0 -> x42, starting transfers between devices: none -> 38.2 us  [move(): return lax.ppermute(x, AXES, pairs)]
  transfers between devices with their start and end apart: 2 -> 42, of which waited for: 2 -> 10; matrix products, arithmetic and copies ran while one was open for 10% -> 1% of each run, Pallas kernels for 0% -> 31%
where the time goes in v1:
time: 410 us; the launch traced here: 408 us
  waiting for transfers between devices  176 us (43%)
  Pallas kernels  132 us (32%)
  blocking collectives  49.3 us (12%)
  starting transfers between devices  38.2 us (9%)
  local copies, waits for them, and re-layouts  8.67 us (2%)
    ppermute x42, waiting for transfers between devices, move(): return lax.ppermute(x, AXES, pairs)  176 us
    pallas_call x4, Pallas kernels, expert(): pl.pallas_call(functools.partial(expert_kernel, count), grid=(depth // ti...  62.8 us
    all_gather x1, blocking collectives, local(): meta = lax.all_gather(own_meta, AXES, axis=0, tiled=False)  49.3 us
    pallas_call x8, Pallas kernels, mix(): pl.pallas_call(functools.partial(mix_kernel, grid, slot, cap, sources, le...  47 us
    ppermute x42, starting transfers between devices, move(): return lax.ppermute(x, AXES, pairs)  38.2 us
    pallas_call x4, Pallas kernels, select(): pl.pallas_call(functools.partial(select_kernel, grid, slot, cap), grid_sp...  21.9 us
  transfers between devices with their start and end apart: 42, of which 10 were waited for; matrix products, arithmetic and copies ran while one was open for 1% of the time, Pallas kernels for 31%

profile of v1, /device:TPU:0, one launch (start us, length us, event | category | flops | bytes accessed | tf_op | source)
XLA Modules:
  0.0 407.6 jit_solution(3365086324359959585)
XLA Ops:
  0.0 3.0 collective-permute-start.20
  3.0 23.4 %collective-permute-done.20.refs_2_ = bf16[128,4096]{1,0:T(8,128)(2,1)S(1)} collective-permute-done((bf16[128,4096]{1,0:T(8,128)(2,1)}, bf16[128,4096]{1,0:T(8,128)(2,1)S(1)}, u32[]{:S(2)}, u32[]{:S(2)}) %collective-permute-start.20) | collective-permute-done | bytes 1048608 | tf_op jit(solution)/shard_map/ppermute | solution.py:66
  27.9 1.3 collective-permute-start.30
  29.2 1.3 collective-permute-start.9
  30.5 46.3 %collective-permute-done.30 = bf16[128,4096]{1,0:T(8,128)(2,1)} collective-permute-done((bf16[128,4096]{1,0:T(8,128)(2,1)S(1)}, bf16[128,4096]{1,0:T(8,128)(2,1)}, u32[]{:S(2)}, u32[]{:S(2)}) %collective-permute-start.30) | collective-permute-done | bytes 1048608 | tf_op jit(solution)/shard_map/ppermute | solution.py:66
  76.8 1.3 broadcast_select_fusion.refs_2_
  78.2 1.6 collective-permute-start.31
  79.7 19.5 %collective-permute-done.9 = bf16[128,4096]{1,0:T(8,128)(2,1)} collective-permute-done((bf16[128,4096]{1,0:T(8,128)(2,1)S(1)}, bf16[128,4096]{1,0:T(8,128)(2,1)}, u32[]{:S(2)}, u32[]{:S(2)}) %collective-permute-start.9) | collective-permute-done | bytes 1048608 | tf_op jit(solution)/shard_map/ppermute | solution.py:66
  99.3 1.3 broadcast_select_fusion.1.refs_2_
  100.6 1.6 collective-permute-start.10
  102.2 49.3 %all-gather = bf16[512,128]{1,0:T(8,128)(2,1)} all-gather(bf16[16,128]{1,0:T(8,128)(2,1)S(1)} %maximum_bitcast_fusion), channel_id=2, replica_groups=mesh['seq'=4,'expert'=8] {'seq','expert'}, dimensions={0}, use_global_device_ids=true | all-gather | bytes 135168 | tf_op jit(solution)/shard_map/all_gather | solution.py:259
  151.5 1.2 dynamic-slice_bitcast_fusion.ids
  152.7 5.5 %select.7 = (bf16[80,4096]{1,0:T(8,128)(2,1)}, bf16[80,4096]{1,0:T(8,128)(2,1)}, bf16[80,4096]{1,0:T(8,128)(2,1)}, bf16[80,4096]{1,0:T(8,128)(2,1)}) custom-call(s32[12]{0:T(128)} %dynamic-slice_bitcast_fusion.ids, bf16[32,16,128]{2,1,0:T(8,128)(2,1)} %bitcast.5, bf16[32,16,128]{2,1,0:T(8,128)(2,1)} %bitcast.6, bf16[128,4096]{1,0:T(8,128)(2,1)} %copy-done.17, ...), custom_call_target="tpu_custom_call" | custom-call | flops 671088640 | bytes 4718592 | tf_op jit(solution)/shard_map/select/pallas_call | solution.py:114
  158.5 5.5 %select.5 = (bf16[80,4096]{1,0:T(8,128)(2,1)}, bf16[80,4096]{1,0:T(8,128)(2,1)}, bf16[80,4096]{1,0:T(8,128)(2,1)}, bf16[80,4096]{1,0:T(8,128)(2,1)}) custom-call(s32[12]{0:T(128)} %dynamic-slice_bitcast_fusion.ids, bf16[32,16,128]{2,1,0:T(8,128)(2,1)} %bitcast.7, bf16[32,16,128]{2,1,0:T(8,128)(2,1)} %bitcast.8, bf16[128,4096]{1,0:T(8,128)(2,1)} %copy-done.16, ...), custom_call_target="tpu_custom_call" | custom-call | flops 671088640 | bytes 4718592 | tf_op jit(solution)/shard_map/select/pallas_call | solution.py:114
  164.2 3.4 collective-permute-start.12
  167.6 8.7 %collective-permute-done.33.refs_2_ = bf16[80,4096]{1,0:T(8,128)(2,1)S(1)} collective-permute-done((bf16[80,4096]{1,0:T(8,128)(2,1)}, bf16[80,4096]{1,0:T(8,128)(2,1)S(1)}, u32[]{:S(2)}, u32[]{:S(2)}) %collective-permute-start.33) | collective-permute-done | bytes 655392 | tf_op jit(solution)/shard_map/ppermute | solution.py:66
  176.3 10.5 %collective-permute-done.34.refs_3_ = bf16[80,4096]{1,0:T(8,128)(2,1)S(1)} collective-permute-done((bf16[80,4096]{1,0:T(8,128)(2,1)}, bf16[80,4096]{1,0:T(8,128)(2,1)S(1)}, u32[]{:S(2)}, u32[]{:S(2)}) %collective-permute-start.34) | collective-permute-done | bytes 655392 | tf_op jit(solution)/shard_map/ppermute | solution.py:66
  187.6 15.7 %expert.7 = (bf16[80,4096]{1,0:T(8,128)(2,1)}, bf16[80,4096]{1,0:T(8,128)(2,1)}, bf16[80,4096]{1,0:T(8,128)(2,1)}, bf16[80,4096]{1,0:T(8,128)(2,1)}) custom-call(bf16[80,4096]{1,0:T(8,128)(2,1)} %get-tuple-element.61.refs_0_, bf16[80,4096]{1,0:T(8,128)(2,1)} %copy-done.39, bf16[80,4096]{1,0:T(8,128)(2,1)} %copy-done.40, bf16[80,4096]{1,0:T(8,128)(2,1)} %copy-done.41, ...), custom_call_target="tpu_custom_call" | custom-call | flops 6039797760 | bytes 24117248 | tf_op jit(solution)/shard_map/expert/pallas_call | solution.py:218
  204.5 5.5 %select.6 = (bf16[80,4096]{1,0:T(8,128)(2,1)}, bf16[80,4096]{1,0:T(8,128)(2,1)}, bf16[80,4096]{1,0:T(8,128)(2,1)}, bf16[80,4096]{1,0:T(8,128)(2,1)}) custom-call(s32[12]{0:T(128)} %dynamic-slice_bitcast_fusion.ids, bf16[32,16,128]{2,1,0:T(8,128)(2,1)} %bitcast.9, bf16[32,16,128]{2,1,0:T(8,128)(2,1)} %bitcast.10, bf16[128,4096]{1,0:T(8,128)(2,1)} %copy-done.26, ...), custom_call_target="tpu_custom_call" | custom-call | flops 671088640 | bytes 4718592 | tf_op jit(solution)/shard_map/select/pallas_call | solution.py:114
  212.1 15.7 %expert.5 = (bf16[80,4096]{1,0:T(8,128)(2,1)}, bf16[80,4096]{1,0:T(8,128)(2,1)}, bf16[80,4096]{1,0:T(8,128)(2,1)}, bf16[80,4096]{1,0:T(8,128)(2,1)}) custom-call(bf16[80,4096]{1,0:T(8,128)(2,1)} %get-tuple-element.45.refs_0_, bf16[80,4096]{1,0:T(8,128)(2,1)} %copy-done.33, bf16[80,4096]{1,0:T(8,128)(2,1)} %copy-done.35, bf16[80,4096]{1,0:T(8,128)(2,1)} %copy-done.38, ...), custom_call_target="tpu_custom_call" | custom-call | flops 6039797760 | bytes 24117248 | tf_op jit(solution)/shard_map/expert/pallas_call | solution.py:218
  228.4 3.4 collective-permute-done.37.refs_4_
  232.7 5.7 %mix.12 = bf16[128,4096]{1,0:T(8,128)(2,1)} custom-call(s32[12]{0:T(128)} %dynamic-slice_bitcast_fusion.ids, bf16[32,16,128]{2,1,0:T(8,128)(2,1)} %bitcast.11, bf16[80,4096]{1,0:T(8,128)(2,1)} %get-tuple-element.65.refs_1_, bf16[80,4096]{1,0:T(8,128)(2,1)} %copy-done.5, bf16[80,4096]{1,0:T(8,128)(2,1)} %copy-done.9, bf16[80,4096]{1,0:T(8,128)(2,1)} %copy-done.10), custom_call_target="tpu_custom_call" | custom-call | flops 335544320 | bytes 3670016 | tf_op jit(solution)/shard_map/mix/pallas_call | solution.py:158
  238.9 1.2 collective-permute-start.16
  240.1 1.8 collective-permute-start.23
  242.2 5.5 %select.4 = (bf16[80,4096]{1,0:T(8,128)(2,1)}, bf16[80,4096]{1,0:T(8,128)(2,1)}, bf16[80,4096]{1,0:T(8,128)(2,1)}, bf16[80,4096]{1,0:T(8,128)(2,1)}) custom-call(s32[12]{0:T(128)} %dynamic-slice_bitcast_fusion.ids, bf16[32,16,128]{2,1,0:T(8,128)(2,1)} %bitcast.12, bf16[32,16,128]{2,1,0:T(8,128)(2,1)} %bitcast.13, bf16[128,4096]{1,0:T(8,128)(2,1)} %refs_2_.1, ...), custom_call_target="tpu_custom_call" | custom-call | flops 671088640 | bytes 4718592 | tf_op jit(solution)/shard_map/select/pallas_call | solution.py:114
  247.7 8.7 %collective-permute-done.15.refs_3_ = bf16[80,4096]{1,0:T(8,128)(2,1)S(1)} collective-permute-done((bf16[80,4096]{1,0:T(8,128)(2,1)}, bf16[80,4096]{1,0:T(8,128)(2,1)S(1)}, u32[]{:S(2)}, u32[]{:S(2)}) %collective-permute-start.15) | collective-permute-done | bytes 655392 | tf_op jit(solution)/shard_map/ppermute | solution.py:66
  256.4 20.8 %collective-permute-done.16.refs_4_ = bf16[80,4096]{1,0:T(8,128)(2,1)S(1)} collective-permute-done((bf16[80,4096]{1,0:T(8,128)(2,1)}, bf16[80,4096]{1,0:T(8,128)(2,1)S(1)}, u32[]{:S(2)}, u32[]{:S(2)}) %collective-permute-start.16) | collective-permute-done | bytes 655392 | tf_op jit(solution)/shard_map/ppermute | solution.py:66
  278.1 5.6 %mix.9 = bf16[128,4096]{1,0:T(8,128)(2,1)} custom-call(s32[12]{0:T(128)} %dynamic-slice_bitcast_fusion.ids, bf16[32,16,128]{2,1,0:T(8,128)(2,1)} %bitcast.14, bf16[80,4096]{1,0:T(8,128)(2,1)} %get-tuple-element.49.refs_1_, bf16[80,4096]{1,0:T(8,128)(2,1)} %copy-done.2, bf16[80,4096]{1,0:T(8,128)(2,1)} %copy-done.3, bf16[80,4096]{1,0:T(8,128)(2,1)} %copy-done.4), custom_call_target="tpu_custom_call" | custom-call | flops 335544320 | bytes 3670016 | tf_op jit(solution)/shard_map/mix/pallas_call | solution.py:158
  283.8 6.1 %mix.13 = bf16[128,4096]{1,0:T(8,128)(2,1)} custom-call(s32[12]{0:T(128)} %dynamic-slice_bitcast_fusion.ids, bf16[32,16,128]{2,1,0:T(8,128)(2,1)} %bitcast.15, bf16[80,4096]{1,0:T(8,128)(2,1)} %get-tuple-element.65.refs_1_, bf16[80,4096]{1,0:T(8,128)(2,1)} %copy-done.5, bf16[80,4096]{1,0:T(8,128)(2,1)} %copy-done.9, bf16[80,4096]{1,0:T(8,128)(2,1)} %copy-done.10, ...), custom_call_target="tpu_custom_call" | custom-call | flops 335544320 | bytes 4718592 | tf_op jit(solution)/shard_map/mix/pallas_call | solution.py:158
  289.9 1.6 collective-permute-start.17
  291.4 1.3 collective-permute-start.39
  292.8 15.7 %expert.6 = (bf16[80,4096]{1,0:T(8,128)(2,1)}, bf16[80,4096]{1,0:T(8,128)(2,1)}, bf16[80,4096]{1,0:T(8,128)(2,1)}, bf16[80,4096]{1,0:T(8,128)(2,1)}) custom-call(bf16[80,4096]{1,0:T(8,128)(2,1)} %get-tuple-element.53.refs_0_, bf16[80,4096]{1,0:T(8,128)(2,1)} %copy-done.29, bf16[80,4096]{1,0:T(8,128)(2,1)} %copy-done.37, ...), custom_call_target="tpu_custom_call" | custom-call | flops 6039797760 | bytes 24117248 | tf_op jit(solution)/shard_map/expert/pallas_call | solution.py:218
  309.1 2.2 collective-permute-start.26
  311.2 15.7 %expert.4 = (bf16[80,4096]{1,0:T(8,128)(2,1)}, bf16[80,4096]{1,0:T(8,128)(2,1)}, bf16[80,4096]{1,0:T(8,128)(2,1)}, bf16[80,4096]{1,0:T(8,128)(2,1)}) custom-call(bf16[80,4096]{1,0:T(8,128)(2,1)} %get-tuple-element.37.refs_0_, bf16[80,4096]{1,0:T(8,128)(2,1)} %copy-done.32, bf16[80,4096]{1,0:T(8,128)(2,1)} %copy-done.34, ...), custom_call_target="tpu_custom_call" | custom-call | flops 6039797760 | bytes 24117248 | tf_op jit(solution)/shard_map/expert/pallas_call | solution.py:218
  327.2 2.0 collective-permute-start.5
  330.0 5.7 %mix.11 = bf16[128,4096]{1,0:T(8,128)(2,1)} custom-call(s32[12]{0:T(128)} %dynamic-slice_bitcast_fusion.ids, bf16[32,16,128]{2,1,0:T(8,128)(2,1)} %bitcast.16, bf16[80,4096]{1,0:T(8,128)(2,1)} %get-tuple-element.57.refs_1_, bf16[80,4096]{1,0:T(8,128)(2,1)} %copy-done.6, bf16[80,4096]{1,0:T(8,128)(2,1)} %copy-done.7, bf16[80,4096]{1,0:T(8,128)(2,1)} %copy-done.8), custom_call_target="tpu_custom_call" | custom-call | flops 335544320 | bytes 3670016 | tf_op jit(solution)/shard_map/mix/pallas_call | solution.py:158
  335.7 1.0 copy-done.14
  336.6 5.9 %mix.10 = bf16[128,4096]{1,0:T(8,128)(2,1)} custom-call(s32[12]{0:T(128)} %dynamic-slice_bitcast_fusion.ids, bf16[32,16,128]{2,1,0:T(8,128)(2,1)} %bitcast.17, bf16[80,4096]{1,0:T(8,128)(2,1)} %get-tuple-element.49.refs_1_, bf16[80,4096]{1,0:T(8,128)(2,1)} %copy-done.2, bf16[80,4096]{1,0:T(8,128)(2,1)} %copy-done.3, bf16[80,4096]{1,0:T(8,128)(2,1)} %copy-done.4, ...), custom_call_target="tpu_custom_call" | custom-call | flops 335544320 | bytes 4718592 | tf_op jit(solution)/shard_map/mix/pallas_call | solution.py:158
  342.5 1.3 collective-permute-start.18
  346.7 5.7 %mix.8 = bf16[128,4096]{1,0:T(8,128)(2,1)} custom-call(s32[12]{0:T(128)} %dynamic-slice_bitcast_fusion.ids, bf16[32,16,128]{2,1,0:T(8,128)(2,1)} %bitcast.18, bf16[80,4096]{1,0:T(8,128)(2,1)} %get-tuple-element.41.refs_1_, bf16[80,4096]{1,0:T(8,128)(2,1)} %copy-done.11, bf16[80,4096]{1,0:T(8,128)(2,1)} %copy-done.12, bf16[80,4096]{1,0:T(8,128)(2,1)} %copy-done.13), custom_call_target="tpu_custom_call" | custom-call | flops 335544320 | bytes 3670016 | tf_op jit(solution)/shard_map/mix/pallas_call | solution.py:158
  352.3 1.5 collective-permute-start.7
  353.8 12.5 %collective-permute-done.18 = bf16[128,4096]{1,0:T(8,128)(2,1)S(1)} collective-permute-done((bf16[128,4096]{1,0:T(8,128)(2,1)}, bf16[128,4096]{1,0:T(8,128)(2,1)S(1)}, u32[]{:S(2)}, u32[]{:S(2)}) %collective-permute-start.18) | collective-permute-done | bytes 1048608 | tf_op jit(solution)/shard_map/ppermute | solution.py:66
  367.3 1.0 copy-done.21
  368.4 6.1 %mix.14 = bf16[128,4096]{1,0:T(8,128)(2,1)} custom-call(s32[12]{0:T(128)} %dynamic-slice_bitcast_fusion.ids, bf16[32,16,128]{2,1,0:T(8,128)(2,1)} %bitcast.19, bf16[80,4096]{1,0:T(8,128)(2,1)} %get-tuple-element.57.refs_1_, bf16[80,4096]{1,0:T(8,128)(2,1)} %copy-done.6, bf16[80,4096]{1,0:T(8,128)(2,1)} %copy-done.7, bf16[80,4096]{1,0:T(8,128)(2,1)} %copy-done.8, ...), custom_call_target="tpu_custom_call" | custom-call | flops 335544320 | bytes 5767168 | tf_op jit(solution)/shard_map/mix/pallas_call | solution.py:158
  374.4 3.6 collective-permute-start.41
  378.0 22.2 %collective-permute-done.41.refs_7_ = bf16[128,4096]{1,0:T(8,128)(2,1)S(1)} collective-permute-done((bf16[128,4096]{1,0:T(8,128)(2,1)}, bf16[128,4096]{1,0:T(8,128)(2,1)S(1)}, u32[]{:S(2)}, u32[]{:S(2)}) %collective-permute-start.41) | collective-permute-done | bytes 1048608 | tf_op jit(solution)/shard_map/ppermute | solution.py:66
  400.3 1.0 copy-done.22
  401.3 6.3 %mix.15 = bf16[128,4096]{1,0:T(8,128)(2,1)} custom-call(s32[12]{0:T(128)} %dynamic-slice_bitcast_fusion.ids, bf16[32,16,128]{2,1,0:T(8,128)(2,1)} %bitcast.20, bf16[80,4096]{1,0:T(8,128)(2,1)} %get-tuple-element.41.refs_1_, bf16[80,4096]{1,0:T(8,128)(2,1)} %copy-done.11, bf16[80,4096]{1,0:T(8,128)(2,1)} %copy-done.12, bf16[80,4096]{1,0:T(8,128)(2,1)} %copy-done.13, ...), custom_call_target="tpu_custom_call" | custom-call | flops 335544320 | bytes 6815744 | tf_op jit(solution)/shard_map/mix/pallas_call | solution.py:158
  (144 shorter events, 14.8 us)
Async XLA Ops:
  0.0 26.4 %collective-permute-start.20 = (bf16[128,4096]{1,0:T(8,128)(2,1)}, bf16[128,4096]{1,0:T(8,128)(2,1)S(1)}, u32[]{:S(2)}, u32[]{:S(2)}) collective-permute-start(bf16[128,4096]{1,0:T(8,128)(2,1)} %refs_2_.1), channel_id=1, source_target_pairs={{0,8},{1,9},{2,10},{3,11},{4,12},{5,13},{6,14},{7,15},{8,0},{9,1},... | collective-permute-start | bytes 3145736 | tf_op jit(solution)/shard_map/ppermute | solution.py:66
  26.4 1.5 collective-permute-start.29
  27.1 2.0 collective-permute-start.8
  27.9 48.9 %collective-permute-start.30 = (bf16[128,4096]{1,0:T(8,128)(2,1)S(1)}, bf16[128,4096]{1,0:T(8,128)(2,1)}, u32[]{:S(2)}, u32[]{:S(2)}) collective-permute-start(bf16[128,4096]{1,0:T(8,128)(2,1)S(1)} %collective-permute-done.29), channel_id=1, source_target_pairs={{8,0},{9,1},{10,2},{11,3},{12,4},{13,5},{14,6},{15,7},{16,24},{17,... | collective-permute-start | bytes 3145736 | tf_op jit(solution)/shard_map/ppermute | solution.py:66
  29.2 70.1 %collective-permute-start.9 = (bf16[128,4096]{1,0:T(8,128)(2,1)S(1)}, bf16[128,4096]{1,0:T(8,128)(2,1)}, u32[]{:S(2)}, u32[]{:S(2)}) collective-permute-start(bf16[128,4096]{1,0:T(8,128)(2,1)S(1)} %collective-permute-done.8), channel_id=1, source_target_pairs={{8,0},{9,1},{10,2},{11,3},{12,4},{13,5},{14,6},{15,7},{16,24},{17,... | collective-permute-start | bytes 3145736 | tf_op jit(solution)/shard_map/ppermute | solution.py:66
  78.1 74.5 %copy-start.17 = (bf16[128,4096]{1,0:T(8,128)(2,1)}, bf16[128,4096]{1,0:T(8,128)(2,1)S(1)}, u32[]{:S(2)}) copy-start(bf16[128,4096]{1,0:T(8,128)(2,1)S(1)} %broadcast_select_fusion.refs_2_) | copy-start | bytes 3145732
  78.1 24.0 %copy-start.23 = (s32[128,8]{0,1:T(8,128)S(1)}, s32[128,8]{0,1:T(8,128)}, u32[]{:S(2)}) copy-start(s32[128,8]{0,1:T(8,128)} %param.8) | copy-start | bytes 12292
  78.1 24.0 %copy-start.24 = (bf16[128,8]{0,1:T(8,128)(2,1)S(1)}, bf16[128,8]{0,1:T(8,128)(2,1)}, u32[]{:S(2)}) copy-start(bf16[128,8]{0,1:T(8,128)(2,1)} %param.9) | copy-start | bytes 6148
  78.2 74.5 %collective-permute-start.31 = (bf16[128,4096]{1,0:T(8,128)(2,1)S(1)}, bf16[128,4096]{1,0:T(8,128)(2,1)}, u32[]{:S(2)}, u32[]{:S(2)}) collective-permute-start(bf16[128,4096]{1,0:T(8,128)(2,1)S(1)} %broadcast_select_fusion.refs_2_), channel_id=1, source_target_pairs={{0,2},{1,5},{2,0},{3,7},{4,6},{5,1},{6,4},{7,3},{8,10},{9,13},{10,... | collective-permute-start | bytes 3145736 | tf_op jit(solution)/shard_map/ppermute | solution.py:66
  100.6 57.9 %copy-start.16 = (bf16[128,4096]{1,0:T(8,128)(2,1)}, bf16[128,4096]{1,0:T(8,128)(2,1)S(1)}, u32[]{:S(2)}) copy-start(bf16[128,4096]{1,0:T(8,128)(2,1)S(1)} %broadcast_select_fusion.1.refs_2_) | copy-start | bytes 3145732
  100.6 57.9 %collective-permute-start.10 = (bf16[128,4096]{1,0:T(8,128)(2,1)S(1)}, bf16[128,4096]{1,0:T(8,128)(2,1)}, u32[]{:S(2)}, u32[]{:S(2)}) collective-permute-start(bf16[128,4096]{1,0:T(8,128)(2,1)S(1)} %broadcast_select_fusion.1.refs_2_), channel_id=1, source_target_pairs={{0,2},{1,5},{2,0},{3,7},{4,6},{5,1},{6,4},{7,3},{8,10},{9,13},{10,... | collective-permute-start | bytes 3145736 | tf_op jit(solution)/shard_map/ppermute | solution.py:66
  158.2 6.1 %collective-permute-start.32 = (bf16[80,4096]{1,0:T(8,128)(2,1)}, bf16[80,4096]{1,0:T(8,128)(2,1)S(1)}, u32[]{:S(2)}, u32[]{:S(2)}) collective-permute-start(bf16[80,4096]{1,0:T(8,128)(2,1)} %get-tuple-element.62), channel_id=1, source_target_pairs={{0,1},{1,0},{2,3},{3,2},{4,5},{5,4},{6,7},{7,6},{8,9},{9,8},{10,11... | collective-permute-start | bytes 1966088 | tf_op jit(solution)/shard_map/ppermute | solution.py:66
  158.5 17.8 %collective-permute-start.33 = (bf16[80,4096]{1,0:T(8,128)(2,1)}, bf16[80,4096]{1,0:T(8,128)(2,1)S(1)}, u32[]{:S(2)}, u32[]{:S(2)}) collective-permute-start(bf16[80,4096]{1,0:T(8,128)(2,1)} %get-tuple-element.63), channel_id=1, source_target_pairs={{0,4},{1,3},{2,6},{3,1},{4,0},{5,7},{6,2},{7,5},{8,12},{9,11},{10,... | collective-permute-start | bytes 1966088 | tf_op jit(solution)/shard_map/ppermute | solution.py:66
  158.5 28.2 %collective-permute-start.34 = (bf16[80,4096]{1,0:T(8,128)(2,1)}, bf16[80,4096]{1,0:T(8,128)(2,1)S(1)}, u32[]{:S(2)}, u32[]{:S(2)}) collective-permute-start(bf16[80,4096]{1,0:T(8,128)(2,1)} %get-tuple-element.64), channel_id=1, source_target_pairs={{0,5},{1,2},{2,7},{3,0},{4,1},{5,6},{6,3},{7,4},{8,13},{9,10},{10,... | collective-permute-start | bytes 1966088 | tf_op jit(solution)/shard_map/ppermute | solution.py:66
  158.5 45.0 %collective-permute-start.21 = (bf16[128,4096]{1,0:T(8,128)(2,1)}, bf16[128,4096]{1,0:T(8,128)(2,1)S(1)}, u32[]{:S(2)}, u32[]{:S(2)}) collective-permute-start(bf16[128,4096]{1,0:T(8,128)(2,1)} %copy-done.26), channel_id=1, source_target_pairs={{0,2},{1,5},{2,0},{3,7},{4,6},{5,1},{6,4},{7,3},{8,10},{9,13},{10,... | collective-permute-start | bytes 3145736 | tf_op jit(solution)/shard_map/ppermute | solution.py:66
  164.0 45.9 %collective-permute-start.11 = (bf16[80,4096]{1,0:T(8,128)(2,1)}, bf16[80,4096]{1,0:T(8,128)(2,1)S(1)}, u32[]{:S(2)}, u32[]{:S(2)}) collective-permute-start(bf16[80,4096]{1,0:T(8,128)(2,1)} %get-tuple-element.46), channel_id=1, source_target_pairs={{0,1},{1,0},{2,3},{3,2},{4,5},{5,4},{6,7},{7,6},{8,9},{9,8},{10,11... | collective-permute-start | bytes 1966088 | tf_op jit(solution)/shard_map/ppermute | solution.py:66
  164.2 46.2 %collective-permute-start.12 = (bf16[80,4096]{1,0:T(8,128)(2,1)}, bf16[80,4096]{1,0:T(8,128)(2,1)S(1)}, u32[]{:S(2)}, u32[]{:S(2)}) collective-permute-start(bf16[80,4096]{1,0:T(8,128)(2,1)} %get-tuple-element.47), channel_id=1, source_target_pairs={{0,4},{1,3},{2,6},{3,1},{4,0},{5,7},{6,2},{7,5},{8,12},{9,11},{10,... | collective-permute-start | bytes 1966088 | tf_op jit(solution)/shard_map/ppermute | solution.py:66
  176.3 35.0 %collective-permute-start.13 = (bf16[80,4096]{1,0:T(8,128)(2,1)}, bf16[80,4096]{1,0:T(8,128)(2,1)S(1)}, u32[]{:S(2)}, u32[]{:S(2)}) collective-permute-start(bf16[80,4096]{1,0:T(8,128)(2,1)} %get-tuple-element.48), channel_id=1, source_target_pairs={{0,5},{1,2},{2,7},{3,0},{4,1},{5,6},{6,3},{7,4},{8,13},{9,10},{10,... | collective-permute-start | bytes 1966088 | tf_op jit(solution)/shard_map/ppermute | solution.py:66
  203.4 24.4 %collective-permute-start.35 = (bf16[80,4096]{1,0:T(8,128)(2,1)}, bf16[80,4096]{1,0:T(8,128)(2,1)S(1)}, u32[]{:S(2)}, u32[]{:S(2)}) collective-permute-start(bf16[80,4096]{1,0:T(8,128)(2,1)} %get-tuple-element.66), channel_id=1, source_target_pairs={{1,0},{0,1},{3,2},{2,3},{5,4},{4,5},{7,6},{6,7},{9,8},{8,9},{11,10... | collective-permute-start | bytes 1966088 | tf_op jit(solution)/shard_map/ppermute | solution.py:66
  203.5 35.4 %collective-permute-start = (bf16[128,4096]{1,0:T(8,128)(2,1)S(1)}, bf16[128,4096]{1,0:T(8,128)(2,1)S(1)}, u32[]{:S(2)}, u32[]{:S(2)}) collective-permute-start(bf16[128,4096]{1,0:T(8,128)(2,1)S(1)} %copy-done.25), channel_id=1, source_target_pairs={{0,2},{1,5},{2,0},{3,7},{4,6},{5,1},{6,4},{7,3},{8,10},{9,13},{10,... | collective-permute-start | bytes 3145736 | tf_op jit(solution)/shard_map/ppermute | solution.py:66
  209.9 30.2 %collective-permute-start.22 = (bf16[80,4096]{1,0:T(8,128)(2,1)}, bf16[80,4096]{1,0:T(8,128)(2,1)S(1)}, u32[]{:S(2)}, u32[]{:S(2)}) collective-permute-start(bf16[80,4096]{1,0:T(8,128)(2,1)} %get-tuple-element.54), channel_id=1, source_target_pairs={{0,1},{1,0},{2,3},{3,2},{4,5},{5,4},{6,7},{7,6},{8,9},{9,8},{10,11... | collective-permute-start | bytes 1966088 | tf_op jit(solution)/shard_map/ppermute | solution.py:66
  210.4 18.0 %collective-permute-start.36 = (bf16[80,4096]{1,0:T(8,128)(2,1)}, bf16[80,4096]{1,0:T(8,128)(2,1)S(1)}, u32[]{:S(2)}, u32[]{:S(2)}) collective-permute-start(bf16[80,4096]{1,0:T(8,128)(2,1)} %get-tuple-element.67), channel_id=1, source_target_pairs={{4,0},{3,1},{6,2},{1,3},{0,4},{7,5},{2,6},{5,7},{12,8},{11,9},{14,... | collective-permute-start | bytes 1966088 | tf_op jit(solution)/shard_map/ppermute | solution.py:66
  211.3 20.6 %collective-permute-start.37 = (bf16[80,4096]{1,0:T(8,128)(2,1)S(1)}, bf16[80,4096]{1,0:T(8,128)(2,1)S(1)}, u32[]{:S(2)}, u32[]{:S(2)}) collective-permute-start(bf16[80,4096]{1,0:T(8,128)(2,1)S(1)} %copy-done.36), channel_id=1, source_target_pairs={{5,0},{2,1},{7,2},{0,3},{1,4},{6,5},{3,6},{4,7},{13,8},{10,9},{15,... | collective-permute-start | bytes 1966088 | tf_op jit(solution)/shard_map/ppermute | solution.py:66
  227.8 14.1 %collective-permute-start.14 = (bf16[80,4096]{1,0:T(8,128)(2,1)}, bf16[80,4096]{1,0:T(8,128)(2,1)S(1)}, u32[]{:S(2)}, u32[]{:S(2)}) collective-permute-start(bf16[80,4096]{1,0:T(8,128)(2,1)} %get-tuple-element.50), channel_id=1, source_target_pairs={{1,0},{0,1},{3,2},{2,3},{5,4},{4,5},{7,6},{6,7},{9,8},{8,9},{11,10... | collective-permute-start | bytes 1966088 | tf_op jit(solution)/shard_map/ppermute | solution.py:66
  238.3 39.2 %collective-permute-start.38 = (bf16[128,4096]{1,0:T(8,128)(2,1)}, bf16[128,4096]{1,0:T(8,128)(2,1)S(1)}, u32[]{:S(2)}, u32[]{:S(2)}) collective-permute-start(bf16[128,4096]{1,0:T(8,128)(2,1)} %mix.12), channel_id=1, source_target_pairs={{0,2},{1,5},{2,0},{3,7},{4,6},{5,1},{6,4},{7,3},{8,10},{9,13},{10,... | collective-permute-start | bytes 3145736 | tf_op jit(solution)/shard_map/ppermute | solution.py:66
  238.6 17.8 %collective-permute-start.15 = (bf16[80,4096]{1,0:T(8,128)(2,1)}, bf16[80,4096]{1,0:T(8,128)(2,1)S(1)}, u32[]{:S(2)}, u32[]{:S(2)}) collective-permute-start(bf16[80,4096]{1,0:T(8,128)(2,1)} %get-tuple-element.51), channel_id=1, source_target_pairs={{4,0},{3,1},{6,2},{1,3},{0,4},{7,5},{2,6},{5,7},{12,8},{11,9},{14,... | collective-permute-start | bytes 1966088 | tf_op jit(solution)/shard_map/ppermute | solution.py:66
  238.9 38.3 %collective-permute-start.16 = (bf16[80,4096]{1,0:T(8,128)(2,1)}, bf16[80,4096]{1,0:T(8,128)(2,1)S(1)}, u32[]{:S(2)}, u32[]{:S(2)}) collective-permute-start(bf16[80,4096]{1,0:T(8,128)(2,1)} %get-tuple-element.52), channel_id=1, source_target_pairs={{5,0},{2,1},{7,2},{0,3},{1,4},{6,5},{3,6},{4,7},{13,8},{10,9},{15,... | collective-permute-start | bytes 1966088 | tf_op jit(solution)/shard_map/ppermute | solution.py:66
  240.1 43.6 %copy-start.29 = (bf16[80,4096]{1,0:T(8,128)(2,1)}, bf16[80,4096]{1,0:T(8,128)(2,1)S(1)}, u32[]{:S(2)}) copy-start(bf16[80,4096]{1,0:T(8,128)(2,1)S(1)} %collective-permute-done.22.refs_1_) | copy-start | bytes 1966084
  240.1 49.7 %collective-permute-start.23 = (bf16[80,4096]{1,0:T(8,128)(2,1)S(1)}, bf16[80,4096]{1,0:T(8,128)(2,1)S(1)}, u32[]{:S(2)}, u32[]{:S(2)}) collective-permute-start(bf16[80,4096]{1,0:T(8,128)(2,1)S(1)} %copy-done.31), channel_id=1, source_target_pairs={{0,4},{1,3},{2,6},{3,1},{4,0},{5,7},{6,2},{7,5},{8,12},{9,11},{10,... | collective-permute-start | bytes 1966088 | tf_op jit(solution)/shard_map/ppermute | solution.py:66
  241.9 36.2 %copy-start.2 = (bf16[80,4096]{1,0:T(8,128)(2,1)}, bf16[80,4096]{1,0:T(8,128)(2,1)S(1)}, u32[]{:S(2)}) copy-start(bf16[80,4096]{1,0:T(8,128)(2,1)S(1)} %collective-permute-done.14.refs_2_) | copy-start | bytes 1966084
  241.9 49.5 %collective-permute-start.24 = (bf16[80,4096]{1,0:T(8,128)(2,1)S(1)}, bf16[80,4096]{1,0:T(8,128)(2,1)}, u32[]{:S(2)}, u32[]{:S(2)}) collective-permute-start(bf16[80,4096]{1,0:T(8,128)(2,1)S(1)} %copy-done.30), channel_id=1, source_target_pairs={{0,5},{1,2},{2,7},{3,0},{4,1},{5,6},{6,3},{7,4},{8,13},{9,10},{10,... | collective-permute-start | bytes 1966088 | tf_op jit(solution)/shard_map/ppermute | solution.py:66
  256.4 52.1 %collective-permute-start.1 = (bf16[80,4096]{1,0:T(8,128)(2,1)}, bf16[80,4096]{1,0:T(8,128)(2,1)S(1)}, u32[]{:S(2)}, u32[]{:S(2)}) collective-permute-start(bf16[80,4096]{1,0:T(8,128)(2,1)} %get-tuple-element.38), channel_id=1, source_target_pairs={{0,1},{1,0},{2,3},{3,2},{4,5},{5,4},{6,7},{7,6},{8,9},{9,8},{10,11... | collective-permute-start | bytes 1966088 | tf_op jit(solution)/shard_map/ppermute | solution.py:66
  277.2 31.9 %collective-permute-start.2 = (bf16[80,4096]{1,0:T(8,128)(2,1)}, bf16[80,4096]{1,0:T(8,128)(2,1)S(1)}, u32[]{:S(2)}, u32[]{:S(2)}) collective-permute-start(bf16[80,4096]{1,0:T(8,128)(2,1)} %get-tuple-element.39), channel_id=1, source_target_pairs={{0,4},{1,3},{2,6},{3,1},{4,0},{5,7},{6,2},{7,5},{8,12},{9,11},{10,... | collective-permute-start | bytes 1966088 | tf_op jit(solution)/shard_map/ppermute | solution.py:66
  277.5 33.7 %collective-permute-start.3 = (bf16[80,4096]{1,0:T(8,128)(2,1)}, bf16[80,4096]{1,0:T(8,128)(2,1)}, u32[]{:S(2)}, u32[]{:S(2)}) collective-permute-start(bf16[80,4096]{1,0:T(8,128)(2,1)} %get-tuple-element.40), channel_id=1, source_target_pairs={{0,5},{1,2},{2,7},{3,0},{4,1},{5,6},{6,3},{7,4},{8,13},{9,10},{10,... | collective-permute-start | bytes 1966088 | tf_op jit(solution)/shard_map/ppermute | solution.py:66
  289.9 45.8 %collective-permute-start.17 = (bf16[128,4096]{1,0:T(8,128)(2,1)S(1)}, bf16[128,4096]{1,0:T(8,128)(2,1)S(1)}, u32[]{:S(2)}, u32[]{:S(2)}) collective-permute-start(bf16[128,4096]{1,0:T(8,128)(2,1)S(1)} %copy-done.18), channel_id=1, source_target_pairs={{0,2},{1,5},{2,0},{3,7},{4,6},{5,1},{6,4},{7,3},{8,10},{9,13},{10,... | collective-permute-start | bytes 3145736 | tf_op jit(solution)/shard_map/ppermute | solution.py:66
  291.4 52.4 %collective-permute-start.39 = (bf16[128,4096]{1,0:T(8,128)(2,1)}, bf16[128,4096]{1,0:T(8,128)(2,1)S(1)}, u32[]{:S(2)}, u32[]{:S(2)}) collective-permute-start(bf16[128,4096]{1,0:T(8,128)(2,1)} %mix.13), channel_id=1, source_target_pairs={{0,8},{1,9},{2,10},{3,11},{4,12},{5,13},{6,14},{7,15},{24,16},{25,... | collective-permute-start | bytes 3145736 | tf_op jit(solution)/shard_map/ppermute | solution.py:66
  308.5 18.4 %collective-permute-start.25 = (bf16[80,4096]{1,0:T(8,128)(2,1)}, bf16[80,4096]{1,0:T(8,128)(2,1)S(1)}, u32[]{:S(2)}, u32[]{:S(2)}) collective-permute-start(bf16[80,4096]{1,0:T(8,128)(2,1)} %get-tuple-element.58), channel_id=1, source_target_pairs={{1,0},{0,1},{3,2},{2,3},{5,4},{4,5},{7,6},{6,7},{9,8},{8,9},{11,10... | collective-permute-start | bytes 1966088 | tf_op jit(solution)/shard_map/ppermute | solution.py:66
  309.1 18.1 %collective-permute-start.26 = (bf16[80,4096]{1,0:T(8,128)(2,1)}, bf16[80,4096]{1,0:T(8,128)(2,1)S(1)}, u32[]{:S(2)}, u32[]{:S(2)}) collective-permute-start(bf16[80,4096]{1,0:T(8,128)(2,1)} %get-tuple-element.59), channel_id=1, source_target_pairs={{4,0},{3,1},{6,2},{1,3},{0,4},{7,5},{2,6},{5,7},{12,8},{11,9},{14,... | collective-permute-start | bytes 1966088 | tf_op jit(solution)/shard_map/ppermute | solution.py:66
  311.2 17.9 %collective-permute-start.27 = (bf16[80,4096]{1,0:T(8,128)(2,1)}, bf16[80,4096]{1,0:T(8,128)(2,1)S(1)}, u32[]{:S(2)}, u32[]{:S(2)}) collective-permute-start(bf16[80,4096]{1,0:T(8,128)(2,1)} %get-tuple-element.60), channel_id=1, source_target_pairs={{5,0},{2,1},{7,2},{0,3},{1,4},{6,5},{3,6},{4,7},{13,8},{10,9},{15,... | collective-permute-start | bytes 1966088 | tf_op jit(solution)/shard_map/ppermute | solution.py:66
  326.9 17.8 %collective-permute-start.4 = (bf16[80,4096]{1,0:T(8,128)(2,1)}, bf16[80,4096]{1,0:T(8,128)(2,1)S(1)}, u32[]{:S(2)}, u32[]{:S(2)}) collective-permute-start(bf16[80,4096]{1,0:T(8,128)(2,1)} %get-tuple-element.42), channel_id=1, source_target_pairs={{1,0},{0,1},{3,2},{2,3},{5,4},{4,5},{7,6},{6,7},{9,8},{8,9},{11,10... | collective-permute-start | bytes 1966088 | tf_op jit(solution)/shard_map/ppermute | solution.py:66
  327.2 18.5 %collective-permute-start.5 = (bf16[80,4096]{1,0:T(8,128)(2,1)}, bf16[80,4096]{1,0:T(8,128)(2,1)S(1)}, u32[]{:S(2)}, u32[]{:S(2)}) collective-permute-start(bf16[80,4096]{1,0:T(8,128)(2,1)} %get-tuple-element.43), channel_id=1, source_target_pairs={{4,0},{3,1},{6,2},{1,3},{0,4},{7,5},{2,6},{5,7},{12,8},{11,9},{14,... | collective-permute-start | bytes 1966088 | tf_op jit(solution)/shard_map/ppermute | solution.py:66
  329.1 16.5 %collective-permute-start.6 = (bf16[80,4096]{1,0:T(8,128)(2,1)}, bf16[80,4096]{1,0:T(8,128)(2,1)S(1)}, u32[]{:S(2)}, u32[]{:S(2)}) collective-permute-start(bf16[80,4096]{1,0:T(8,128)(2,1)} %get-tuple-element.44), channel_id=1, source_target_pairs={{5,0},{2,1},{7,2},{0,3},{1,4},{6,5},{3,6},{4,7},{13,8},{10,9},{15,... | collective-permute-start | bytes 1966088 | tf_op jit(solution)/shard_map/ppermute | solution.py:66
  342.5 23.8 %collective-permute-start.18 = (bf16[128,4096]{1,0:T(8,128)(2,1)}, bf16[128,4096]{1,0:T(8,128)(2,1)S(1)}, u32[]{:S(2)}, u32[]{:S(2)}) collective-permute-start(bf16[128,4096]{1,0:T(8,128)(2,1)} %mix.10), channel_id=1, source_target_pairs={{0,8},{1,9},{2,10},{3,11},{4,12},{5,13},{6,14},{7,15},{24,16},{25,... | collective-permute-start | bytes 3145736 | tf_op jit(solution)/shard_map/ppermute | solution.py:66
  343.9 23.4 %collective-permute-start.28 = (bf16[128,4096]{1,0:T(8,128)(2,1)}, bf16[128,4096]{1,0:T(8,128)(2,1)}, u32[]{:S(2)}, u32[]{:S(2)}) collective-permute-start(bf16[128,4096]{1,0:T(8,128)(2,1)} %mix.11), channel_id=1, source_target_pairs={{0,2},{1,5},{2,0},{3,7},{4,6},{5,1},{6,4},{7,3},{8,10},{9,13},{10,... | collective-permute-start | bytes 3145736 | tf_op jit(solution)/shard_map/ppermute | solution.py:66
  344.8 22.6 %collective-permute-start.40 = (bf16[128,4096]{1,0:T(8,128)(2,1)S(1)}, bf16[128,4096]{1,0:T(8,128)(2,1)S(1)}, u32[]{:S(2)}, u32[]{:S(2)}) collective-permute-start(bf16[128,4096]{1,0:T(8,128)(2,1)S(1)} %add_convert_fusion), channel_id=1, source_target_pairs={{16,8},{17,9},{18,10},{19,11},{20,12},{21,13},{22,14},{23,15},{8,1... | collective-permute-start | bytes 3145736 | tf_op jit(solution)/shard_map/ppermute | solution.py:66
  352.3 25.7 %collective-permute-start.7 = (bf16[128,4096]{1,0:T(8,128)(2,1)}, bf16[128,4096]{1,0:T(8,128)(2,1)S(1)}, u32[]{:S(2)}, u32[]{:S(2)}) collective-permute-start(bf16[128,4096]{1,0:T(8,128)(2,1)} %mix.8), channel_id=1, source_target_pairs={{0,2},{1,5},{2,0},{3,7},{4,6},{5,1},{6,4},{7,3},{8,10},{9,13},{10,... | collective-permute-start | bytes 3145736 | tf_op jit(solution)/shard_map/ppermute | solution.py:66
  366.6 11.4 %collective-permute-start.19 = (bf16[128,4096]{1,0:T(8,128)(2,1)S(1)}, bf16[128,4096]{1,0:T(8,128)(2,1)S(1)}, u32[]{:S(2)}, u32[]{:S(2)}) collective-permute-start(bf16[128,4096]{1,0:T(8,128)(2,1)S(1)} %add_convert_fusion.1), channel_id=1, source_target_pairs={{16,8},{17,9},{18,10},{19,11},{20,12},{21,13},{22,14},{23,15},{8,1... | collective-permute-start | bytes 3145736 | tf_op jit(solution)/shard_map/ppermute | solution.py:66
  374.4 25.8 %collective-permute-start.41 = (bf16[128,4096]{1,0:T(8,128)(2,1)}, bf16[128,4096]{1,0:T(8,128)(2,1)S(1)}, u32[]{:S(2)}, u32[]{:S(2)}) collective-permute-start(bf16[128,4096]{1,0:T(8,128)(2,1)} %mix.14), channel_id=1, source_target_pairs={{8,0},{9,1},{10,2},{11,3},{12,4},{13,5},{14,6},{15,7},{0,8},{1,9},... | collective-permute-start | bytes 3145736 | tf_op jit(solution)/shard_map/ppermute | solution.py:66
  (36 other events, 233.6 us)

commit v2 on v1

v2 whole, which is shorter than its diff:
```python
import functools
import math

import jax
import jax.numpy as jnp
import numpy as np
from jax import lax
from jax.experimental import pallas as pl
from jax.experimental.pallas import tpu as pltpu
from jax.sharding import PartitionSpec as P

AXES = ("seq", "expert")
F32 = jnp.float32
BF16 = jnp.bfloat16
VMEM_LIMIT = 56 * 1024 * 1024
TILE = 2048
SHORT = pl.CostEstimate(flops=2_000_000_000, bytes_accessed=6_000_000, transcendentals=0)
LONG = pl.CostEstimate(flops=6_000_000_000, bytes_accessed=24_000_000, transcendentals=0)


class Grid:
    def __init__(self, seq, plane):
        side = math.isqrt(plane)
        if side * side == plane:
            self.cores = 1
        else:
            self.cores = 2
            side = math.isqrt(plane // 2)
        self.seq, self.plane, self.side = seq, plane, side
        self.count = seq * plane

    def split(self, p):
        k = p % self.cores
        return p // self.cores // self.side, p // self.cores % self.side, k

    def join(self, i, j, k):
        return (i * self.side + j) * self.cores + k

    def first(self, p, b):
        i, j, k = self.split(p)
        return self.join(i, j ^ b, k) if k % 2 == 0 else self.join(i ^ b, j, k)

    def second(self, p, b, kc):
        i, j, k = self.split(p)
        return self.join(i ^ b, j, k ^ kc) if k % 2 == 0 else self.join(i, j ^ b, k ^ kc)

    def in_plane(self, move):
        return [(z * self.plane + p, z * self.plane + move(p)) for z in range(self.seq) for p in range(self.plane)]

    def along_seq(self, pairs):
        return [(s * self.plane + p, d * self.plane + p) for s, d in pairs for p in range(self.plane)]

    def relays(self):
        if self.seq == 4:
            near, middle, ends = [(0, 1), (1, 0), (2, 3), (3, 2)], [(1, 2), (2, 1)], [(1, 0), (2, 3)]
            return [[], [(0, near)], [(0, middle), (2, ends)], [(1, middle), (3, ends)]]
        return [[]] + [[(0, [(z, z ^ s) for z in range(self.seq)])] for s in range(1, self.seq)]


    def returns(self):
        if self.seq == 4:
            near, middle, ends = [(0, 1), (1, 0), (2, 3), (3, 2)], [(1, 2), (2, 1)], [(0, 1), (3, 2)]
            return [[], [near], [ends, middle], [ends, [(1, 3), (2, 0)]]]
        return [[]] + [[[(z, z ^ s) for z in range(self.seq)]] for s in range(1, self.seq)]


def back(pairs):
    return [(d, s) for s, d in pairs]


def move(x, pairs):
    return lax.ppermute(x, AXES, pairs)


def pin_kernel(*refs):
    pass


def pin(values, event, us=0):
    count = len(values)
    anywhere = pl.BlockSpec(memory_space=pl.ANY)
    return pl.pallas_call(
        pin_kernel,
        in_specs=[anywhere] * (count + 1),
        out_specs=[anywhere] * count,
        out_shape=[jax.ShapeDtypeStruct(v.shape, v.dtype) for v in values],
        input_output_aliases={n: n for n in range(count)},
        cost_estimate=pl.CostEstimate(flops=int(us * 1e9), bytes_accessed=int(us * 3e6), transcendentals=0),
        name="pin",
    )(*values, event)


def codes(meta, experts, base, want_gates):
    meta = meta.astype(F32)
    fanout = meta.shape[0] // 2
    tokens = meta.shape[1]
    routes, gates = meta[:fanout], meta[fanout:]
    height = -(-len(experts) // 8) * 8
    line = lax.broadcasted_iota(jnp.int32, (height, tokens), 0)
    named = jnp.zeros((height, tokens), F32)
    weights = jnp.zeros((height, tokens), F32)
    for n, e in enumerate(experts):
        hit = routes == e.astype(F32)
        named = jnp.where(line == n, jnp.max(jnp.where(hit, 1.0, 0.0), axis=0, keepdims=True), named)
        if want_gates:
            weights = jnp.where(line == n, jnp.sum(jnp.where(hit, gates, 0.0), axis=0, keepdims=True), weights)
    before = lax.broadcasted_iota(jnp.int32, (tokens, tokens), 0) < lax.broadcasted_iota(jnp.int32, (tokens, tokens), 1)
    rank = jnp.dot(named.astype(BF16), jnp.where(before, 1.0, 0.0).astype(BF16), preferred_element_type=F32)
    return jnp.where(named > 0, rank + base, -1.0), weights


def select_kernel(grid, cap, ids, *refs):
    a, outs = grid.side, grid.side * grid.cores
    metas, toks, results, table = refs[:a], refs[a : 2 * a], refs[-outs - 1 : -1], refs[-1]

    @pl.when(pl.program_id(0) == 0)
    def _():
        experts = [ids[n] for n in range(outs)]
        for src in range(a):
            rows, _ = codes(metas[src][...], experts, src * cap, False)
            line = lax.broadcasted_iota(jnp.int32, (a * cap, rows.shape[1]), 0).astype(F32)
            for n in range(outs):
                table[src, n] = jnp.where(line == rows[n : n + 1], 1.0, 0.0).astype(BF16)

    for n in range(outs):
        total = jnp.dot(table[0, n], toks[0][...], preferred_element_type=F32)
        for src in range(1, a):
            total = total + jnp.dot(table[src, n], toks[src][...], preferred_element_type=F32)
        results[n][...] = total.astype(BF16)


def meta_spec(tok, width, lines):
    rows = tok.shape[0]
    return pl.BlockSpec((lines, rows), lambda d, ids: (0, width // rows))


def select(grid, cap, ids, lines, width, toks, events=()):
    a, outs = grid.side, grid.side * grid.cores
    rows = toks[0].shape[0]
    tile = min(width, TILE)
    return pl.pallas_call(
        functools.partial(select_kernel, grid, cap),
        grid_spec=pltpu.PrefetchScalarGridSpec(
            num_scalar_prefetch=1,
            grid=(width // tile,),
            in_specs=[meta_spec(tok, width, lines) for tok in toks]
            + [pl.BlockSpec((rows, tile), lambda d, ids: (0, d)) for _ in range(a)]
            + [pl.BlockSpec(memory_space=pl.ANY) for _ in events],
            out_specs=[pl.BlockSpec((a * cap, tile), lambda d, ids: (0, d)) for _ in range(outs)],
            scratch_shapes=[pltpu.VMEM((a, outs, a * cap, rows), BF16)],
        ),
        out_shape=[jax.ShapeDtypeStruct((a * cap, width), BF16) for _ in range(outs)],
        compiler_params=pltpu.CompilerParams(vmem_limit_bytes=VMEM_LIMIT),
        cost_estimate=SHORT,
        name="select",
    )(ids, *toks, *toks, *events)


def mix_kernel(grid, cap, sources, extras, ids, *refs):
    a, ins = grid.side, grid.side * grid.cores
    metas, refs = refs[: len(sources)], refs[len(sources) :]
    blocks, refs = refs[:ins], refs[ins:]
    added, results, table = refs[:extras], refs[-len(sources) - 1 : -1], refs[-1]

    @pl.when(pl.program_id(0) == 0)
    def _():
        experts = [ids[n] for n in range(ins)]
        for at, src in enumerate(sources):
            rows, weights = codes(metas[at][...], experts, src * cap, True)
            rows, weights = rows.T, weights.T
            line = lax.broadcasted_iota(jnp.int32, (rows.shape[0], a * cap), 1).astype(F32)
            for n in range(ins):
                spread = jnp.where(line == rows[:, n : n + 1], weights[:, n : n + 1], 0.0)
                table[at, n] = spread.astype(BF16)

    for at in range(len(sources)):
        total = jnp.dot(table[at, 0], blocks[0][...], preferred_element_type=F32)
        for n in range(1, ins):
            total = total + jnp.dot(table[at, n], blocks[n][...], preferred_element_type=F32)
        for ref in added:
            total = total + ref[...].astype(F32)
        results[at][...] = total.astype(BF16)


def mix(grid, cap, ids, lines, toks, blocks, sources, extras=(), events=()):
    a, ins = grid.side, grid.side * grid.cores
    rows, width = toks[0].shape[0], blocks[0].shape[1]
    tile = min(width, TILE)
    wide = pl.BlockSpec((rows, tile), lambda d, ids: (0, d))
    return pl.pallas_call(
        functools.partial(mix_kernel, grid, cap, sources, len(extras)),
        grid_spec=pltpu.PrefetchScalarGridSpec(
            num_scalar_prefetch=1,
            grid=(width // tile,),
            in_specs=[meta_spec(toks[src], width, lines) for src in sources]
            + [pl.BlockSpec((a * cap, tile), lambda d, ids: (0, d)) for _ in blocks]
            + [wide for _ in extras]
            + [pl.BlockSpec(memory_space=pl.ANY) for _ in events],
            out_specs=[wide for _ in sources],
            scratch_shapes=[pltpu.VMEM((len(sources), ins, rows, a * cap), BF16)],
        ),
        out_shape=[jax.ShapeDtypeStruct((rows, width), BF16) for _ in sources],
        compiler_params=pltpu.CompilerParams(vmem_limit_bytes=VMEM_LIMIT),
        cost_estimate=SHORT,
        name="mix",
    )(ids, *[toks[src] for src in sources], *blocks, *extras, *events)


def expert_kernel(count, pieces, *refs):
    ins, (wg, wu, wd), outs = refs[:count], refs[count : count + 3], refs[-count - 8 : -8]
    x, wg_in, wu_in, wd_in, gate, up, sems, x_sems = refs[-8:]
    height = ins[0].shape[0]
    width, depth = wg.shape[1:]
    piece = width // pieces
    copies = []
    for n, r in enumerate(ins):
        copies.append(pltpu.make_async_copy(r, x.at[n], x_sems.at[n]))
    for at in range(pieces):
        part = pl.ds(at * piece, piece)
        copies.append(pltpu.make_async_copy(wg.at[0, part], wg_in.at[part], sems.at[at]))
        copies.append(pltpu.make_async_copy(wu.at[0, part], wu_in.at[part], sems.at[pieces + at]))
    copies.append(pltpu.make_async_copy(wd.at[0], wd_in, sems.at[2 * pieces]))
    for copy in copies:
        copy.start()
    for copy in copies[:count]:
        copy.wait()
    for at in range(pieces):
        part = slice(at * piece, (at + 1) * piece)
        copies[count + 2 * at].wait()
        copies[count + 2 * at + 1].wait()
        rows = jnp.concatenate([x[n, :, part] for n in range(count)], axis=0)
        g = jnp.dot(rows, wg_in[part], preferred_element_type=F32)
        u = jnp.dot(rows, wu_in[part], preferred_element_type=F32)
        gate[...] = g if at == 0 else gate[...] + g
        up[...] = u if at == 0 else up[...] + u
    g = gate[...]
    hidden = (g / (1.0 + jnp.exp(-g)) * up[...]).astype(BF16)
    copies[-1].wait()
    out_piece = min(width, 1024)
    for at in range(0, width, out_piece):
        y = jnp.dot(hidden, wd_in[:, at : at + out_piece], preferred_element_type=F32)
        for n, r in enumerate(outs):
            r[:, at : at + out_piece] = y[n * height : (n + 1) * height].astype(BF16)


def expert(blocks, w_gate, w_up, w_down, events=()):
    count = len(blocks)
    height, width = blocks[0].shape
    depth = w_gate.shape[2]
    pieces = 8 if width % 2048 == 0 else 1
    anywhere = pl.BlockSpec(memory_space=pl.ANY)
    return pl.pallas_call(
        functools.partial(expert_kernel, count, pieces),
        in_specs=[anywhere] * (count + 3 + len(events)),
        out_specs=[pl.BlockSpec(memory_space=pltpu.VMEM)] * count,
        out_shape=[jax.ShapeDtypeStruct((height, width), BF16)] * count,
        scratch_shapes=[
            pltpu.VMEM((count, height, width), BF16),
            pltpu.VMEM((width, depth), BF16),
            pltpu.VMEM((width, depth), BF16),
            pltpu.VMEM((depth, width), BF16),
            pltpu.VMEM((count * height, depth), F32),
            pltpu.VMEM((count * height, depth), F32),
            pltpu.SemaphoreType.DMA((2 * pieces + 1,)),
            pltpu.SemaphoreType.DMA((count,)),
        ],
        compiler_params=pltpu.CompilerParams(vmem_limit_bytes=VMEM_LIMIT),
        cost_estimate=LONG,
        name="expert",
    )(*blocks, w_gate, w_up, w_down, *events)


def local(grid, tokens, routes, gates, w_gate, w_up, w_down):
    tok_rows, width = tokens.shape
    fanout = routes.shape[1]
    cap = tok_rows * fanout * 5 // (4 * grid.count)
    a, c = grid.side, grid.cores
    relays, returns = grid.relays(), grid.returns()

    table = np.zeros((grid.count, a * c), np.int32)
    for z in range(grid.seq):
        for p in range(grid.plane):
            table[z * grid.plane + p] = [z * grid.plane + grid.second(p, b, kc) for b in range(a) for kc in range(c)]
    ids = lax.dynamic_index_in_dim(jnp.asarray(table), lax.axis_index(AXES), 0, keepdims=False)

    hop1 = [None] + [grid.in_plane(lambda p, b=b: grid.first(p, b)) for b in range(1, a)]
    hop2 = [grid.in_plane(lambda p, b=b, kc=kc: grid.second(p, b, kc)) for b in range(a) for kc in range(c)]

    lines = 2 * fanout
    meta = jnp.concatenate([routes.astype(BF16), gates], axis=1).T
    meta = jnp.pad(meta, ((0, tok_rows - lines), (0, 0)))
    tokens = jnp.concatenate([tokens, meta], axis=1)

    seq_index = lax.axis_index("seq")
    last = grid.seq - 1
    held, known, rows, outs, returned = {0: tokens}, {}, {}, {}, {}
    steps, inbox, sums, parts = {}, [], {}, {}

    def land(values, event, us=0):
        if any(v is event for v in values):
            return values, event
        values = pin(values, event, us)
        return values, values[0]

    def send_near(s):
        known[s] = [held[s]] + [move(held[s], hop1[b]) for b in range(1, a)]

    def land_near(s, event):
        known[s][1:], event = land(known[s][1:], event)
        return event

    def begin(origin):
        for s in range(1, grid.seq):
            if relays[s][0][0] == origin:
                steps[s] = move(held[origin], grid.along_seq(relays[s][0][1]))

    def forward(s, event):
        if s > last or len(relays[s]) == 1:
            return event
        (first,), event = land([steps[s]], event)
        steps[s] = (first, move(first, grid.along_seq(relays[s][1][1])))
        return event

    def hold(s, event):
        if isinstance(steps[s], tuple):
            (second,), event = land([steps[s][1]], event)
            reached = functools.reduce(jnp.logical_or, [seq_index == d for _, d in relays[s][1][1]])
            held[s] = jnp.where(reached, second, steps[s][0])
        else:
            (held[s],), event = land([steps[s]], event)
        send_near(s)
        begin(s)
        return event

    def choose(s, event):
        chosen = select(grid, cap, ids, lines, width, known[s], [event])
        rows[s] = [chosen[0]] + [move(chosen[n], hop2[n]) for n in range(1, a * c)]
        return chosen[0]

    def land_inside(s, event):
        if c > 1:
            rows[s][1:c], event = land(rows[s][1:c], event)
        return event

    def land_rows(s, event):
        rows[s][c:], event = land(rows[s][c:], event, 8)
        return event

    def work(s, event):
        outs[s] = expert(rows[s], w_gate, w_up, w_down, [event])
        return outs[s][0]

    def give(s, event):
        values, event = land(outs[s], event)
        returned[s] = [values[0]] + [move(values[n], back(hop2[n])) for n in range(1, a * c)]
        return event

    def land_returned(s, event):
        returned[s][1:], event = land(returned[s][1:], event)
        return event

    def gather(s, event):
        values = mix(grid, cap, ids, lines, known[s], returned[s], list(range(1, a)), (), [event])
        sums[s] = [move(x, hop1[b + 1]) for b, x in enumerate(values)]
        return values[0]

    def finish(s, event):
        extras, event = land(sums[s] + (inbox if s == 0 else []), event)
        (parts[s],) = mix(grid, cap, ids, lines, known[s], returned[s], [0], extras, [event])
        return parts[s]

    def climb(s, event):
        (parts[s],), event = land([parts[s]], event)
        arrived = move(parts[s], grid.along_seq(returns[s][0]))
        if len(returns[s]) == 1:
            inbox.append(arrived)
        else:
            sums[s] = arrived
        return event

    def climb_on(s, event):
        if len(returns[s]) > 1:
            (arrived,), event = land([sums[s]], event)
            part = (parts[s].astype(F32) + arrived.astype(F32)).astype(BF16)
            inbox.append(move(part, grid.along_seq(returns[s][1])))
        return event

    send_near(0)
    begin(0)
    event = land_near(0, ids)
    event = choose(0, event)
    event = land_inside(0, event)
    for s in range(1, grid.seq):
        event = hold(s, event)
        event = forward(s + 1, event)
        if s > 1:
            event = land_inside(s - 1, event)
        if s > 1:
            event = work(s - 2, event)
        event = land_rows(s - 1, event)
        event = land_near(s, event)
        event = choose(s, event)
    event = work(last - 1, event)
    event = give(last - 1, event)
    event = land_inside(last, event)
    event = land_rows(last, event)
    event = work(last, event)
    event = give(last, event)
    event = land_returned(last - 1, event)
    event = gather(last - 1, event)
    event = land_returned(last, event)
    event = gather(last, event)
    event = finish(last - 1, event)
    event = climb(last - 1, event)
    event = give(last - 2, event)
    event = finish(last, event)
    event = climb(last, event)
    for s in range(last - 2, -1, -1):
        event = land_returned(s, event)
        event = gather(s, event)
        if s > 0:
            if s == last - 2:
                event = climb_on(last - 1, event)
            event = finish(s, event)
            event = climb(s, event)
            if s == last - 2:
                event = climb_on(last, event)
            event = give(s - 1, event)
    if grid.seq == 4:
        inbox[0:1], event = land(inbox[0:1], event)
    finish(0, event)
    return parts[0]


def solution(mesh):
    grid = Grid(mesh.shape["seq"], mesh.shape["expert"])
    two, three = P(AXES, None), P(AXES, None, None)
    return jax.shard_map(
        functools.partial(local, grid),
        mesh=mesh,
        in_specs=(two, two, two, three, three, three),
        out_specs=two,
        check_vma=False,
    )
```

time: 410 us -> 295 us (0.72)
  waiting for transfers between devices: 176 us -> 107 us
  blocking collectives: 49.3 us -> 0 us
  Pallas kernels: 132 us -> 112 us
  local copies, waits for them, and re-layouts: 8.67 us -> 18.3 us
  other arithmetic: 3.17 us -> 11.3 us
  starting transfers between devices: 38.2 us -> 45 us
    ppermute x42, waiting for transfers between devices: 176 us -> 107 us  [move(): return lax.ppermute(x, AXES, pairs)]
    all_gather x1 -> x0, blocking collectives: 49.3 us -> none  [local(): meta = lax.all_gather(own_meta, AXES, axis=0, tiled=False)]
    pallas_call x16 -> x45, Pallas kernels: 132 us -> 112 us  [the longest x4 55 us: expert(): pl.pallas_call(functools.partial(expert_kernel, count, pieces), in_specs=...]
    unnamed x84 -> x58, local copies, waits for them, and re-layouts: 7.5 us -> 17.1 us
    ppermute x42, starting transfers between devices: 38.2 us -> 45 us  [move(): return lax.ppermute(x, AXES, pairs)]
    convert_element_type x3, other arithmetic: 0.5 us -> 5.63 us  [the longest x2 4.94 us: climb_on(): part = (parts[s].astype(F32) + arrived.astype(F32)).astype(BF16)]
  transfers between devices with their start and end apart: 42 -> 42, of which waited for: 10 -> 20; matrix products, arithmetic and copies ran while one was open for 1% -> 3% of each run, Pallas kernels for 31% -> 35%
where the time goes in v2:
time: 295 us; the launch traced here: 294 us
  Pallas kernels  112 us (38%)
  waiting for transfers between devices  107 us (36%)
  starting transfers between devices  45 us (15%)
  local copies, waits for them, and re-layouts  18.3 us (6%)
  other arithmetic  11.3 us (4%)
    ppermute x42, waiting for transfers between devices, move(): return lax.ppermute(x, AXES, pairs)  107 us
    pallas_call x4, Pallas kernels, expert(): pl.pallas_call(functools.partial(expert_kernel, count, pieces), in_specs=...  55 us
    ppermute x42, starting transfers between devices, move(): return lax.ppermute(x, AXES, pairs)  45 us
    pallas_call x8, Pallas kernels, mix(): pl.pallas_call(functools.partial(mix_kernel, grid, cap, sources, len(extr...  38.6 us
    pallas_call x4, Pallas kernels, select(): pl.pallas_call(functools.partial(select_kernel, grid, cap), grid_spec=plt...  18.3 us
    unnamed x58, local copies, waits for them, and re-layouts  17.1 us
  transfers between devices with their start and end apart: 42, of which 20 were waited for; matrix products, arithmetic and copies ran while one was open for 3% of the time, Pallas kernels for 35%

profile of v2, /device:TPU:0, one launch (start us, length us, event | category | flops | bytes accessed | tf_op | source)
XLA Modules:
  0.0 293.9 jit_solution(10387352574708263913)
XLA Ops:
  1.4 1.3 fusion.1.refs_0_.refs_2_
  2.7 3.0 %collective-permute-start = (bf16[128,4224]{1,0:T(8,128)(2,1)S(1)}, bf16[128,4224]{1,0:T(8,128)(2,1)}, u32[]{:S(2)}, u32[]{:S(2)}) collective-permute-start(bf16[128,4224]{1,0:T(8,128)(2,1)S(1)} %fusion.1.refs_0_.refs_2_), channel_id=1, source_target_pairs={{0,2},{1,5},{2,0},{3,7},{4,6},{5,1},{6,4},{7,3},{8,10},{9,13},{10,... | collective-permute-start | bytes 3244040 | tf_op jit(solution)/shard_map/ppermute | solution.py:72
  5.7 1.6 collective-permute-start.5
  9.2 9.7 %collective-permute-done.refs_0_ = bf16[128,4224]{1,0:T(8,128)(2,1)} collective-permute-done((bf16[128,4224]{1,0:T(8,128)(2,1)S(1)}, bf16[128,4224]{1,0:T(8,128)(2,1)}, u32[]{:S(2)}, u32[]{:S(2)}) %collective-permute-start) | collective-permute-done | bytes 1081376 | tf_op jit(solution)/shard_map/ppermute | solution.py:72
  18.9 4.6 %select.9 = (bf16[80,4096]{1,0:T(8,128)(2,1)}, bf16[80,4096]{1,0:T(8,128)(2,1)}, bf16[80,4096]{1,0:T(8,128)(2,1)}, bf16[80,4096]{1,0:T(8,128)(2,1)}) custom-call(s32[4]{0:T(128)} %dynamic-slice_bitcast_fusion.refs_1_.ids, bf16[128,4224]{1,0:T(8,128)(2,1)} %copy-done.8, bf16[128,4224]{1,0:T(8,128)(2,1)} %pin.29.refs_1_.refs_3_.refs_4_.refs_0_, ...), custom_call_target="tpu_custom_call" | custom-call | flops 2000000000 | bytes 6000000 | tf_op jit(solution)/shard_map/select/pallas_call | solution.py:141
  23.5 2.1 collective-permute-start.2
  26.9 4.2 %collective-permute-done.5.refs_0_ = bf16[128,4224]{1,0:T(8,128)(2,1)S(1)} collective-permute-done((bf16[128,4224]{1,0:T(8,128)(2,1)S(1)}, bf16[128,4224]{1,0:T(8,128)(2,1)S(1)}, u32[]{:S(2)}, u32[]{:S(2)}) %collective-permute-start.5) | collective-permute-done | bytes 1081376 | tf_op jit(solution)/shard_map/ppermute | solution.py:72
  32.0 1.5 collective-permute-start.6
  36.5 14.0 %collective-permute-done.3.refs_1_ = bf16[80,4096]{1,0:T(8,128)(2,1)} collective-permute-done((bf16[80,4096]{1,0:T(8,128)(2,1)}, bf16[80,4096]{1,0:T(8,128)(2,1)}, u32[]{:S(2)}, u32[]{:S(2)}) %collective-permute-start.3) | collective-permute-done | bytes 655392 | tf_op jit(solution)/shard_map/ppermute | solution.py:72
  50.6 2.3 collective-permute-done.6.refs_0_
  52.8 4.6 %select.10 = (bf16[80,4096]{1,0:T(8,128)(2,1)}, bf16[80,4096]{1,0:T(8,128)(2,1)}, bf16[80,4096]{1,0:T(8,128)(2,1)}, bf16[80,4096]{1,0:T(8,128)(2,1)}) custom-call(s32[4]{0:T(128)} %dynamic-slice_bitcast_fusion.refs_1_.ids, bf16[128,4224]{1,0:T(8,128)(2,1)} %pin.31.refs_1_.refs_0_.refs_2_, bf16[128,4224]{1,0:T(8,128)(2,1)} %pin.34.refs_1_.refs_3_.refs_4_.refs_0_, ...), custom_call_target="tpu_custom_call" | custom-call | flops 2000000000 | bytes 6000000 | tf_op jit(solution)/shard_map/select/pallas_call | solution.py:141
  57.7 2.0 collective-permute-start.12
  63.3 2.4 broadcast_select_fusion.1.refs_0_.refs_2_
  67.9 2.6 collective-permute-start.11
  70.5 13.7 %expert.4 = (bf16[80,4096]{1,0:T(8,128)(2,1)}, bf16[80,4096]{1,0:T(8,128)(2,1)}, bf16[80,4096]{1,0:T(8,128)(2,1)}, bf16[80,4096]{1,0:T(8,128)(2,1)}) custom-call(bf16[80,4096]{1,0:T(8,128)(2,1)} %get-tuple-element.65.refs_1_.refs_0_, bf16[80,4096]{1,0:T(8,128)(2,1)} %pin.30.refs_1_, bf16[80,4096]{1,0:T(8,128)(2,1)} %get-tuple-element.69.refs_1_.refs_2_, ...), custom_call_target="tpu_custom_call" | custom-call | flops 6000000000 | bytes 24000000 | tf_op jit(solution)/shard_map/expert/pallas_call | solution.py:252
  84.3 2.2 collective-permute-done.11.refs_0_
  87.5 4.5 %select.11 = (bf16[80,4096]{1,0:T(8,128)(2,1)}, bf16[80,4096]{1,0:T(8,128)(2,1)}, bf16[80,4096]{1,0:T(8,128)(2,1)}, bf16[80,4096]{1,0:T(8,128)(2,1)}) custom-call(s32[4]{0:T(128)} %dynamic-slice_bitcast_fusion.refs_1_.ids, bf16[128,4224]{1,0:T(8,128)(2,1)} %broadcast_select_fusion.1.refs_0_.refs_2_, bf16[128,4224]{1,0:T(8,128)(2,1)} %pin.39.refs_1_.refs_3_.refs_4_.refs_0_, ...), custom_call_target="tpu_custom_call" | custom-call | flops 2000000000 | bytes 6000000 | tf_op jit(solution)/shard_map/select/pallas_call | solution.py:141
  92.1 1.8 collective-permute-start.15
  93.8 1.8 collective-permute-start.16
  98.0 1.4 broadcast_select_fusion.refs_0_.refs_2_
  100.3 13.8 %expert.5 = (bf16[80,4096]{1,0:T(8,128)(2,1)}, bf16[80,4096]{1,0:T(8,128)(2,1)}, bf16[80,4096]{1,0:T(8,128)(2,1)}, bf16[80,4096]{1,0:T(8,128)(2,1)}) custom-call(bf16[80,4096]{1,0:T(8,128)(2,1)} %get-tuple-element.72.refs_1_.refs_0_, bf16[80,4096]{1,0:T(8,128)(2,1)} %pin.37.refs_7_.refs_1_, bf16[80,4096]{1,0:T(8,128)(2,1)} %get-tuple-element.79.refs_1_.refs_2_, ...), custom_call_target="tpu_custom_call" | custom-call | flops 6000000000 | bytes 24000000 | tf_op jit(solution)/shard_map/expert/pallas_call | solution.py:252
  114.1 3.7 %collective-permute-done.16.refs_1_ = bf16[80,4096]{1,0:T(8,128)(2,1)} collective-permute-done((bf16[80,4096]{1,0:T(8,128)(2,1)}, bf16[80,4096]{1,0:T(8,128)(2,1)}, u32[]{:S(2)}, u32[]{:S(2)}) %collective-permute-start.16) | collective-permute-done | bytes 655392 | tf_op jit(solution)/shard_map/ppermute | solution.py:72
  117.8 3.7 %collective-permute-done.14.refs_0_ = bf16[128,4224]{1,0:T(8,128)(2,1)S(1)} collective-permute-done((bf16[128,4224]{1,0:T(8,128)(2,1)S(1)}, bf16[128,4224]{1,0:T(8,128)(2,1)S(1)}, u32[]{:S(2)}, u32[]{:S(2)}) %collective-permute-start.14) | collective-permute-done | bytes 1081376 | tf_op jit(solution)/shard_map/ppermute | solution.py:72
  122.6 4.5 %select.12 = (bf16[80,4096]{1,0:T(8,128)(2,1)}, bf16[80,4096]{1,0:T(8,128)(2,1)}, bf16[80,4096]{1,0:T(8,128)(2,1)}, bf16[80,4096]{1,0:T(8,128)(2,1)}) custom-call(s32[4]{0:T(128)} %dynamic-slice_bitcast_fusion.refs_1_.ids, bf16[128,4224]{1,0:T(8,128)(2,1)} %copy-done.16, bf16[128,4224]{1,0:T(8,128)(2,1)} %pin.43.refs_1_.refs_3_.refs_4_.refs_0_, ...), custom_call_target="tpu_custom_call" | custom-call | flops 2000000000 | bytes 6000000 | tf_op jit(solution)/shard_map/select/pallas_call | solution.py:141
  127.2 1.8 collective-permute-start.19
  130.2 13.7 %expert.6 = (bf16[80,4096]{1,0:T(8,128)(2,1)}, bf16[80,4096]{1,0:T(8,128)(2,1)}, bf16[80,4096]{1,0:T(8,128)(2,1)}, bf16[80,4096]{1,0:T(8,128)(2,1)}) custom-call(bf16[80,4096]{1,0:T(8,128)(2,1)} %get-tuple-element.80.refs_1_.refs_0_, bf16[80,4096]{1,0:T(8,128)(2,1)} %pin.41.refs_7_.refs_1_, bf16[80,4096]{1,0:T(8,128)(2,1)} %get-tuple-element.86.refs_1_.refs_2_, ...), custom_call_target="tpu_custom_call" | custom-call | flops 6000000000 | bytes 24000000 | tf_op jit(solution)/shard_map/expert/pallas_call | solution.py:252
  145.9 13.8 %expert.7 = (bf16[80,4096]{1,0:T(8,128)(2,1)}, bf16[80,4096]{1,0:T(8,128)(2,1)}, bf16[80,4096]{1,0:T(8,128)(2,1)}, bf16[80,4096]{1,0:T(8,128)(2,1)}) custom-call(bf16[80,4096]{1,0:T(8,128)(2,1)} %get-tuple-element.87.refs_7_.refs_0_, bf16[80,4096]{1,0:T(8,128)(2,1)} %pin.44.refs_2_.refs_1_, bf16[80,4096]{1,0:T(8,128)(2,1)} %get-tuple-element.93.refs_2_.refs_7_, ...), custom_call_target="tpu_custom_call" | custom-call | flops 6000000000 | bytes 24000000 | tf_op jit(solution)/shard_map/expert/pallas_call | solution.py:252
  163.2 4.6 %mix.8.refs_3_ = bf16[128,4096]{1,0:T(8,128)(2,1)} custom-call(s32[4]{0:T(128)} %dynamic-slice_bitcast_fusion.refs_1_.ids, bf16[128,4224]{1,0:T(8,128)(2,1)} %pin.39.refs_1_.refs_3_.refs_4_.refs_0_, bf16[80,4096]{1,0:T(8,128)(2,1)} %get-tuple-element.90.refs_1_, bf16[80,4096]{1,0:T(8,128)(2,1)} %get-tuple-element.102.refs_2_.refs_5_, ...), custom_call_target="tpu_custom_call" | custom-call | flops 2000000000 | bytes 6000000 | tf_op jit(solution)/shard_map/mix/pallas_call | solution.py:190
  168.1 10.0 %collective-permute-done.22.refs_1_ = bf16[80,4096]{1,0:T(8,128)(2,1)} collective-permute-done((bf16[80,4096]{1,0:T(8,128)(2,1)}, bf16[80,4096]{1,0:T(8,128)(2,1)}, u32[]{:S(2)}, u32[]{:S(2)}) %collective-permute-start.22) | collective-permute-done | bytes 655392 | tf_op jit(solution)/shard_map/ppermute | solution.py:72
  178.4 4.6 %mix.9.refs_1_ = bf16[128,4096]{1,0:T(8,128)(2,1)} custom-call(s32[4]{0:T(128)} %dynamic-slice_bitcast_fusion.refs_1_.ids, bf16[128,4224]{1,0:T(8,128)(2,1)} %pin.43.refs_1_.refs_3_.refs_4_.refs_0_, bf16[80,4096]{1,0:T(8,128)(2,1)} %get-tuple-element.95.refs_3_.refs_1_, bf16[80,4096]{1,0:T(8,128)(2,1)} %get-tuple-element.105.refs_2_.refs_5_, ...), custom_call_target="tpu_custom_call" | custom-call | flops 2000000000 | bytes 6000000 | tf_op jit(solution)/shard_map/mix/pallas_call | solution.py:190
  183.6 5.1 %collective-permute-done.28.refs_0_ = bf16[128,4096]{1,0:T(8,128)(2,1)S(1)} collective-permute-done((bf16[128,4096]{1,0:T(8,128)(2,1)}, bf16[128,4096]{1,0:T(8,128)(2,1)S(1)}, u32[]{:S(2)}, u32[]{:S(2)}) %collective-permute-start.28) | collective-permute-done | bytes 1048608 | tf_op jit(solution)/shard_map/ppermute | solution.py:72
  189.6 4.9 %mix.10.refs_4_ = bf16[128,4096]{1,0:T(8,128)(2,1)} custom-call(s32[4]{0:T(128)} %dynamic-slice_bitcast_fusion.refs_1_.ids, bf16[128,4224]{1,0:T(8,128)(2,1)} %broadcast_select_fusion.1.refs_0_.refs_2_, bf16[80,4096]{1,0:T(8,128)(2,1)} %get-tuple-element.90.refs_1_, bf16[80,4096]{1,0:T(8,128)(2,1)} %get-tuple-element.102.refs_2_.refs_5_, ...), custom_call_target="tpu_custom_call" | custom-call | flops 2000000000 | bytes 6000000 | tf_op jit(solution)/shard_map/mix/pallas_call | solution.py:190
  194.5 3.3 %collective-permute-start.34 = (bf16[128,4096]{1,0:T(8,128)(2,1)}, bf16[128,4096]{1,0:T(8,128)(2,1)S(1)}, u32[]{:S(2)}, u32[]{:S(2)}) collective-permute-start(bf16[128,4096]{1,0:T(8,128)(2,1)} %mix.10.refs_4_), channel_id=1, source_target_pairs={{0,8},{1,9},{2,10},{3,11},{4,12},{5,13},{6,14},{7,15},{24,16},{25,... | collective-permute-start | bytes 3145736 | tf_op jit(solution)/shard_map/ppermute | solution.py:72
  201.0 4.8 %mix.11.refs_3_ = bf16[128,4096]{1,0:T(8,128)(2,1)} custom-call(s32[4]{0:T(128)} %dynamic-slice_bitcast_fusion.refs_1_.ids, bf16[128,4224]{1,0:T(8,128)(2,1)} %copy-done.16, bf16[80,4096]{1,0:T(8,128)(2,1)} %get-tuple-element.95.refs_3_.refs_1_, bf16[80,4096]{1,0:T(8,128)(2,1)} %get-tuple-element.105.refs_2_.refs_5_, ...), custom_call_target="tpu_custom_call" | custom-call | flops 2000000000 | bytes 6000000 | tf_op jit(solution)/shard_map/mix/pallas_call | solution.py:190
  205.9 10.5 %collective-permute-done.31.refs_1_ = bf16[80,4096]{1,0:T(8,128)(2,1)} collective-permute-done((bf16[80,4096]{1,0:T(8,128)(2,1)}, bf16[80,4096]{1,0:T(8,128)(2,1)}, u32[]{:S(2)}, u32[]{:S(2)}) %collective-permute-start.31) | collective-permute-done | bytes 655392 | tf_op jit(solution)/shard_map/ppermute | solution.py:72
  216.5 4.6 %mix.12.refs_1_ = bf16[128,4096]{1,0:T(8,128)(2,1)} custom-call(s32[4]{0:T(128)} %dynamic-slice_bitcast_fusion.refs_1_.ids, bf16[128,4224]{1,0:T(8,128)(2,1)} %pin.34.refs_1_.refs_3_.refs_4_.refs_0_, bf16[80,4096]{1,0:T(8,128)(2,1)} %get-tuple-element.111.refs_1_, bf16[80,4096]{1,0:T(8,128)(2,1)} %get-tuple-element.115.refs_2_.refs_5_, ...), custom_call_target="tpu_custom_call" | custom-call | flops 2000000000 | bytes 6000000 | tf_op jit(solution)/shard_map/mix/pallas_call | solution.py:190
  221.7 1.6 collective-permute-start.29
  224.3 2.5 add_convert_fusion.1
  227.5 8.7 %collective-permute-done.33.refs_0_ = bf16[128,4096]{1,0:T(8,128)(2,1)} collective-permute-done((bf16[128,4096]{1,0:T(8,128)(2,1)}, bf16[128,4096]{1,0:T(8,128)(2,1)}, u32[]{:S(2)}, u32[]{:S(2)}) %collective-permute-start.33) | collective-permute-done | bytes 1048608 | tf_op jit(solution)/shard_map/ppermute | solution.py:72
  236.2 4.8 %mix.13.refs_1_ = bf16[128,4096]{1,0:T(8,128)(2,1)} custom-call(s32[4]{0:T(128)} %dynamic-slice_bitcast_fusion.refs_1_.ids, bf16[128,4224]{1,0:T(8,128)(2,1)} %pin.31.refs_1_.refs_0_.refs_2_, bf16[80,4096]{1,0:T(8,128)(2,1)} %get-tuple-element.111.refs_1_, bf16[80,4096]{1,0:T(8,128)(2,1)} %get-tuple-element.115.refs_2_.refs_5_, ...), custom_call_target="tpu_custom_call" | custom-call | flops 2000000000 | bytes 6000000 | tf_op jit(solution)/shard_map/mix/pallas_call | solution.py:190
  241.0 6.1 %collective-permute-done.29.refs_0_ = bf16[128,4096]{1,0:T(8,128)(2,1)S(1)} collective-permute-done((bf16[128,4096]{1,0:T(8,128)(2,1)}, bf16[128,4096]{1,0:T(8,128)(2,1)S(1)}, u32[]{:S(2)}, u32[]{:S(2)}) %collective-permute-start.29) | collective-permute-done | bytes 1048608 | tf_op jit(solution)/shard_map/ppermute | solution.py:72
  250.0 2.5 add_convert_fusion
  253.7 11.7 %collective-permute-done.36.refs_1_ = bf16[80,4096]{1,0:T(8,128)(2,1)S(1)} collective-permute-done((bf16[80,4096]{1,0:T(8,128)(2,1)}, bf16[80,4096]{1,0:T(8,128)(2,1)S(1)}, u32[]{:S(2)}, u32[]{:S(2)}) %collective-permute-start.36) | collective-permute-done | bytes 655392 | tf_op jit(solution)/shard_map/ppermute | solution.py:72
  266.3 4.6 %mix.14.refs_1_ = bf16[128,4096]{1,0:T(8,128)(2,1)} custom-call(s32[4]{0:T(128)} %dynamic-slice_bitcast_fusion.refs_1_.ids, bf16[128,4224]{1,0:T(8,128)(2,1)} %pin.29.refs_1_.refs_3_.refs_4_.refs_0_, bf16[80,4096]{1,0:T(8,128)(2,1)} %get-tuple-element.118.refs_3_.refs_1_, bf16[80,4096]{1,0:T(8,128)(2,1)} %get-tuple-element.122.refs_2_.refs_5_, ...), custom_call_target="tpu_custom_call" | custom-call | flops 2000000000 | bytes 6000000 | tf_op jit(solution)/shard_map/mix/pallas_call | solution.py:190
  270.9 1.8 collective-permute-start.38
  273.6 7.4 %collective-permute-done.41.refs_8_ = bf16[128,4096]{1,0:T(8,128)(2,1)S(1)} collective-permute-done((bf16[128,4096]{1,0:T(8,128)(2,1)}, bf16[128,4096]{1,0:T(8,128)(2,1)S(1)}, u32[]{:S(2)}, u32[]{:S(2)}) %collective-permute-start.41) | collective-permute-done | bytes 1048608 | tf_op jit(solution)/shard_map/ppermute | solution.py:72
  281.0 6.2 %collective-permute-done.40.refs_7_ = bf16[128,4096]{1,0:T(8,128)(2,1)} collective-permute-done((bf16[128,4096]{1,0:T(8,128)(2,1)}, bf16[128,4096]{1,0:T(8,128)(2,1)}, u32[]{:S(2)}, u32[]{:S(2)}) %collective-permute-start.40) | collective-permute-done | bytes 1048608 | tf_op jit(solution)/shard_map/ppermute | solution.py:72
  288.2 5.7 %mix.15 = bf16[128,4096]{1,0:T(8,128)(2,1)} custom-call(s32[4]{0:T(128)} %dynamic-slice_bitcast_fusion.refs_1_.ids, bf16[128,4224]{1,0:T(8,128)(2,1)} %copy-done.8, bf16[80,4096]{1,0:T(8,128)(2,1)} %get-tuple-element.118.refs_3_.refs_1_, bf16[80,4096]{1,0:T(8,128)(2,1)} %get-tuple-element.122.refs_2_.refs_5_, bf16[80,4096]{1,0:T(8,128)(2,1)} %get-tuple-element.123.refs_3_, ...), custom_call_target="tpu_custom_call" | custom-call | flops 2000000000 | bytes 6000000 | tf_op jit(solution)/shard_map/mix/pallas_call | solution.py:190
  (147 shorter events, 41.4 us)
Async XLA Ops:
  2.7 16.3 %copy-start.8 = (bf16[128,4224]{1,0:T(8,128)(2,1)}, bf16[128,4224]{1,0:T(8,128)(2,1)S(1)}, u32[]{:S(2)}) copy-start(bf16[128,4224]{1,0:T(8,128)(2,1)S(1)} %fusion.1.refs_0_.refs_2_) | copy-start | bytes 3244036
  2.7 16.2 %collective-permute-start = (bf16[128,4224]{1,0:T(8,128)(2,1)S(1)}, bf16[128,4224]{1,0:T(8,128)(2,1)}, u32[]{:S(2)}, u32[]{:S(2)}) collective-permute-start(bf16[128,4224]{1,0:T(8,128)(2,1)S(1)} %fusion.1.refs_0_.refs_2_), channel_id=1, source_target_pairs={{0,2},{1,5},{2,0},{3,7},{4,6},{5,1},{6,4},{7,3},{8,10},{9,13},{10,... | collective-permute-start | bytes 3244040 | tf_op jit(solution)/shard_map/ppermute | solution.py:72
  5.7 25.3 %collective-permute-start.5 = (bf16[128,4224]{1,0:T(8,128)(2,1)S(1)}, bf16[128,4224]{1,0:T(8,128)(2,1)S(1)}, u32[]{:S(2)}, u32[]{:S(2)}) collective-permute-start(bf16[128,4224]{1,0:T(8,128)(2,1)S(1)} %fusion.1.refs_0_.refs_2_), channel_id=1, source_target_pairs={{0,8},{1,9},{2,10},{3,11},{4,12},{5,13},{6,14},{7,15},{8,0},{9,1},... | collective-permute-start | bytes 3244040 | tf_op jit(solution)/shard_map/ppermute | solution.py:72
  7.3 26.2 %collective-permute-start.4 = (bf16[128,4224]{1,0:T(8,128)(2,1)S(1)}, bf16[128,4224]{1,0:T(8,128)(2,1)S(1)}, u32[]{:S(2)}, u32[]{:S(2)}) collective-permute-start(bf16[128,4224]{1,0:T(8,128)(2,1)S(1)} %fusion.1.refs_0_.refs_2_), channel_id=1, source_target_pairs={{8,16},{9,17},{10,18},{11,19},{12,20},{13,21},{14,22},{15,23},{16,... | collective-permute-start | bytes 3244040 | tf_op jit(solution)/shard_map/ppermute | solution.py:72
  23.5 3.4 %collective-permute-start.1 = (bf16[80,4096]{1,0:T(8,128)(2,1)}, bf16[80,4096]{1,0:T(8,128)(2,1)}, u32[]{:S(2)}, u32[]{:S(2)}) collective-permute-start(bf16[80,4096]{1,0:T(8,128)(2,1)} %get-tuple-element.66), channel_id=1, source_target_pairs={{0,1},{1,0},{2,3},{3,2},{4,5},{5,4},{6,7},{7,6},{8,9},{9,8},{10,11... | collective-permute-start | bytes 1966088 | tf_op jit(solution)/shard_map/ppermute | solution.py:72
  23.5 13.0 %collective-permute-start.2 = (bf16[80,4096]{1,0:T(8,128)(2,1)}, bf16[80,4096]{1,0:T(8,128)(2,1)}, u32[]{:S(2)}, u32[]{:S(2)}) collective-permute-start(bf16[80,4096]{1,0:T(8,128)(2,1)} %get-tuple-element.67), channel_id=1, source_target_pairs={{0,4},{1,3},{2,6},{3,1},{4,0},{5,7},{6,2},{7,5},{8,12},{9,11},{10,... | collective-permute-start | bytes 1966088 | tf_op jit(solution)/shard_map/ppermute | solution.py:72
  25.6 24.9 %collective-permute-start.3 = (bf16[80,4096]{1,0:T(8,128)(2,1)}, bf16[80,4096]{1,0:T(8,128)(2,1)}, u32[]{:S(2)}, u32[]{:S(2)}) collective-permute-start(bf16[80,4096]{1,0:T(8,128)(2,1)} %get-tuple-element.68), channel_id=1, source_target_pairs={{0,5},{1,2},{2,7},{3,0},{4,1},{5,6},{6,3},{7,4},{8,13},{9,10},{10,... | collective-permute-start | bytes 1966088 | tf_op jit(solution)/shard_map/ppermute | solution.py:72
  32.0 20.8 %collective-permute-start.6 = (bf16[128,4224]{1,0:T(8,128)(2,1)}, bf16[128,4224]{1,0:T(8,128)(2,1)}, u32[]{:S(2)}, u32[]{:S(2)}) collective-permute-start(bf16[128,4224]{1,0:T(8,128)(2,1)} %pin.31.refs_1_.refs_0_.refs_2_), channel_id=1, source_target_pairs={{0,2},{1,5},{2,0},{3,7},{4,6},{5,1},{6,4},{7,3},{8,10},{9,13},{10,... | collective-permute-start | bytes 3244040 | tf_op jit(solution)/shard_map/ppermute | solution.py:72
  34.5 26.4 %collective-permute-start.9 = (bf16[128,4224]{1,0:T(8,128)(2,1)}, bf16[128,4224]{1,0:T(8,128)(2,1)S(1)}, u32[]{:S(2)}, u32[]{:S(2)}) collective-permute-start(bf16[128,4224]{1,0:T(8,128)(2,1)} %pin.32.refs_2_), channel_id=1, source_target_pairs={{8,0},{9,1},{10,2},{11,3},{12,4},{13,5},{14,6},{15,7},{16,24},{17,... | collective-permute-start | bytes 3244040 | tf_op jit(solution)/shard_map/ppermute | solution.py:72
  35.8 29.8 %collective-permute-start.8 = (bf16[128,4224]{1,0:T(8,128)(2,1)}, bf16[128,4224]{1,0:T(8,128)(2,1)S(1)}, u32[]{:S(2)}, u32[]{:S(2)}) collective-permute-start(bf16[128,4224]{1,0:T(8,128)(2,1)} %pin.31.refs_1_.refs_0_.refs_2_), channel_id=1, source_target_pairs={{8,16},{9,17},{10,18},{11,19},{12,20},{13,21},{14,22},{15,23},{16,... | collective-permute-start | bytes 3244040 | tf_op jit(solution)/shard_map/ppermute | solution.py:72
  57.4 13.1 %collective-permute-start.7 = (bf16[80,4096]{1,0:T(8,128)(2,1)}, bf16[80,4096]{1,0:T(8,128)(2,1)}, u32[]{:S(2)}, u32[]{:S(2)}) collective-permute-start(bf16[80,4096]{1,0:T(8,128)(2,1)} %get-tuple-element.71), channel_id=1, source_target_pairs={{0,1},{1,0},{2,3},{3,2},{4,5},{5,4},{6,7},{7,6},{8,9},{9,8},{10,11... | collective-permute-start | bytes 1966088 | tf_op jit(solution)/shard_map/ppermute | solution.py:72
  57.7 26.5 %collective-permute-start.12 = (bf16[80,4096]{1,0:T(8,128)(2,1)}, bf16[80,4096]{1,0:T(8,128)(2,1)}, u32[]{:S(2)}, u32[]{:S(2)}) collective-permute-start(bf16[80,4096]{1,0:T(8,128)(2,1)} %get-tuple-element.77), channel_id=1, source_target_pairs={{0,4},{1,3},{2,6},{3,1},{4,0},{5,7},{6,2},{7,5},{8,12},{9,11},{10,... | collective-permute-start | bytes 1966088 | tf_op jit(solution)/shard_map/ppermute | solution.py:72
  59.8 24.5 %collective-permute-start.13 = (bf16[80,4096]{1,0:T(8,128)(2,1)}, bf16[80,4096]{1,0:T(8,128)(2,1)}, u32[]{:S(2)}, u32[]{:S(2)}) collective-permute-start(bf16[80,4096]{1,0:T(8,128)(2,1)} %get-tuple-element.78), channel_id=1, source_target_pairs={{0,5},{1,2},{2,7},{3,0},{4,1},{5,6},{6,3},{7,4},{8,13},{9,10},{10,... | collective-permute-start | bytes 1966088 | tf_op jit(solution)/shard_map/ppermute | solution.py:72
  66.6 29.1 %collective-permute-start.10 = (bf16[128,4224]{1,0:T(8,128)(2,1)}, bf16[128,4224]{1,0:T(8,128)(2,1)S(1)}, u32[]{:S(2)}, u32[]{:S(2)}) collective-permute-start(bf16[128,4224]{1,0:T(8,128)(2,1)} %pin.36.refs_1_), channel_id=1, source_target_pairs={{8,0},{9,1},{10,2},{11,3},{12,4},{13,5},{14,6},{15,7},{16,24},{17,... | collective-permute-start | bytes 3244040 | tf_op jit(solution)/shard_map/ppermute | solution.py:72
  67.9 18.6 %collective-permute-start.11 = (bf16[128,4224]{1,0:T(8,128)(2,1)S(1)}, bf16[128,4224]{1,0:T(8,128)(2,1)S(1)}, u32[]{:S(2)}, u32[]{:S(2)}) collective-permute-start(bf16[128,4224]{1,0:T(8,128)(2,1)S(1)} %copy-done.15), channel_id=1, source_target_pairs={{0,2},{1,5},{2,0},{3,7},{4,6},{5,1},{6,4},{7,3},{8,10},{9,13},{10,... | collective-permute-start | bytes 3244040 | tf_op jit(solution)/shard_map/ppermute | solution.py:72
  92.1 22.0 %collective-permute-start.15 = (bf16[80,4096]{1,0:T(8,128)(2,1)}, bf16[80,4096]{1,0:T(8,128)(2,1)}, u32[]{:S(2)}, u32[]{:S(2)}) collective-permute-start(bf16[80,4096]{1,0:T(8,128)(2,1)} %get-tuple-element.81), channel_id=1, source_target_pairs={{0,4},{1,3},{2,6},{3,1},{4,0},{5,7},{6,2},{7,5},{8,12},{9,11},{10,... | collective-permute-start | bytes 1966088 | tf_op jit(solution)/shard_map/ppermute | solution.py:72
  93.8 24.0 %collective-permute-start.16 = (bf16[80,4096]{1,0:T(8,128)(2,1)}, bf16[80,4096]{1,0:T(8,128)(2,1)}, u32[]{:S(2)}, u32[]{:S(2)}) collective-permute-start(bf16[80,4096]{1,0:T(8,128)(2,1)} %get-tuple-element.82), channel_id=1, source_target_pairs={{0,5},{1,2},{2,7},{3,0},{4,1},{5,6},{6,3},{7,4},{8,13},{9,10},{10,... | collective-permute-start | bytes 1966088 | tf_op jit(solution)/shard_map/ppermute | solution.py:72
  95.6 4.5 %collective-permute-start.17 = (bf16[80,4096]{1,0:T(8,128)(2,1)}, bf16[80,4096]{1,0:T(8,128)(2,1)}, u32[]{:S(2)}, u32[]{:S(2)}) collective-permute-start(bf16[80,4096]{1,0:T(8,128)(2,1)} %get-tuple-element.84), channel_id=1, source_target_pairs={{0,1},{1,0},{2,3},{3,2},{4,5},{5,4},{6,7},{7,6},{8,9},{9,8},{10,11... | collective-permute-start | bytes 1966088 | tf_op jit(solution)/shard_map/ppermute | solution.py:72
  99.3 22.1 %collective-permute-start.14 = (bf16[128,4224]{1,0:T(8,128)(2,1)S(1)}, bf16[128,4224]{1,0:T(8,128)(2,1)S(1)}, u32[]{:S(2)}, u32[]{:S(2)}) collective-permute-start(bf16[128,4224]{1,0:T(8,128)(2,1)S(1)} %broadcast_select_fusion.refs_0_.refs_2_), channel_id=1, source_target_pairs={{0,2},{1,5},{2,0},{3,7},{4,6},{5,1},{6,4},{7,3},{8,10},{9,13},{10,... | collective-permute-start | bytes 3244040 | tf_op jit(solution)/shard_map/ppermute | solution.py:72
  127.1 17.8 %collective-permute-start.18 = (bf16[80,4096]{1,0:T(8,128)(2,1)}, bf16[80,4096]{1,0:T(8,128)(2,1)S(1)}, u32[]{:S(2)}, u32[]{:S(2)}) collective-permute-start(bf16[80,4096]{1,0:T(8,128)(2,1)} %get-tuple-element.88), channel_id=1, source_target_pairs={{0,1},{1,0},{2,3},{3,2},{4,5},{5,4},{6,7},{7,6},{8,9},{9,8},{10,11... | collective-permute-start | bytes 1966088 | tf_op jit(solution)/shard_map/ppermute | solution.py:72
  127.2 18.7 %collective-permute-start.19 = (bf16[80,4096]{1,0:T(8,128)(2,1)}, bf16[80,4096]{1,0:T(8,128)(2,1)}, u32[]{:S(2)}, u32[]{:S(2)}) collective-permute-start(bf16[80,4096]{1,0:T(8,128)(2,1)} %get-tuple-element.91), channel_id=1, source_target_pairs={{0,4},{1,3},{2,6},{3,1},{4,0},{5,7},{6,2},{7,5},{8,12},{9,11},{10,... | collective-permute-start | bytes 1966088 | tf_op jit(solution)/shard_map/ppermute | solution.py:72
  129.0 16.9 %collective-permute-start.20 = (bf16[80,4096]{1,0:T(8,128)(2,1)}, bf16[80,4096]{1,0:T(8,128)(2,1)}, u32[]{:S(2)}, u32[]{:S(2)}) collective-permute-start(bf16[80,4096]{1,0:T(8,128)(2,1)} %get-tuple-element.92), channel_id=1, source_target_pairs={{0,5},{1,2},{2,7},{3,0},{4,1},{5,6},{6,3},{7,4},{8,13},{9,10},{10,... | collective-permute-start | bytes 1966088 | tf_op jit(solution)/shard_map/ppermute | solution.py:72
  144.0 17.2 %collective-permute-start.24 = (bf16[80,4096]{1,0:T(8,128)(2,1)}, bf16[80,4096]{1,0:T(8,128)(2,1)S(1)}, u32[]{:S(2)}, u32[]{:S(2)}) collective-permute-start(bf16[80,4096]{1,0:T(8,128)(2,1)} %get-tuple-element.99), channel_id=1, source_target_pairs={{1,0},{0,1},{3,2},{2,3},{5,4},{4,5},{7,6},{6,7},{9,8},{8,9},{11,10... | collective-permute-start | bytes 1966088 | tf_op jit(solution)/shard_map/ppermute | solution.py:72
  144.4 17.8 %collective-permute-start.25 = (bf16[80,4096]{1,0:T(8,128)(2,1)}, bf16[80,4096]{1,0:T(8,128)(2,1)S(1)}, u32[]{:S(2)}, u32[]{:S(2)}) collective-permute-start(bf16[80,4096]{1,0:T(8,128)(2,1)} %get-tuple-element.100), channel_id=1, source_target_pairs={{4,0},{3,1},{6,2},{1,3},{0,4},{7,5},{2,6},{5,7},{12,8},{11,9},{14,... | collective-permute-start | bytes 1966088 | tf_op jit(solution)/shard_map/ppermute | solution.py:72
  144.9 17.2 %collective-permute-start.26 = (bf16[80,4096]{1,0:T(8,128)(2,1)}, bf16[80,4096]{1,0:T(8,128)(2,1)S(1)}, u32[]{:S(2)}, u32[]{:S(2)}) collective-permute-start(bf16[80,4096]{1,0:T(8,128)(2,1)} %get-tuple-element.101), channel_id=1, source_target_pairs={{5,0},{2,1},{7,2},{0,3},{1,4},{6,5},{3,6},{4,7},{13,8},{10,9},{15,... | collective-permute-start | bytes 1966088 | tf_op jit(solution)/shard_map/ppermute | solution.py:72
  159.7 8.4 %collective-permute-start.21 = (bf16[80,4096]{1,0:T(8,128)(2,1)}, bf16[80,4096]{1,0:T(8,128)(2,1)S(1)}, u32[]{:S(2)}, u32[]{:S(2)}) collective-permute-start(bf16[80,4096]{1,0:T(8,128)(2,1)} %get-tuple-element.96), channel_id=1, source_target_pairs={{1,0},{0,1},{3,2},{2,3},{5,4},{4,5},{7,6},{6,7},{9,8},{8,9},{11,10... | collective-permute-start | bytes 1966088 | tf_op jit(solution)/shard_map/ppermute | solution.py:72
  160.4 17.7 %collective-permute-start.22 = (bf16[80,4096]{1,0:T(8,128)(2,1)}, bf16[80,4096]{1,0:T(8,128)(2,1)}, u32[]{:S(2)}, u32[]{:S(2)}) collective-permute-start(bf16[80,4096]{1,0:T(8,128)(2,1)} %get-tuple-element.97), channel_id=1, source_target_pairs={{4,0},{3,1},{6,2},{1,3},{0,4},{7,5},{2,6},{5,7},{12,8},{11,9},{14,... | collective-permute-start | bytes 1966088 | tf_op jit(solution)/shard_map/ppermute | solution.py:72
  161.2 17.1 %collective-permute-start.23 = (bf16[80,4096]{1,0:T(8,128)(2,1)}, bf16[80,4096]{1,0:T(8,128)(2,1)}, u32[]{:S(2)}, u32[]{:S(2)}) collective-permute-start(bf16[80,4096]{1,0:T(8,128)(2,1)} %get-tuple-element.98), channel_id=1, source_target_pairs={{5,0},{2,1},{7,2},{0,3},{1,4},{6,5},{3,6},{4,7},{13,8},{10,9},{15,... | collective-permute-start | bytes 1966088 | tf_op jit(solution)/shard_map/ppermute | solution.py:72
  167.8 20.8 %collective-permute-start.28 = (bf16[128,4096]{1,0:T(8,128)(2,1)}, bf16[128,4096]{1,0:T(8,128)(2,1)S(1)}, u32[]{:S(2)}, u32[]{:S(2)}) collective-permute-start(bf16[128,4096]{1,0:T(8,128)(2,1)} %mix.8.refs_3_), channel_id=1, source_target_pairs={{0,2},{1,5},{2,0},{3,7},{4,6},{5,1},{6,4},{7,3},{8,10},{9,13},{10,... | collective-permute-start | bytes 3145736 | tf_op jit(solution)/shard_map/ppermute | solution.py:72
  168.1 10.2 %copy-start.26 = (bf16[80,4096]{1,0:T(8,128)(2,1)}, bf16[80,4096]{1,0:T(8,128)(2,1)S(1)}, u32[]{:S(2)}) copy-start(bf16[80,4096]{1,0:T(8,128)(2,1)S(1)} %collective-permute-done.21.refs_0_) | copy-start | bytes 1966084
  183.0 17.1 %collective-permute-start.27 = (bf16[128,4096]{1,0:T(8,128)(2,1)}, bf16[128,4096]{1,0:T(8,128)(2,1)S(1)}, u32[]{:S(2)}, u32[]{:S(2)}) collective-permute-start(bf16[128,4096]{1,0:T(8,128)(2,1)} %mix.9.refs_1_), channel_id=1, source_target_pairs={{0,2},{1,5},{2,0},{3,7},{4,6},{5,1},{6,4},{7,3},{8,10},{9,13},{10,... | collective-permute-start | bytes 3145736 | tf_op jit(solution)/shard_map/ppermute | solution.py:72
  194.5 28.8 %collective-permute-start.34 = (bf16[128,4096]{1,0:T(8,128)(2,1)}, bf16[128,4096]{1,0:T(8,128)(2,1)S(1)}, u32[]{:S(2)}, u32[]{:S(2)}) collective-permute-start(bf16[128,4096]{1,0:T(8,128)(2,1)} %mix.10.refs_4_), channel_id=1, source_target_pairs={{0,8},{1,9},{2,10},{3,11},{4,12},{5,13},{6,14},{7,15},{24,16},{25,... | collective-permute-start | bytes 3145736 | tf_op jit(solution)/shard_map/ppermute | solution.py:72
  197.8 8.0 %collective-permute-start.30 = (bf16[80,4096]{1,0:T(8,128)(2,1)}, bf16[80,4096]{1,0:T(8,128)(2,1)S(1)}, u32[]{:S(2)}, u32[]{:S(2)}) collective-permute-start(bf16[80,4096]{1,0:T(8,128)(2,1)} %get-tuple-element.112), channel_id=1, source_target_pairs={{1,0},{0,1},{3,2},{2,3},{5,4},{4,5},{7,6},{6,7},{9,8},{8,9},{11,10... | collective-permute-start | bytes 1966088 | tf_op jit(solution)/shard_map/ppermute | solution.py:72
  198.6 17.7 %collective-permute-start.31 = (bf16[80,4096]{1,0:T(8,128)(2,1)}, bf16[80,4096]{1,0:T(8,128)(2,1)}, u32[]{:S(2)}, u32[]{:S(2)}) collective-permute-start(bf16[80,4096]{1,0:T(8,128)(2,1)} %get-tuple-element.113), channel_id=1, source_target_pairs={{4,0},{3,1},{6,2},{1,3},{0,4},{7,5},{2,6},{5,7},{12,8},{11,9},{14,... | collective-permute-start | bytes 1966088 | tf_op jit(solution)/shard_map/ppermute | solution.py:72
  199.4 17.1 %collective-permute-start.32 = (bf16[80,4096]{1,0:T(8,128)(2,1)}, bf16[80,4096]{1,0:T(8,128)(2,1)}, u32[]{:S(2)}, u32[]{:S(2)}) collective-permute-start(bf16[80,4096]{1,0:T(8,128)(2,1)} %get-tuple-element.114), channel_id=1, source_target_pairs={{5,0},{2,1},{7,2},{0,3},{1,4},{6,5},{3,6},{4,7},{13,8},{10,9},{15,... | collective-permute-start | bytes 1966088 | tf_op jit(solution)/shard_map/ppermute | solution.py:72
  205.8 10.7 %copy-start.27 = (bf16[80,4096]{1,0:T(8,128)(2,1)}, bf16[80,4096]{1,0:T(8,128)(2,1)S(1)}, u32[]{:S(2)}) copy-start(bf16[80,4096]{1,0:T(8,128)(2,1)S(1)} %collective-permute-done.30.refs_0_) | copy-start | bytes 1966084
  221.1 3.2 %copy-start.12 = (bf16[128,4096]{1,0:T(8,128)(2,1)S(1)}, bf16[128,4096]{1,0:T(8,128)(2,1)}, u32[]{:S(2)}) copy-start(bf16[128,4096]{1,0:T(8,128)(2,1)} %mix.10.refs_4_) | copy-start | bytes 3145732
  221.1 15.1 %collective-permute-start.33 = (bf16[128,4096]{1,0:T(8,128)(2,1)}, bf16[128,4096]{1,0:T(8,128)(2,1)}, u32[]{:S(2)}, u32[]{:S(2)}) collective-permute-start(bf16[128,4096]{1,0:T(8,128)(2,1)} %mix.12.refs_1_), channel_id=1, source_target_pairs={{0,2},{1,5},{2,0},{3,7},{4,6},{5,1},{6,4},{7,3},{8,10},{9,13},{10,... | collective-permute-start | bytes 3145736 | tf_op jit(solution)/shard_map/ppermute | solution.py:72
  221.7 25.5 %collective-permute-start.29 = (bf16[128,4096]{1,0:T(8,128)(2,1)}, bf16[128,4096]{1,0:T(8,128)(2,1)S(1)}, u32[]{:S(2)}, u32[]{:S(2)}) collective-permute-start(bf16[128,4096]{1,0:T(8,128)(2,1)} %mix.11.refs_3_), channel_id=1, source_target_pairs={{0,8},{1,9},{2,10},{3,11},{4,12},{5,13},{6,14},{7,15},{24,16},{25,... | collective-permute-start | bytes 3145736 | tf_op jit(solution)/shard_map/ppermute | solution.py:72
  226.7 45.9 %collective-permute-start.39 = (bf16[128,4096]{1,0:T(8,128)(2,1)}, bf16[128,4096]{1,0:T(8,128)(2,1)S(1)}, u32[]{:S(2)}, u32[]{:S(2)}) collective-permute-start(bf16[128,4096]{1,0:T(8,128)(2,1)} %add_convert_fusion.1), channel_id=1, source_target_pairs={{8,16},{9,17},{10,18},{11,19},{12,20},{13,21},{14,22},{15,23},{16,... | collective-permute-start | bytes 3145736 | tf_op jit(solution)/shard_map/ppermute | solution.py:72
  241.0 46.2 %collective-permute-start.40 = (bf16[128,4096]{1,0:T(8,128)(2,1)}, bf16[128,4096]{1,0:T(8,128)(2,1)}, u32[]{:S(2)}, u32[]{:S(2)}) collective-permute-start(bf16[128,4096]{1,0:T(8,128)(2,1)} %mix.13.refs_1_), channel_id=1, source_target_pairs={{0,8},{1,9},{2,10},{3,11},{4,12},{5,13},{6,14},{7,15},{8,0},{9,1},... | collective-permute-start | bytes 3145736 | tf_op jit(solution)/shard_map/ppermute | solution.py:72
  248.1 4.3 %collective-permute-start.35 = (bf16[80,4096]{1,0:T(8,128)(2,1)}, bf16[80,4096]{1,0:T(8,128)(2,1)S(1)}, u32[]{:S(2)}, u32[]{:S(2)}) collective-permute-start(bf16[80,4096]{1,0:T(8,128)(2,1)} %get-tuple-element.119), channel_id=1, source_target_pairs={{1,0},{0,1},{3,2},{2,3},{5,4},{4,5},{7,6},{6,7},{9,8},{8,9},{11,10... | collective-permute-start | bytes 1966088 | tf_op jit(solution)/shard_map/ppermute | solution.py:72
  248.1 17.4 %collective-permute-start.36 = (bf16[80,4096]{1,0:T(8,128)(2,1)}, bf16[80,4096]{1,0:T(8,128)(2,1)S(1)}, u32[]{:S(2)}, u32[]{:S(2)}) collective-permute-start(bf16[80,4096]{1,0:T(8,128)(2,1)} %get-tuple-element.120), channel_id=1, source_target_pairs={{4,0},{3,1},{6,2},{1,3},{0,4},{7,5},{2,6},{5,7},{12,8},{11,9},{14,... | collective-permute-start | bytes 1966088 | tf_op jit(solution)/shard_map/ppermute | solution.py:72
  249.2 16.8 %collective-permute-start.37 = (bf16[80,4096]{1,0:T(8,128)(2,1)}, bf16[80,4096]{1,0:T(8,128)(2,1)}, u32[]{:S(2)}, u32[]{:S(2)}) collective-permute-start(bf16[80,4096]{1,0:T(8,128)(2,1)} %get-tuple-element.121), channel_id=1, source_target_pairs={{5,0},{2,1},{7,2},{0,3},{1,4},{6,5},{3,6},{4,7},{13,8},{10,9},{15,... | collective-permute-start | bytes 1966088 | tf_op jit(solution)/shard_map/ppermute | solution.py:72
  252.4 13.6 %copy-start.13 = (bf16[80,4096]{1,0:T(8,128)(2,1)}, bf16[80,4096]{1,0:T(8,128)(2,1)S(1)}, u32[]{:S(2)}) copy-start(bf16[80,4096]{1,0:T(8,128)(2,1)S(1)} %collective-permute-done.35.refs_0_) | copy-start | bytes 1966084
  252.4 28.6 %collective-permute-start.41 = (bf16[128,4096]{1,0:T(8,128)(2,1)}, bf16[128,4096]{1,0:T(8,128)(2,1)S(1)}, u32[]{:S(2)}, u32[]{:S(2)}) collective-permute-start(bf16[128,4096]{1,0:T(8,128)(2,1)} %add_convert_fusion), channel_id=1, source_target_pairs={{8,24},{9,25},{10,26},{11,27},{12,28},{13,29},{14,30},{15,31},{16,... | collective-permute-start | bytes 3145736 | tf_op jit(solution)/shard_map/ppermute | solution.py:72
  270.9 16.4 %collective-permute-start.38 = (bf16[128,4096]{1,0:T(8,128)(2,1)}, bf16[128,4096]{1,0:T(8,128)(2,1)S(1)}, u32[]{:S(2)}, u32[]{:S(2)}) collective-permute-start(bf16[128,4096]{1,0:T(8,128)(2,1)} %mix.14.refs_1_), channel_id=1, source_target_pairs={{0,2},{1,5},{2,0},{3,7},{4,6},{5,1},{6,4},{7,3},{8,10},{9,13},{10,... | collective-permute-start | bytes 3145736 | tf_op jit(solution)/shard_map/ppermute | solution.py:72
  281.0 6.2 %copy-start.19 = (bf16[128,4096]{1,0:T(8,128)(2,1)}, bf16[128,4096]{1,0:T(8,128)(2,1)S(1)}, u32[]{:S(2)}) copy-start(bf16[128,4096]{1,0:T(8,128)(2,1)S(1)} %collective-permute-done.41.refs_8_) | copy-start | bytes 3145732
  (23 other events, 25.3 us)

commit v3 on v2

--- a/solution.py
+++ b/solution.py
@@ -423,9 +423,9 @@
                 event = climb_on(last - 1, event)
             event = finish(s, event)
             event = climb(s, event)
+            event = give(s - 1, event)
             if s == last - 2:
                 event = climb_on(last, event)
-            event = give(s - 1, event)
     if grid.seq == 4:
         inbox[0:1], event = land(inbox[0:1], event)
     finish(0, event)

time: 295 us -> 294 us (level)
    unnamed x58 -> x52, local copies, waits for them, and re-layouts: 17.1 us -> 15.8 us
where the time goes in v3:
time: 294 us; the launch traced here: 293 us
  Pallas kernels  112 us (38%)
  waiting for transfers between devices  109 us (37%)
  starting transfers between devices  43.5 us (15%)
  local copies, waits for them, and re-layouts  17 us (6%)
  other arithmetic  11.6 us (4%)
    ppermute x42, waiting for transfers between devices, move(): return lax.ppermute(x, AXES, pairs)  109 us
    pallas_call x4, Pallas kernels, expert(): pl.pallas_call(functools.partial(expert_kernel, count, pieces), in_specs=...  55.1 us
    ppermute x42, starting transfers between devices, move(): return lax.ppermute(x, AXES, pairs)  43.5 us
    pallas_call x8, Pallas kernels, mix(): pl.pallas_call(functools.partial(mix_kernel, grid, cap, sources, len(extr...  38.5 us
    pallas_call x4, Pallas kernels, select(): pl.pallas_call(functools.partial(select_kernel, grid, cap), grid_spec=plt...  18.2 us
    unnamed x52, local copies, waits for them, and re-layouts  15.8 us
  transfers between devices with their start and end apart: 42, of which 20 were waited for; matrix products, arithmetic and copies ran while one was open for 3% of the time, Pallas kernels for 35%

profile of v3, /device:TPU:0, one launch (start us, length us, event | category | flops | bytes accessed | tf_op | source)
XLA Modules:
  0.0 293.5 jit_solution(17923081934697956000)
XLA Ops:
  1.4 1.3 fusion.1.refs_0_.refs_2_
  2.7 3.0 %collective-permute-start = (bf16[128,4224]{1,0:T(8,128)(2,1)S(1)}, bf16[128,4224]{1,0:T(8,128)(2,1)}, u32[]{:S(2)}, u32[]{:S(2)}) collective-permute-start(bf16[128,4224]{1,0:T(8,128)(2,1)S(1)} %fusion.1.refs_0_.refs_2_), channel_id=1, source_target_pairs={{0,2},{1,5},{2,0},{3,7},{4,6},{5,1},{6,4},{7,3},{8,10},{9,13},{10,... | collective-permute-start | bytes 3244040 | tf_op jit(solution)/shard_map/ppermute | solution.py:72
  5.7 1.6 collective-permute-start.5
  9.3 9.7 %collective-permute-done.refs_0_ = bf16[128,4224]{1,0:T(8,128)(2,1)} collective-permute-done((bf16[128,4224]{1,0:T(8,128)(2,1)S(1)}, bf16[128,4224]{1,0:T(8,128)(2,1)}, u32[]{:S(2)}, u32[]{:S(2)}) %collective-permute-start) | collective-permute-done | bytes 1081376 | tf_op jit(solution)/shard_map/ppermute | solution.py:72
  18.9 4.5 %select.9 = (bf16[80,4096]{1,0:T(8,128)(2,1)}, bf16[80,4096]{1,0:T(8,128)(2,1)}, bf16[80,4096]{1,0:T(8,128)(2,1)}, bf16[80,4096]{1,0:T(8,128)(2,1)}) custom-call(s32[4]{0:T(128)} %dynamic-slice_bitcast_fusion.refs_1_.ids, bf16[128,4224]{1,0:T(8,128)(2,1)} %copy-done.7, bf16[128,4224]{1,0:T(8,128)(2,1)} %pin.29.refs_1_.refs_3_.refs_4_.refs_0_, ...), custom_call_target="tpu_custom_call" | custom-call | flops 2000000000 | bytes 6000000 | tf_op jit(solution)/shard_map/select/pallas_call | solution.py:141
  23.5 2.1 collective-permute-start.2
  26.9 4.2 %collective-permute-done.5.refs_0_ = bf16[128,4224]{1,0:T(8,128)(2,1)S(1)} collective-permute-done((bf16[128,4224]{1,0:T(8,128)(2,1)S(1)}, bf16[128,4224]{1,0:T(8,128)(2,1)S(1)}, u32[]{:S(2)}, u32[]{:S(2)}) %collective-permute-start.5) | collective-permute-done | bytes 1081376 | tf_op jit(solution)/shard_map/ppermute | solution.py:72
  32.0 1.5 collective-permute-start.6
  36.6 13.9 %collective-permute-done.3.refs_1_ = bf16[80,4096]{1,0:T(8,128)(2,1)} collective-permute-done((bf16[80,4096]{1,0:T(8,128)(2,1)}, bf16[80,4096]{1,0:T(8,128)(2,1)}, u32[]{:S(2)}, u32[]{:S(2)}) %collective-permute-start.3) | collective-permute-done | bytes 655392 | tf_op jit(solution)/shard_map/ppermute | solution.py:72
  50.5 2.3 collective-permute-done.6.refs_0_
  52.8 4.6 %select.10 = (bf16[80,4096]{1,0:T(8,128)(2,1)}, bf16[80,4096]{1,0:T(8,128)(2,1)}, bf16[80,4096]{1,0:T(8,128)(2,1)}, bf16[80,4096]{1,0:T(8,128)(2,1)}) custom-call(s32[4]{0:T(128)} %dynamic-slice_bitcast_fusion.refs_1_.ids, bf16[128,4224]{1,0:T(8,128)(2,1)} %pin.31.refs_1_.refs_0_.refs_2_, bf16[128,4224]{1,0:T(8,128)(2,1)} %pin.34.refs_1_.refs_3_.refs_4_.refs_0_, ...), custom_call_target="tpu_custom_call" | custom-call | flops 2000000000 | bytes 6000000 | tf_op jit(solution)/shard_map/select/pallas_call | solution.py:141
  57.7 2.0 collective-permute-start.10
  63.2 2.4 broadcast_select_fusion.1.refs_0_.refs_2_
  67.8 2.6 collective-permute-start.12
  70.5 13.8 %expert.4 = (bf16[80,4096]{1,0:T(8,128)(2,1)}, bf16[80,4096]{1,0:T(8,128)(2,1)}, bf16[80,4096]{1,0:T(8,128)(2,1)}, bf16[80,4096]{1,0:T(8,128)(2,1)}) custom-call(bf16[80,4096]{1,0:T(8,128)(2,1)} %get-tuple-element.65.refs_1_.refs_0_, bf16[80,4096]{1,0:T(8,128)(2,1)} %pin.30.refs_1_, bf16[80,4096]{1,0:T(8,128)(2,1)} %get-tuple-element.69.refs_1_.refs_2_, ...), custom_call_target="tpu_custom_call" | custom-call | flops 6000000000 | bytes 24000000 | tf_op jit(solution)/shard_map/expert/pallas_call | solution.py:252
  84.3 2.1 collective-permute-done.12.refs_0_
  87.5 4.5 %select.11 = (bf16[80,4096]{1,0:T(8,128)(2,1)}, bf16[80,4096]{1,0:T(8,128)(2,1)}, bf16[80,4096]{1,0:T(8,128)(2,1)}, bf16[80,4096]{1,0:T(8,128)(2,1)}) custom-call(s32[4]{0:T(128)} %dynamic-slice_bitcast_fusion.refs_1_.ids, bf16[128,4224]{1,0:T(8,128)(2,1)} %broadcast_select_fusion.1.refs_0_.refs_2_, bf16[128,4224]{1,0:T(8,128)(2,1)} %pin.39.refs_1_.refs_3_.refs_4_.refs_0_, ...), custom_call_target="tpu_custom_call" | custom-call | flops 2000000000 | bytes 6000000 | tf_op jit(solution)/shard_map/select/pallas_call | solution.py:141
  92.7 2.0 collective-permute-start.15
  97.9 1.4 broadcast_select_fusion.refs_0_.refs_2_
  100.2 13.7 %expert.5 = (bf16[80,4096]{1,0:T(8,128)(2,1)}, bf16[80,4096]{1,0:T(8,128)(2,1)}, bf16[80,4096]{1,0:T(8,128)(2,1)}, bf16[80,4096]{1,0:T(8,128)(2,1)}) custom-call(bf16[80,4096]{1,0:T(8,128)(2,1)} %get-tuple-element.72.refs_1_.refs_0_, bf16[80,4096]{1,0:T(8,128)(2,1)} %pin.37.refs_7_.refs_1_, bf16[80,4096]{1,0:T(8,128)(2,1)} %get-tuple-element.79.refs_1_.refs_2_, ...), custom_call_target="tpu_custom_call" | custom-call | flops 6000000000 | bytes 24000000 | tf_op jit(solution)/shard_map/expert/pallas_call | solution.py:252
  114.0 5.6 %collective-permute-done.16.refs_1_ = bf16[80,4096]{1,0:T(8,128)(2,1)} collective-permute-done((bf16[80,4096]{1,0:T(8,128)(2,1)}, bf16[80,4096]{1,0:T(8,128)(2,1)}, u32[]{:S(2)}, u32[]{:S(2)}) %collective-permute-start.16) | collective-permute-done | bytes 655392 | tf_op jit(solution)/shard_map/ppermute | solution.py:72
  119.6 1.9 collective-permute-done.17.refs_0_
  122.5 4.6 %select.12 = (bf16[80,4096]{1,0:T(8,128)(2,1)}, bf16[80,4096]{1,0:T(8,128)(2,1)}, bf16[80,4096]{1,0:T(8,128)(2,1)}, bf16[80,4096]{1,0:T(8,128)(2,1)}) custom-call(s32[4]{0:T(128)} %dynamic-slice_bitcast_fusion.refs_1_.ids, bf16[128,4224]{1,0:T(8,128)(2,1)} %copy-done.14, bf16[128,4224]{1,0:T(8,128)(2,1)} %pin.43.refs_1_.refs_3_.refs_4_.refs_0_, ...), custom_call_target="tpu_custom_call" | custom-call | flops 2000000000 | bytes 6000000 | tf_op jit(solution)/shard_map/select/pallas_call | solution.py:141
  127.5 2.0 collective-permute-start.22
  130.4 13.7 %expert.6 = (bf16[80,4096]{1,0:T(8,128)(2,1)}, bf16[80,4096]{1,0:T(8,128)(2,1)}, bf16[80,4096]{1,0:T(8,128)(2,1)}, bf16[80,4096]{1,0:T(8,128)(2,1)}) custom-call(bf16[80,4096]{1,0:T(8,128)(2,1)} %get-tuple-element.82.refs_1_.refs_0_, bf16[80,4096]{1,0:T(8,128)(2,1)} %pin.41.refs_7_.refs_1_, bf16[80,4096]{1,0:T(8,128)(2,1)} %get-tuple-element.89.refs_1_.refs_2_, ...), custom_call_target="tpu_custom_call" | custom-call | flops 6000000000 | bytes 24000000 | tf_op jit(solution)/shard_map/expert/pallas_call | solution.py:252
  146.4 13.8 %expert.7 = (bf16[80,4096]{1,0:T(8,128)(2,1)}, bf16[80,4096]{1,0:T(8,128)(2,1)}, bf16[80,4096]{1,0:T(8,128)(2,1)}, bf16[80,4096]{1,0:T(8,128)(2,1)}) custom-call(bf16[80,4096]{1,0:T(8,128)(2,1)} %get-tuple-element.91.refs_7_.refs_0_, bf16[80,4096]{1,0:T(8,128)(2,1)} %pin.44.refs_2_.refs_1_, bf16[80,4096]{1,0:T(8,128)(2,1)} %get-tuple-element.99.refs_2_.refs_7_, ...), custom_call_target="tpu_custom_call" | custom-call | flops 6000000000 | bytes 24000000 | tf_op jit(solution)/shard_map/expert/pallas_call | solution.py:252
  163.8 4.6 %mix.8.refs_3_ = bf16[128,4096]{1,0:T(8,128)(2,1)} custom-call(s32[4]{0:T(128)} %dynamic-slice_bitcast_fusion.refs_1_.ids, bf16[128,4224]{1,0:T(8,128)(2,1)} %pin.39.refs_1_.refs_3_.refs_4_.refs_0_, bf16[80,4096]{1,0:T(8,128)(2,1)} %get-tuple-element.92.refs_1_, bf16[80,4096]{1,0:T(8,128)(2,1)} %get-tuple-element.102.refs_2_.refs_5_, ...), custom_call_target="tpu_custom_call" | custom-call | flops 2000000000 | bytes 6000000 | tf_op jit(solution)/shard_map/mix/pallas_call | solution.py:190
  168.7 10.0 %collective-permute-done.26.refs_1_ = bf16[80,4096]{1,0:T(8,128)(2,1)} collective-permute-done((bf16[80,4096]{1,0:T(8,128)(2,1)}, bf16[80,4096]{1,0:T(8,128)(2,1)}, u32[]{:S(2)}, u32[]{:S(2)}) %collective-permute-start.26) | collective-permute-done | bytes 655392 | tf_op jit(solution)/shard_map/ppermute | solution.py:72
  179.0 4.6 %mix.9.refs_1_ = bf16[128,4096]{1,0:T(8,128)(2,1)} custom-call(s32[4]{0:T(128)} %dynamic-slice_bitcast_fusion.refs_1_.ids, bf16[128,4224]{1,0:T(8,128)(2,1)} %pin.43.refs_1_.refs_3_.refs_4_.refs_0_, bf16[80,4096]{1,0:T(8,128)(2,1)} %get-tuple-element.101.refs_3_.refs_1_, bf16[80,4096]{1,0:T(8,128)(2,1)} %get-tuple-element.108.refs_2_.refs_5_, ...), custom_call_target="tpu_custom_call" | custom-call | flops 2000000000 | bytes 6000000 | tf_op jit(solution)/shard_map/mix/pallas_call | solution.py:190
  184.1 5.1 %collective-permute-done.24.refs_0_ = bf16[128,4096]{1,0:T(8,128)(2,1)S(1)} collective-permute-done((bf16[128,4096]{1,0:T(8,128)(2,1)}, bf16[128,4096]{1,0:T(8,128)(2,1)S(1)}, u32[]{:S(2)}, u32[]{:S(2)}) %collective-permute-start.24) | collective-permute-done | bytes 1048608 | tf_op jit(solution)/shard_map/ppermute | solution.py:72
  190.2 4.8 %mix.10.refs_4_ = bf16[128,4096]{1,0:T(8,128)(2,1)} custom-call(s32[4]{0:T(128)} %dynamic-slice_bitcast_fusion.refs_1_.ids, bf16[128,4224]{1,0:T(8,128)(2,1)} %broadcast_select_fusion.1.refs_0_.refs_2_, bf16[80,4096]{1,0:T(8,128)(2,1)} %get-tuple-element.92.refs_1_, bf16[80,4096]{1,0:T(8,128)(2,1)} %get-tuple-element.102.refs_2_.refs_5_, ...), custom_call_target="tpu_custom_call" | custom-call | flops 2000000000 | bytes 6000000 | tf_op jit(solution)/shard_map/mix/pallas_call | solution.py:190
  195.0 3.3 %collective-permute-start.33 = (bf16[128,4096]{1,0:T(8,128)(2,1)}, bf16[128,4096]{1,0:T(8,128)(2,1)S(1)}, u32[]{:S(2)}, u32[]{:S(2)}) collective-permute-start(bf16[128,4096]{1,0:T(8,128)(2,1)} %mix.10.refs_4_), channel_id=1, source_target_pairs={{0,8},{1,9},{2,10},{3,11},{4,12},{5,13},{6,14},{7,15},{24,16},{25,... | collective-permute-start | bytes 3145736 | tf_op jit(solution)/shard_map/ppermute | solution.py:72
  201.5 4.8 %mix.11.refs_3_ = bf16[128,4096]{1,0:T(8,128)(2,1)} custom-call(s32[4]{0:T(128)} %dynamic-slice_bitcast_fusion.refs_1_.ids, bf16[128,4224]{1,0:T(8,128)(2,1)} %copy-done.14, bf16[80,4096]{1,0:T(8,128)(2,1)} %get-tuple-element.101.refs_3_.refs_1_, bf16[80,4096]{1,0:T(8,128)(2,1)} %get-tuple-element.108.refs_2_.refs_5_, ...), custom_call_target="tpu_custom_call" | custom-call | flops 2000000000 | bytes 6000000 | tf_op jit(solution)/shard_map/mix/pallas_call | solution.py:190
  206.3 10.5 %collective-permute-done.29.refs_1_ = bf16[80,4096]{1,0:T(8,128)(2,1)} collective-permute-done((bf16[80,4096]{1,0:T(8,128)(2,1)}, bf16[80,4096]{1,0:T(8,128)(2,1)}, u32[]{:S(2)}, u32[]{:S(2)}) %collective-permute-start.29) | collective-permute-done | bytes 655392 | tf_op jit(solution)/shard_map/ppermute | solution.py:72
  217.0 4.6 %mix.12.refs_1_ = bf16[128,4096]{1,0:T(8,128)(2,1)} custom-call(s32[4]{0:T(128)} %dynamic-slice_bitcast_fusion.refs_1_.ids, bf16[128,4224]{1,0:T(8,128)(2,1)} %pin.34.refs_1_.refs_3_.refs_4_.refs_0_, bf16[80,4096]{1,0:T(8,128)(2,1)} %get-tuple-element.111.refs_1_, bf16[80,4096]{1,0:T(8,128)(2,1)} %get-tuple-element.115.refs_2_.refs_5_, ...), custom_call_target="tpu_custom_call" | custom-call | flops 2000000000 | bytes 6000000 | tf_op jit(solution)/shard_map/mix/pallas_call | solution.py:190
  222.1 1.8 collective-permute-start.37
  224.9 2.5 add_convert_fusion.1
  228.0 8.7 %collective-permute-done.32.refs_0_ = bf16[128,4096]{1,0:T(8,128)(2,1)} collective-permute-done((bf16[128,4096]{1,0:T(8,128)(2,1)}, bf16[128,4096]{1,0:T(8,128)(2,1)}, u32[]{:S(2)}, u32[]{:S(2)}) %collective-permute-start.32) | collective-permute-done | bytes 1048608 | tf_op jit(solution)/shard_map/ppermute | solution.py:72
  236.7 4.8 %mix.13.refs_4_ = bf16[128,4096]{1,0:T(8,128)(2,1)} custom-call(s32[4]{0:T(128)} %dynamic-slice_bitcast_fusion.refs_1_.ids, bf16[128,4224]{1,0:T(8,128)(2,1)} %pin.31.refs_1_.refs_0_.refs_2_, bf16[80,4096]{1,0:T(8,128)(2,1)} %get-tuple-element.111.refs_1_, bf16[80,4096]{1,0:T(8,128)(2,1)} %get-tuple-element.115.refs_2_.refs_5_, ...), custom_call_target="tpu_custom_call" | custom-call | flops 2000000000 | bytes 6000000 | tf_op jit(solution)/shard_map/mix/pallas_call | solution.py:190
  242.5 5.2 %collective-permute-done.37.refs_0_ = bf16[128,4096]{1,0:T(8,128)(2,1)S(1)} collective-permute-done((bf16[128,4096]{1,0:T(8,128)(2,1)}, bf16[128,4096]{1,0:T(8,128)(2,1)S(1)}, u32[]{:S(2)}, u32[]{:S(2)}) %collective-permute-start.37) | collective-permute-done | bytes 1048608 | tf_op jit(solution)/shard_map/ppermute | solution.py:72
  248.7 2.8 add_convert_fusion
  251.5 1.3 collective-permute-start.41
  252.8 1.3 collective-permute-done.35.refs_1_
  254.1 5.5 %collective-permute-done.36.refs_2_ = bf16[80,4096]{1,0:T(8,128)(2,1)} collective-permute-done((bf16[80,4096]{1,0:T(8,128)(2,1)}, bf16[80,4096]{1,0:T(8,128)(2,1)}, u32[]{:S(2)}, u32[]{:S(2)}) %collective-permute-start.36) | collective-permute-done | bytes 655392 | tf_op jit(solution)/shard_map/ppermute | solution.py:72
  259.6 4.7 %mix.14.refs_1_ = bf16[128,4096]{1,0:T(8,128)(2,1)} custom-call(s32[4]{0:T(128)} %dynamic-slice_bitcast_fusion.refs_1_.ids, bf16[128,4224]{1,0:T(8,128)(2,1)} %pin.29.refs_1_.refs_3_.refs_4_.refs_0_, bf16[80,4096]{1,0:T(8,128)(2,1)} %get-tuple-element.118.refs_1_, bf16[80,4096]{1,0:T(8,128)(2,1)} %get-tuple-element.122.refs_2_.refs_5_, ...), custom_call_target="tpu_custom_call" | custom-call | flops 2000000000 | bytes 6000000 | tf_op jit(solution)/shard_map/mix/pallas_call | solution.py:190
  265.8 14.3 %collective-permute-done.41.refs_8_ = bf16[128,4096]{1,0:T(8,128)(2,1)S(1)} collective-permute-done((bf16[128,4096]{1,0:T(8,128)(2,1)}, bf16[128,4096]{1,0:T(8,128)(2,1)S(1)}, u32[]{:S(2)}, u32[]{:S(2)}) %collective-permute-start.41) | collective-permute-done | bytes 1048608 | tf_op jit(solution)/shard_map/ppermute | solution.py:72
  280.1 7.7 %collective-permute-done.40.refs_7_ = bf16[128,4096]{1,0:T(8,128)(2,1)} collective-permute-done((bf16[128,4096]{1,0:T(8,128)(2,1)}, bf16[128,4096]{1,0:T(8,128)(2,1)}, u32[]{:S(2)}, u32[]{:S(2)}) %collective-permute-start.40) | collective-permute-done | bytes 1048608 | tf_op jit(solution)/shard_map/ppermute | solution.py:72
  287.8 5.7 %mix.15 = bf16[128,4096]{1,0:T(8,128)(2,1)} custom-call(s32[4]{0:T(128)} %dynamic-slice_bitcast_fusion.refs_1_.ids, bf16[128,4224]{1,0:T(8,128)(2,1)} %copy-done.7, bf16[80,4096]{1,0:T(8,128)(2,1)} %get-tuple-element.118.refs_1_, bf16[80,4096]{1,0:T(8,128)(2,1)} %get-tuple-element.122.refs_2_.refs_5_, bf16[80,4096]{1,0:T(8,128)(2,1)} %get-tuple-element.123.refs_3_, ...), custom_call_target="tpu_custom_call" | custom-call | flops 2000000000 | bytes 6000000 | tf_op jit(solution)/shard_map/mix/pallas_call | solution.py:190
  (141 shorter events, 39.8 us)
Async XLA Ops:
  2.7 16.3 %copy-start.7 = (bf16[128,4224]{1,0:T(8,128)(2,1)}, bf16[128,4224]{1,0:T(8,128)(2,1)S(1)}, u32[]{:S(2)}) copy-start(bf16[128,4224]{1,0:T(8,128)(2,1)S(1)} %fusion.1.refs_0_.refs_2_) | copy-start | bytes 3244036
  2.7 16.2 %collective-permute-start = (bf16[128,4224]{1,0:T(8,128)(2,1)S(1)}, bf16[128,4224]{1,0:T(8,128)(2,1)}, u32[]{:S(2)}, u32[]{:S(2)}) collective-permute-start(bf16[128,4224]{1,0:T(8,128)(2,1)S(1)} %fusion.1.refs_0_.refs_2_), channel_id=1, source_target_pairs={{0,2},{1,5},{2,0},{3,7},{4,6},{5,1},{6,4},{7,3},{8,10},{9,13},{10,... | collective-permute-start | bytes 3244040 | tf_op jit(solution)/shard_map/ppermute | solution.py:72
  5.7 25.3 %collective-permute-start.5 = (bf16[128,4224]{1,0:T(8,128)(2,1)S(1)}, bf16[128,4224]{1,0:T(8,128)(2,1)S(1)}, u32[]{:S(2)}, u32[]{:S(2)}) collective-permute-start(bf16[128,4224]{1,0:T(8,128)(2,1)S(1)} %fusion.1.refs_0_.refs_2_), channel_id=1, source_target_pairs={{0,8},{1,9},{2,10},{3,11},{4,12},{5,13},{6,14},{7,15},{8,0},{9,1},... | collective-permute-start | bytes 3244040 | tf_op jit(solution)/shard_map/ppermute | solution.py:72
  7.3 26.2 %collective-permute-start.4 = (bf16[128,4224]{1,0:T(8,128)(2,1)S(1)}, bf16[128,4224]{1,0:T(8,128)(2,1)S(1)}, u32[]{:S(2)}, u32[]{:S(2)}) collective-permute-start(bf16[128,4224]{1,0:T(8,128)(2,1)S(1)} %fusion.1.refs_0_.refs_2_), channel_id=1, source_target_pairs={{8,16},{9,17},{10,18},{11,19},{12,20},{13,21},{14,22},{15,23},{16,... | collective-permute-start | bytes 3244040 | tf_op jit(solution)/shard_map/ppermute | solution.py:72
  23.5 3.4 %collective-permute-start.1 = (bf16[80,4096]{1,0:T(8,128)(2,1)}, bf16[80,4096]{1,0:T(8,128)(2,1)}, u32[]{:S(2)}, u32[]{:S(2)}) collective-permute-start(bf16[80,4096]{1,0:T(8,128)(2,1)} %get-tuple-element.66), channel_id=1, source_target_pairs={{0,1},{1,0},{2,3},{3,2},{4,5},{5,4},{6,7},{7,6},{8,9},{9,8},{10,11... | collective-permute-start | bytes 1966088 | tf_op jit(solution)/shard_map/ppermute | solution.py:72
  23.5 13.1 %collective-permute-start.2 = (bf16[80,4096]{1,0:T(8,128)(2,1)}, bf16[80,4096]{1,0:T(8,128)(2,1)}, u32[]{:S(2)}, u32[]{:S(2)}) collective-permute-start(bf16[80,4096]{1,0:T(8,128)(2,1)} %get-tuple-element.67), channel_id=1, source_target_pairs={{0,4},{1,3},{2,6},{3,1},{4,0},{5,7},{6,2},{7,5},{8,12},{9,11},{10,... | collective-permute-start | bytes 1966088 | tf_op jit(solution)/shard_map/ppermute | solution.py:72
  25.6 24.9 %collective-permute-start.3 = (bf16[80,4096]{1,0:T(8,128)(2,1)}, bf16[80,4096]{1,0:T(8,128)(2,1)}, u32[]{:S(2)}, u32[]{:S(2)}) collective-permute-start(bf16[80,4096]{1,0:T(8,128)(2,1)} %get-tuple-element.68), channel_id=1, source_target_pairs={{0,5},{1,2},{2,7},{3,0},{4,1},{5,6},{6,3},{7,4},{8,13},{9,10},{10,... | collective-permute-start | bytes 1966088 | tf_op jit(solution)/shard_map/ppermute | solution.py:72
  32.0 20.8 %collective-permute-start.6 = (bf16[128,4224]{1,0:T(8,128)(2,1)}, bf16[128,4224]{1,0:T(8,128)(2,1)}, u32[]{:S(2)}, u32[]{:S(2)}) collective-permute-start(bf16[128,4224]{1,0:T(8,128)(2,1)} %pin.31.refs_1_.refs_0_.refs_2_), channel_id=1, source_target_pairs={{0,2},{1,5},{2,0},{3,7},{4,6},{5,1},{6,4},{7,3},{8,10},{9,13},{10,... | collective-permute-start | bytes 3244040 | tf_op jit(solution)/shard_map/ppermute | solution.py:72
  34.5 26.4 %collective-permute-start.9 = (bf16[128,4224]{1,0:T(8,128)(2,1)}, bf16[128,4224]{1,0:T(8,128)(2,1)S(1)}, u32[]{:S(2)}, u32[]{:S(2)}) collective-permute-start(bf16[128,4224]{1,0:T(8,128)(2,1)} %pin.32.refs_2_), channel_id=1, source_target_pairs={{8,0},{9,1},{10,2},{11,3},{12,4},{13,5},{14,6},{15,7},{16,24},{17,... | collective-permute-start | bytes 3244040 | tf_op jit(solution)/shard_map/ppermute | solution.py:72
  35.8 29.7 %collective-permute-start.8 = (bf16[128,4224]{1,0:T(8,128)(2,1)}, bf16[128,4224]{1,0:T(8,128)(2,1)S(1)}, u32[]{:S(2)}, u32[]{:S(2)}) collective-permute-start(bf16[128,4224]{1,0:T(8,128)(2,1)} %pin.31.refs_1_.refs_0_.refs_2_), channel_id=1, source_target_pairs={{8,16},{9,17},{10,18},{11,19},{12,20},{13,21},{14,22},{15,23},{16,... | collective-permute-start | bytes 3244040 | tf_op jit(solution)/shard_map/ppermute | solution.py:72
  57.4 13.1 %collective-permute-start.7 = (bf16[80,4096]{1,0:T(8,128)(2,1)}, bf16[80,4096]{1,0:T(8,128)(2,1)}, u32[]{:S(2)}, u32[]{:S(2)}) collective-permute-start(bf16[80,4096]{1,0:T(8,128)(2,1)} %get-tuple-element.71), channel_id=1, source_target_pairs={{0,1},{1,0},{2,3},{3,2},{4,5},{5,4},{6,7},{7,6},{8,9},{9,8},{10,11... | collective-permute-start | bytes 1966088 | tf_op jit(solution)/shard_map/ppermute | solution.py:72
  57.7 26.6 %collective-permute-start.10 = (bf16[80,4096]{1,0:T(8,128)(2,1)}, bf16[80,4096]{1,0:T(8,128)(2,1)}, u32[]{:S(2)}, u32[]{:S(2)}) collective-permute-start(bf16[80,4096]{1,0:T(8,128)(2,1)} %get-tuple-element.77), channel_id=1, source_target_pairs={{0,4},{1,3},{2,6},{3,1},{4,0},{5,7},{6,2},{7,5},{8,12},{9,11},{10,... | collective-permute-start | bytes 1966088 | tf_op jit(solution)/shard_map/ppermute | solution.py:72
  59.7 24.6 %collective-permute-start.11 = (bf16[80,4096]{1,0:T(8,128)(2,1)}, bf16[80,4096]{1,0:T(8,128)(2,1)}, u32[]{:S(2)}, u32[]{:S(2)}) collective-permute-start(bf16[80,4096]{1,0:T(8,128)(2,1)} %get-tuple-element.78), channel_id=1, source_target_pairs={{0,5},{1,2},{2,7},{3,0},{4,1},{5,6},{6,3},{7,4},{8,13},{9,10},{10,... | collective-permute-start | bytes 1966088 | tf_op jit(solution)/shard_map/ppermute | solution.py:72
  66.5 29.1 %collective-permute-start.14 = (bf16[128,4224]{1,0:T(8,128)(2,1)}, bf16[128,4224]{1,0:T(8,128)(2,1)S(1)}, u32[]{:S(2)}, u32[]{:S(2)}) collective-permute-start(bf16[128,4224]{1,0:T(8,128)(2,1)} %pin.36.refs_1_), channel_id=1, source_target_pairs={{8,0},{9,1},{10,2},{11,3},{12,4},{13,5},{14,6},{15,7},{16,24},{17,... | collective-permute-start | bytes 3244040 | tf_op jit(solution)/shard_map/ppermute | solution.py:72
  67.8 18.6 %collective-permute-start.12 = (bf16[128,4224]{1,0:T(8,128)(2,1)S(1)}, bf16[128,4224]{1,0:T(8,128)(2,1)S(1)}, u32[]{:S(2)}, u32[]{:S(2)}) collective-permute-start(bf16[128,4224]{1,0:T(8,128)(2,1)S(1)} %copy-done.13), channel_id=1, source_target_pairs={{0,2},{1,5},{2,0},{3,7},{4,6},{5,1},{6,4},{7,3},{8,10},{9,13},{10,... | collective-permute-start | bytes 3244040 | tf_op jit(solution)/shard_map/ppermute | solution.py:72
  92.0 8.0 %collective-permute-start.13 = (bf16[80,4096]{1,0:T(8,128)(2,1)}, bf16[80,4096]{1,0:T(8,128)(2,1)}, u32[]{:S(2)}, u32[]{:S(2)}) collective-permute-start(bf16[80,4096]{1,0:T(8,128)(2,1)} %get-tuple-element.81), channel_id=1, source_target_pairs={{0,1},{1,0},{2,3},{3,2},{4,5},{5,4},{6,7},{7,6},{8,9},{9,8},{10,11... | collective-permute-start | bytes 1966088 | tf_op jit(solution)/shard_map/ppermute | solution.py:72
  92.7 21.3 %collective-permute-start.15 = (bf16[80,4096]{1,0:T(8,128)(2,1)}, bf16[80,4096]{1,0:T(8,128)(2,1)}, u32[]{:S(2)}, u32[]{:S(2)}) collective-permute-start(bf16[80,4096]{1,0:T(8,128)(2,1)} %get-tuple-element.87), channel_id=1, source_target_pairs={{0,4},{1,3},{2,6},{3,1},{4,0},{5,7},{6,2},{7,5},{8,12},{9,11},{10,... | collective-permute-start | bytes 1966088 | tf_op jit(solution)/shard_map/ppermute | solution.py:72
  94.8 24.8 %collective-permute-start.16 = (bf16[80,4096]{1,0:T(8,128)(2,1)}, bf16[80,4096]{1,0:T(8,128)(2,1)}, u32[]{:S(2)}, u32[]{:S(2)}) collective-permute-start(bf16[80,4096]{1,0:T(8,128)(2,1)} %get-tuple-element.88), channel_id=1, source_target_pairs={{0,5},{1,2},{2,7},{3,0},{4,1},{5,6},{6,3},{7,4},{8,13},{9,10},{10,... | collective-permute-start | bytes 1966088 | tf_op jit(solution)/shard_map/ppermute | solution.py:72
  99.3 22.2 %collective-permute-start.17 = (bf16[128,4224]{1,0:T(8,128)(2,1)S(1)}, bf16[128,4224]{1,0:T(8,128)(2,1)S(1)}, u32[]{:S(2)}, u32[]{:S(2)}) collective-permute-start(bf16[128,4224]{1,0:T(8,128)(2,1)S(1)} %broadcast_select_fusion.refs_0_.refs_2_), channel_id=1, source_target_pairs={{0,2},{1,5},{2,0},{3,7},{4,6},{5,1},{6,4},{7,3},{8,10},{9,13},{10,... | collective-permute-start | bytes 3244040 | tf_op jit(solution)/shard_map/ppermute | solution.py:72
  127.1 18.4 %collective-permute-start.21 = (bf16[80,4096]{1,0:T(8,128)(2,1)}, bf16[80,4096]{1,0:T(8,128)(2,1)S(1)}, u32[]{:S(2)}, u32[]{:S(2)}) collective-permute-start(bf16[80,4096]{1,0:T(8,128)(2,1)} %get-tuple-element.96), channel_id=1, source_target_pairs={{0,1},{1,0},{2,3},{3,2},{4,5},{5,4},{6,7},{7,6},{8,9},{9,8},{10,11... | collective-permute-start | bytes 1966088 | tf_op jit(solution)/shard_map/ppermute | solution.py:72
  127.5 18.9 %collective-permute-start.22 = (bf16[80,4096]{1,0:T(8,128)(2,1)}, bf16[80,4096]{1,0:T(8,128)(2,1)}, u32[]{:S(2)}, u32[]{:S(2)}) collective-permute-start(bf16[80,4096]{1,0:T(8,128)(2,1)} %get-tuple-element.97), channel_id=1, source_target_pairs={{0,4},{1,3},{2,6},{3,1},{4,0},{5,7},{6,2},{7,5},{8,12},{9,11},{10,... | collective-permute-start | bytes 1966088 | tf_op jit(solution)/shard_map/ppermute | solution.py:72
  129.6 16.9 %collective-permute-start.23 = (bf16[80,4096]{1,0:T(8,128)(2,1)}, bf16[80,4096]{1,0:T(8,128)(2,1)}, u32[]{:S(2)}, u32[]{:S(2)}) collective-permute-start(bf16[80,4096]{1,0:T(8,128)(2,1)} %get-tuple-element.98), channel_id=1, source_target_pairs={{0,5},{1,2},{2,7},{3,0},{4,1},{5,6},{6,3},{7,4},{8,13},{9,10},{10,... | collective-permute-start | bytes 1966088 | tf_op jit(solution)/shard_map/ppermute | solution.py:72
  144.2 17.6 %collective-permute-start.18 = (bf16[80,4096]{1,0:T(8,128)(2,1)}, bf16[80,4096]{1,0:T(8,128)(2,1)S(1)}, u32[]{:S(2)}, u32[]{:S(2)}) collective-permute-start(bf16[80,4096]{1,0:T(8,128)(2,1)} %get-tuple-element.93), channel_id=1, source_target_pairs={{1,0},{0,1},{3,2},{2,3},{5,4},{4,5},{7,6},{6,7},{9,8},{8,9},{11,10... | collective-permute-start | bytes 1966088 | tf_op jit(solution)/shard_map/ppermute | solution.py:72
  145.0 17.8 %collective-permute-start.19 = (bf16[80,4096]{1,0:T(8,128)(2,1)}, bf16[80,4096]{1,0:T(8,128)(2,1)S(1)}, u32[]{:S(2)}, u32[]{:S(2)}) collective-permute-start(bf16[80,4096]{1,0:T(8,128)(2,1)} %get-tuple-element.94), channel_id=1, source_target_pairs={{4,0},{3,1},{6,2},{1,3},{0,4},{7,5},{2,6},{5,7},{12,8},{11,9},{14,... | collective-permute-start | bytes 1966088 | tf_op jit(solution)/shard_map/ppermute | solution.py:72
  145.5 17.2 %collective-permute-start.20 = (bf16[80,4096]{1,0:T(8,128)(2,1)}, bf16[80,4096]{1,0:T(8,128)(2,1)S(1)}, u32[]{:S(2)}, u32[]{:S(2)}) collective-permute-start(bf16[80,4096]{1,0:T(8,128)(2,1)} %get-tuple-element.95), channel_id=1, source_target_pairs={{5,0},{2,1},{7,2},{0,3},{1,4},{6,5},{3,6},{4,7},{13,8},{10,9},{15,... | collective-permute-start | bytes 1966088 | tf_op jit(solution)/shard_map/ppermute | solution.py:72
  160.3 8.5 %collective-permute-start.25 = (bf16[80,4096]{1,0:T(8,128)(2,1)}, bf16[80,4096]{1,0:T(8,128)(2,1)S(1)}, u32[]{:S(2)}, u32[]{:S(2)}) collective-permute-start(bf16[80,4096]{1,0:T(8,128)(2,1)} %get-tuple-element.105), channel_id=1, source_target_pairs={{1,0},{0,1},{3,2},{2,3},{5,4},{4,5},{7,6},{6,7},{9,8},{8,9},{11,10... | collective-permute-start | bytes 1966088 | tf_op jit(solution)/shard_map/ppermute | solution.py:72
  161.0 17.7 %collective-permute-start.26 = (bf16[80,4096]{1,0:T(8,128)(2,1)}, bf16[80,4096]{1,0:T(8,128)(2,1)}, u32[]{:S(2)}, u32[]{:S(2)}) collective-permute-start(bf16[80,4096]{1,0:T(8,128)(2,1)} %get-tuple-element.106), channel_id=1, source_target_pairs={{4,0},{3,1},{6,2},{1,3},{0,4},{7,5},{2,6},{5,7},{12,8},{11,9},{14,... | collective-permute-start | bytes 1966088 | tf_op jit(solution)/shard_map/ppermute | solution.py:72
  161.8 17.1 %collective-permute-start.27 = (bf16[80,4096]{1,0:T(8,128)(2,1)}, bf16[80,4096]{1,0:T(8,128)(2,1)}, u32[]{:S(2)}, u32[]{:S(2)}) collective-permute-start(bf16[80,4096]{1,0:T(8,128)(2,1)} %get-tuple-element.107), channel_id=1, source_target_pairs={{5,0},{2,1},{7,2},{0,3},{1,4},{6,5},{3,6},{4,7},{13,8},{10,9},{15,... | collective-permute-start | bytes 1966088 | tf_op jit(solution)/shard_map/ppermute | solution.py:72
  168.4 20.8 %collective-permute-start.24 = (bf16[128,4096]{1,0:T(8,128)(2,1)}, bf16[128,4096]{1,0:T(8,128)(2,1)S(1)}, u32[]{:S(2)}, u32[]{:S(2)}) collective-permute-start(bf16[128,4096]{1,0:T(8,128)(2,1)} %mix.8.refs_3_), channel_id=1, source_target_pairs={{0,2},{1,5},{2,0},{3,7},{4,6},{5,1},{6,4},{7,3},{8,10},{9,13},{10,... | collective-permute-start | bytes 3145736 | tf_op jit(solution)/shard_map/ppermute | solution.py:72
  168.7 10.2 %copy-start.23 = (bf16[80,4096]{1,0:T(8,128)(2,1)}, bf16[80,4096]{1,0:T(8,128)(2,1)S(1)}, u32[]{:S(2)}) copy-start(bf16[80,4096]{1,0:T(8,128)(2,1)S(1)} %collective-permute-done.25.refs_0_) | copy-start | bytes 1966084
  183.6 17.0 %collective-permute-start.31 = (bf16[128,4096]{1,0:T(8,128)(2,1)}, bf16[128,4096]{1,0:T(8,128)(2,1)S(1)}, u32[]{:S(2)}, u32[]{:S(2)}) collective-permute-start(bf16[128,4096]{1,0:T(8,128)(2,1)} %mix.9.refs_1_), channel_id=1, source_target_pairs={{0,2},{1,5},{2,0},{3,7},{4,6},{5,1},{6,4},{7,3},{8,10},{9,13},{10,... | collective-permute-start | bytes 3145736 | tf_op jit(solution)/shard_map/ppermute | solution.py:72
  195.0 28.9 %collective-permute-start.33 = (bf16[128,4096]{1,0:T(8,128)(2,1)}, bf16[128,4096]{1,0:T(8,128)(2,1)S(1)}, u32[]{:S(2)}, u32[]{:S(2)}) collective-permute-start(bf16[128,4096]{1,0:T(8,128)(2,1)} %mix.10.refs_4_), channel_id=1, source_target_pairs={{0,8},{1,9},{2,10},{3,11},{4,12},{5,13},{6,14},{7,15},{24,16},{25,... | collective-permute-start | bytes 3145736 | tf_op jit(solution)/shard_map/ppermute | solution.py:72
  198.3 8.0 %collective-permute-start.28 = (bf16[80,4096]{1,0:T(8,128)(2,1)}, bf16[80,4096]{1,0:T(8,128)(2,1)S(1)}, u32[]{:S(2)}, u32[]{:S(2)}) collective-permute-start(bf16[80,4096]{1,0:T(8,128)(2,1)} %get-tuple-element.112), channel_id=1, source_target_pairs={{1,0},{0,1},{3,2},{2,3},{5,4},{4,5},{7,6},{6,7},{9,8},{8,9},{11,10... | collective-permute-start | bytes 1966088 | tf_op jit(solution)/shard_map/ppermute | solution.py:72
  199.1 17.7 %collective-permute-start.29 = (bf16[80,4096]{1,0:T(8,128)(2,1)}, bf16[80,4096]{1,0:T(8,128)(2,1)}, u32[]{:S(2)}, u32[]{:S(2)}) collective-permute-start(bf16[80,4096]{1,0:T(8,128)(2,1)} %get-tuple-element.113), channel_id=1, source_target_pairs={{4,0},{3,1},{6,2},{1,3},{0,4},{7,5},{2,6},{5,7},{12,8},{11,9},{14,... | collective-permute-start | bytes 1966088 | tf_op jit(solution)/shard_map/ppermute | solution.py:72
  199.9 17.1 %collective-permute-start.30 = (bf16[80,4096]{1,0:T(8,128)(2,1)}, bf16[80,4096]{1,0:T(8,128)(2,1)}, u32[]{:S(2)}, u32[]{:S(2)}) collective-permute-start(bf16[80,4096]{1,0:T(8,128)(2,1)} %get-tuple-element.114), channel_id=1, source_target_pairs={{5,0},{2,1},{7,2},{0,3},{1,4},{6,5},{3,6},{4,7},{13,8},{10,9},{15,... | collective-permute-start | bytes 1966088 | tf_op jit(solution)/shard_map/ppermute | solution.py:72
  206.3 10.7 %copy-start.24 = (bf16[80,4096]{1,0:T(8,128)(2,1)}, bf16[80,4096]{1,0:T(8,128)(2,1)S(1)}, u32[]{:S(2)}) copy-start(bf16[80,4096]{1,0:T(8,128)(2,1)S(1)} %collective-permute-done.28.refs_0_) | copy-start | bytes 1966084
  221.6 3.3 %copy-start.11 = (bf16[128,4096]{1,0:T(8,128)(2,1)S(1)}, bf16[128,4096]{1,0:T(8,128)(2,1)}, u32[]{:S(2)}) copy-start(bf16[128,4096]{1,0:T(8,128)(2,1)} %mix.10.refs_4_) | copy-start | bytes 3145732
  221.6 15.1 %collective-permute-start.32 = (bf16[128,4096]{1,0:T(8,128)(2,1)}, bf16[128,4096]{1,0:T(8,128)(2,1)}, u32[]{:S(2)}, u32[]{:S(2)}) collective-permute-start(bf16[128,4096]{1,0:T(8,128)(2,1)} %mix.12.refs_1_), channel_id=1, source_target_pairs={{0,2},{1,5},{2,0},{3,7},{4,6},{5,1},{6,4},{7,3},{8,10},{9,13},{10,... | collective-permute-start | bytes 3145736 | tf_op jit(solution)/shard_map/ppermute | solution.py:72
  222.1 25.6 %collective-permute-start.37 = (bf16[128,4096]{1,0:T(8,128)(2,1)}, bf16[128,4096]{1,0:T(8,128)(2,1)S(1)}, u32[]{:S(2)}, u32[]{:S(2)}) collective-permute-start(bf16[128,4096]{1,0:T(8,128)(2,1)} %mix.11.refs_3_), channel_id=1, source_target_pairs={{0,8},{1,9},{2,10},{3,11},{4,12},{5,13},{6,14},{7,15},{24,16},{25,... | collective-permute-start | bytes 3145736 | tf_op jit(solution)/shard_map/ppermute | solution.py:72
  227.3 37.5 %collective-permute-start.39 = (bf16[128,4096]{1,0:T(8,128)(2,1)}, bf16[128,4096]{1,0:T(8,128)(2,1)S(1)}, u32[]{:S(2)}, u32[]{:S(2)}) collective-permute-start(bf16[128,4096]{1,0:T(8,128)(2,1)} %add_convert_fusion.1), channel_id=1, source_target_pairs={{8,16},{9,17},{10,18},{11,19},{12,20},{13,21},{14,22},{15,23},{16,... | collective-permute-start | bytes 3145736 | tf_op jit(solution)/shard_map/ppermute | solution.py:72
  241.5 46.2 %collective-permute-start.40 = (bf16[128,4096]{1,0:T(8,128)(2,1)}, bf16[128,4096]{1,0:T(8,128)(2,1)}, u32[]{:S(2)}, u32[]{:S(2)}) collective-permute-start(bf16[128,4096]{1,0:T(8,128)(2,1)} %mix.13.refs_4_), channel_id=1, source_target_pairs={{0,8},{1,9},{2,10},{3,11},{4,12},{5,13},{6,14},{7,15},{8,0},{9,1},... | collective-permute-start | bytes 3145736 | tf_op jit(solution)/shard_map/ppermute | solution.py:72
  241.5 10.0 %collective-permute-start.34 = (bf16[80,4096]{1,0:T(8,128)(2,1)}, bf16[80,4096]{1,0:T(8,128)(2,1)S(1)}, u32[]{:S(2)}, u32[]{:S(2)}) collective-permute-start(bf16[80,4096]{1,0:T(8,128)(2,1)} %get-tuple-element.119), channel_id=1, source_target_pairs={{1,0},{0,1},{3,2},{2,3},{5,4},{4,5},{7,6},{6,7},{9,8},{8,9},{11,10... | collective-permute-start | bytes 1966088 | tf_op jit(solution)/shard_map/ppermute | solution.py:72
  241.6 12.5 %collective-permute-start.35 = (bf16[80,4096]{1,0:T(8,128)(2,1)}, bf16[80,4096]{1,0:T(8,128)(2,1)}, u32[]{:S(2)}, u32[]{:S(2)}) collective-permute-start(bf16[80,4096]{1,0:T(8,128)(2,1)} %get-tuple-element.120), channel_id=1, source_target_pairs={{4,0},{3,1},{6,2},{1,3},{0,4},{7,5},{2,6},{5,7},{12,8},{11,9},{14,... | collective-permute-start | bytes 1966088 | tf_op jit(solution)/shard_map/ppermute | solution.py:72
  247.7 11.9 %collective-permute-start.36 = (bf16[80,4096]{1,0:T(8,128)(2,1)}, bf16[80,4096]{1,0:T(8,128)(2,1)}, u32[]{:S(2)}, u32[]{:S(2)}) collective-permute-start(bf16[80,4096]{1,0:T(8,128)(2,1)} %get-tuple-element.121), channel_id=1, source_target_pairs={{5,0},{2,1},{7,2},{0,3},{1,4},{6,5},{3,6},{4,7},{13,8},{10,9},{15,... | collective-permute-start | bytes 1966088 | tf_op jit(solution)/shard_map/ppermute | solution.py:72
  251.5 8.1 %copy-start.12 = (bf16[80,4096]{1,0:T(8,128)(2,1)}, bf16[80,4096]{1,0:T(8,128)(2,1)S(1)}, u32[]{:S(2)}) copy-start(bf16[80,4096]{1,0:T(8,128)(2,1)S(1)} %collective-permute-done.34.refs_0_) | copy-start | bytes 1966084
  251.5 28.6 %collective-permute-start.41 = (bf16[128,4096]{1,0:T(8,128)(2,1)}, bf16[128,4096]{1,0:T(8,128)(2,1)S(1)}, u32[]{:S(2)}, u32[]{:S(2)}) collective-permute-start(bf16[128,4096]{1,0:T(8,128)(2,1)} %add_convert_fusion), channel_id=1, source_target_pairs={{8,24},{9,25},{10,26},{11,27},{12,28},{13,29},{14,30},{15,31},{16,... | collective-permute-start | bytes 3145736 | tf_op jit(solution)/shard_map/ppermute | solution.py:72
  264.3 23.5 %collective-permute-start.38 = (bf16[128,4096]{1,0:T(8,128)(2,1)}, bf16[128,4096]{1,0:T(8,128)(2,1)}, u32[]{:S(2)}, u32[]{:S(2)}) collective-permute-start(bf16[128,4096]{1,0:T(8,128)(2,1)} %mix.14.refs_1_), channel_id=1, source_target_pairs={{0,2},{1,5},{2,0},{3,7},{4,6},{5,1},{6,4},{7,3},{8,10},{9,13},{10,... | collective-permute-start | bytes 3145736 | tf_op jit(solution)/shard_map/ppermute | solution.py:72
  280.1 7.7 %copy-start.17 = (bf16[128,4096]{1,0:T(8,128)(2,1)}, bf16[128,4096]{1,0:T(8,128)(2,1)S(1)}, u32[]{:S(2)}) copy-start(bf16[128,4096]{1,0:T(8,128)(2,1)S(1)} %collective-permute-done.41.refs_8_) | copy-start | bytes 3145732
  (20 other events, 21.5 us)
